TPU v7x, 32 devices: a whole 2x2x4 slice. The times are simulated.
32 devices in a mesh: dp: 4 (over y, x), lon: 8 (over z, core).
Axes of the slice: x: 2, y: 2, z: 4, core: 2. Of those that a mesh axis runs over, the one named last changes fastest.
Arguments:
- fields: bfloat16 [4, 64, 128, 384], P('dp', None, 'lon'), may hold values from -6 to 6
- cotangent: bfloat16 [4, 64, 128, 384], P('dp', None, 'lon'), may hold values from -6 to 6
- kernel_first: bfloat16 [3, 3, 64, 64], replicated, may hold values from -0.25 to 0.25
- kernel_second: bfloat16 [3, 3, 64, 64], replicated, may hold values from -0.25 to 0.25
- metric: float32 [384], replicated, may hold values from 0.5 to 3
Outputs:
- field_grad: bfloat16 [4, 64, 128, 384], P('dp', None, 'lon')
- grad_first: bfloat16 [3, 3, 64, 64], replicated
- grad_second: bfloat16 [3, 3, 64, 64], replicated
All inputs are finite; a program needn't handle non-finite values.
Results may differ from a plain program's by a relative error of at most 0.0063.
Values may be sent and summed in bfloat16 or wider, within the bound.
No kernel may reach another device: no remote copies, remote signals or barrier semaphores. Data moves between devices by JAX's collectives and lax.ppermute only.
A program may use at most 64 MiB of HBM per device.

v0:
```python
import jax
import jax.numpy as jnp
from jax import lax
from jax.sharding import PartitionSpec as P

gelu_coef = 0.7978845608


def extended(shard, sides, width):
    for axis, dim in sides:
        count, length = (lax.axis_size(axis), shard.shape[dim])
        up = [(i, (i + 1) % count) for i in range(count)]
        down = [(j, i) for i, j in up]
        last = lax.slice_in_dim(shard, length - width, length, axis=dim)
        first = lax.slice_in_dim(shard, 0, width, axis=dim)
        before = lax.ppermute(last, axis, up)
        after = lax.ppermute(first, axis, down)
        shard = jnp.concatenate([before, shard, after], axis=dim)
    return shard


def gelu_value(u):
    inner = jnp.tanh(gelu_coef * (u + 0.044715 * u * u * u))
    return 0.5 * u * (1.0 + inner)


def gelu_slope(u):
    inner = jnp.tanh(gelu_coef * (u + 0.044715 * u * u * u))
    return 0.5 * (1.0 + inner) + 0.5 * u * (1.0 - inner * inner) * gelu_coef * (
        1.0 + 3.0 * 0.044715 * u * u
    )


def pad_rows(value):
    return jnp.pad(value, ((0, 0), (0, 0), (0, 0), (1, 1)))


def stencil_apply(padded, taps, metric):
    columns = padded.shape[2] - 2
    lat_rows = padded.shape[3] - 2
    total = None
    for p in range(3):
        summed = None
        for q in range(3):
            term = jnp.einsum(
                "oc,bcij->boij",
                taps[p, q],
                padded[:, :, p : p + columns, q : q + lat_rows],
                preferred_element_type=jnp.float32,
            )
            summed = term if summed is None else summed + term
        summed = summed if p == 1 else summed * metric[None, None, None, :]
        total = summed if total is None else total + summed
    return total


def stencil_adjoint(plain_pad, scaled_pad, taps):
    columns = plain_pad.shape[2] - 2
    lat_rows = plain_pad.shape[3] - 2
    total = None
    for p in range(3):
        source = plain_pad if p == 1 else scaled_pad
        for q in range(3):
            term = jnp.einsum(
                "oc,boij->bcij",
                taps[p, q],
                source[:, :, 2 - p : 2 - p + columns, 2 - q : 2 - q + lat_rows],
                preferred_element_type=jnp.float32,
            )
            total = term if total is None else total + term
    return total


def kernel_term(plain, scaled, padded):
    columns = plain.shape[2]
    lat_rows = plain.shape[3]
    terms = []
    for p in range(3):
        source = plain if p == 1 else scaled
        row_terms = []
        for q in range(3):
            row_terms.append(
                jnp.einsum(
                    "boij,bcij->oc",
                    source,
                    padded[:, :, p : p + columns, q : q + lat_rows],
                    preferred_element_type=jnp.float32,
                )
            )
        terms.append(jnp.stack(row_terms))
    return jnp.stack(terms)


def per_device(fields, cotangent, kernel_first, kernel_second, metric):
    metric_padded = jnp.pad(metric, (1, 1))[None, None, None, :]
    samples_here = fields.shape[0]
    stacked = jnp.concatenate((fields, cotangent), axis=0)
    both_pad = extended(stacked, (("lon", 2),), 2)
    input_pad = pad_rows(both_pad[:samples_here])
    upstream_pad = pad_rows(both_pad[samples_here:])
    before_gelu = stencil_apply(input_pad, kernel_first, metric)
    hidden_pad = pad_rows(gelu_value(before_gelu).astype(jnp.bfloat16))
    scaled_pad = (metric_padded * upstream_pad.astype(jnp.float32)).astype(jnp.bfloat16)
    second = kernel_term(cotangent, scaled_pad[:, :, 2:-2, 1:-1], hidden_pad)
    hidden_grad = stencil_adjoint(upstream_pad, scaled_pad, kernel_second)
    delta_wide = (hidden_grad * gelu_slope(before_gelu)).astype(jnp.bfloat16)
    delta_pad = pad_rows(delta_wide)
    delta_scaled = (metric_padded * delta_pad.astype(jnp.float32)).astype(jnp.bfloat16)
    field_grad = (
        cotangent.astype(jnp.float32) + stencil_adjoint(delta_pad, delta_scaled, kernel_first)
    ).astype(jnp.bfloat16)
    first = kernel_term(
        delta_wide[:, :, 1:-1], delta_scaled[:, :, 1:-1, 1:-1], input_pad[:, :, 1:-1]
    )
    first, second = lax.psum((first, second), ("dp", "lon"))
    counted = (
        float(fields.shape[0] * lax.axis_size("dp"))
        * float(fields.shape[2] * lax.axis_size("lon"))
        * float(fields.shape[3])
    )
    factor = jnp.float32(1.0 / counted**0.5)
    return (
        field_grad,
        (first * factor).astype(jnp.bfloat16),
        (second * factor).astype(jnp.bfloat16),
    )


def solution(mesh):
    placed = (P("dp", None, "lon", None), P("dp", None, "lon", None), P(), P(), P())
    return jax.shard_map(
        per_device,
        mesh=mesh,
        in_specs=placed,
        out_specs=(P("dp", None, "lon", None), P(), P()),
        check_vma=False,
    )
```

profile of v0, /device:TPU:0, one launch (start us, length us, event | category | flops | bytes accessed | tf_op | source)
XLA Modules:
  0.0 193.5 jit_solution(16097254031813786648)
XLA Ops:
  7.2 1.4 copy_dynamic-update-slice_fusion
  8.9 0.5 collective-permute-start
  9.4 4.1 %collective-permute-start.1 = (bf16[2,64,2,384]{3,1,2,0:T(8,128)(2,1)S(1)}, bf16[2,64,2,384]{3,1,2,0:T(8,128)(2,1)S(1)}, u32[]{:S(2)}, u32[]{:S(2)}) collective-permute-start(bf16[2,64,2,384]{3,1,2,0:T(8,128)(2,1)S(1)} %get-tuple-element.11), channel_id=1, source_target_pairs={{1,0},{2,1},{3,2},{4,3},{5,4},{6,5},{7,6},{0,7},{9,8},{10,9},{11,1... | collective-permute-start | bytes 589832 | tf_op jit(solution)/shard_map/ppermute | solution.py:17
  13.6 3.3 %collective-permute-done = bf16[2,64,2,384]{3,1,2,0:T(8,128)(2,1)S(1)} collective-permute-done((bf16[2,64,2,384]{3,1,2,0:T(8,128)(2,1)S(1)}, bf16[2,64,2,384]{3,1,2,0:T(8,128)(2,1)S(1)}, u32[]{:S(2)}, u32[]{:S(2)}) %collective-permute-start) | collective-permute-done | bytes 196640 | tf_op jit(solution)/shard_map/ppermute | solution.py:16
  17.5 0.7 copy-done.2
  18.1 0.5 fusion.16
  18.6 0.5 fusion.19
  19.1 0.5 fusion.22
  19.6 0.5 fusion.25
  20.1 0.5 fusion.28
  20.5 0.5 fusion.31
  21.4 0.6 multiply_convert_fusion
  22.4 1.3 multiply_convert_fusion.2
  23.8 0.7 convolution_bitcast_fusion.6
  24.9 0.7 convolution_bitcast_fusion.8
  25.6 0.5 convolution_bitcast_fusion.3
  26.5 0.5 convolution_bitcast_fusion.5
  27.0 0.7 convolution_bitcast_fusion
  28.1 0.7 convolution_bitcast_fusion.2
  29.3 0.5 fusion.42
  29.7 0.5 fusion.43
  30.6 0.5 fusion.45
  31.1 0.5 fusion.46
  31.6 0.6 fusion.10
  32.2 0.5 fusion.13
  32.7 1.9 fusion.6
  34.6 0.6 multiply_convert_fusion.1
  35.2 0.7 convolution_bitcast_fusion.15
  35.9 0.7 convolution_bitcast_fusion.17
  37.5 0.7 convolution_bitcast_fusion.11
  38.2 0.7 convolution_bitcast_fusion.9
  38.9 0.5 fusion.83
  39.4 1.6 fusion.84
  41.0 1.6 fusion.85
  42.6 1.6 fusion.86
  44.2 1.7 fusion.87
  45.9 1.6 fusion.48
  47.6 1.6 fusion.51
  49.2 1.6 fusion.92
  51.2 0.7 pad_maximum_fusion.4
  51.9 0.5 convolution_bitcast_fusion.10
  52.4 0.5 convolution_bitcast_fusion.16
  52.9 0.7 pad_maximum_fusion.3
  53.7 5.4 %fusion.8 = bf16[1,64,16,384]{3,1,2,0:T(8,128)(2,1)S(1)} fusion(f32[16,384,64]{1,2,0:T(8,128)S(1)} %fusion.83, f32[16,384,64]{1,2,0:T(8,128)} %fusion.84, f32[16,384,64]{1,2,0:T(8,128)} %fusion.51, f32[16,384,64]{1,2,0:T(8,128)} %fusion.92, f32[16,384,64]{1,2,0:T(8,128)} %fusion.48, f32[16,384,64]{1,2,0:T(8,128)} %fusion.85, f32[16,384,64]{1,2,0:T(8,128)} %fusion.87, ...), kind=kOutput, calls=%fused_computation.23 | convolution fusion | flops 54657024 | bytes 14958592 | tf_op jit(solution)/shard_map/oc,boij->bcij/dot_general | solution.py:64
  59.1 1.3 copy.36
  60.4 122.9 %all-reduce.8.cloned.1.call-done = (f32[3,3,64,64]{3,2,1,0:T(8,128)}, f32[3,3,64,64]{3,2,1,0:T(8,128)}) async-done(((f32[3,3,64,64]{3,2,1,0:T(8,128)}, f32[3,3,64,64]{3,2,1,0:T(8,128)}), (f32[3,3,64,64]{3,2,1,0:T(8,128)}, f32[3,3,64,64]{3,2,1,0:T(8,128)})) %all-reduce.8.cloned.1.call-update) | async-done | bytes 294928 | tf_op jit(solution)/shard_map/psum | solution.py:115
  183.3 1.7 multiply_convert_fusion.3
  185.0 1.7 multiply_convert_fusion.4
  (31 shorter events, 5.1 us)
Async XLA Ops:
  7.2 1.4 copy-start
  7.2 6.4 %copy-start.4 = (f32[384]{0:T(512)S(1)}, f32[384]{0:T(512)}, u32[]{:S(2)}) copy-start(f32[384]{0:T(512)} %param.9) | copy-start | bytes 4612
  7.2 176.1 %all-reduce.8.cloned.1.call-start = ((), (), s32[]{:S(2)}) async-start(), calls=%async_computation | async-start | bytes 1179648 | tf_op jit(solution)/shard_map/psum | solution.py:115
  8.9 8.0 %collective-permute-start = (bf16[2,64,2,384]{3,1,2,0:T(8,128)(2,1)S(1)}, bf16[2,64,2,384]{3,1,2,0:T(8,128)(2,1)S(1)}, u32[]{:S(2)}, u32[]{:S(2)}) collective-permute-start(bf16[2,64,2,384]{3,1,2,0:T(8,128)(2,1)S(1)} %get-tuple-element.10), channel_id=1, source_target_pairs={{0,1},{1,2},{2,3},{3,4},{4,5},{5,6},{6,7},{7,0},{8,9},{9,10},{10,1... | collective-permute-start | bytes 589832 | tf_op jit(solution)/shard_map/ppermute | solution.py:16
  9.4 7.5 %collective-permute-start.1 = (bf16[2,64,2,384]{3,1,2,0:T(8,128)(2,1)S(1)}, bf16[2,64,2,384]{3,1,2,0:T(8,128)(2,1)S(1)}, u32[]{:S(2)}, u32[]{:S(2)}) collective-permute-start(bf16[2,64,2,384]{3,1,2,0:T(8,128)(2,1)S(1)} %get-tuple-element.11), channel_id=1, source_target_pairs={{1,0},{2,1},{3,2},{4,3},{5,4},{6,5},{7,6},{0,7},{9,8},{10,9},{11,1... | collective-permute-start | bytes 589832 | tf_op jit(solution)/shard_map/ppermute | solution.py:17
  17.2 0.9 copy-start.2
  27.7 1.2 copy-start.3
  49.2 1.6 copy-start.1
Sparse Core Ops, SparseCore 0:
  53.8 129.4 all-reduce.7
where the time goes:
time: 194 us; the launch traced here: 193 us
  waiting for transfers between devices  126 us (65%)
  matrix products  37.8 us (19%)
  between operations  14.4 us (7%)
  other arithmetic  6.37 us (3%)
  starting transfers between devices  4.64 us (2%)
  local copies, waits for them, and re-layouts  4 us (2%)
    psum x1, waiting for transfers between devices, per_device(): first, second = lax.psum((first, second), ('dp', 'lon'))  123 us
    dot_general x18, matrix products, stencil_adjoint(): jnp.einsum('oc,boij->bcij', taps[p, q], source[:, :, 2 - p:2 - p + column...  23 us
    dot_general x18, matrix products, kernel_term(): jnp.einsum('boij,bcij->oc', source, padded[:, :, p:p + columns, q:q + lat...  9.91 us
    dot_general x9, matrix products, stencil_apply(): jnp.einsum('oc,bcij->boij', taps[p, q], padded[:, :, p:p + columns, q:q +...  4.92 us
    ppermute x1, starting transfers between devices, extended(): after = lax.ppermute(first, axis, down)  4.1 us
  transfers between devices with their start and end apart: 3, of which 2 were waited for; matrix products, arithmetic and copies ran while one was open for 4% of the time, Pallas kernels for 0%

commit v1 on v0

v1 whole, which is shorter than its diff:
```python
import functools

import jax
import jax.numpy as jnp
from jax import lax
from jax.experimental import pallas as pl
from jax.experimental.pallas import tpu as pltpu
from jax.sharding import PartitionSpec as P

gelu_coef = 0.7978845608
F32 = jnp.float32
BF16 = jnp.bfloat16
NT = (((1,), (1,)), ((), ()))


def gelu_pair(u):
    inner = jnp.tanh(gelu_coef * (u + 0.044715 * u * u * u))
    value = 0.5 * u * (1.0 + inner)
    slope = 0.5 * (1.0 + inner) + 0.5 * u * (1.0 - inner * inner) * gelu_coef * (
        1.0 + 3.0 * 0.044715 * u * u
    )
    return value, slope


def neighbours(v):
    lat = v.shape[-1]
    row = lax.broadcasted_iota(jnp.int32, v.shape, 1)
    zero = jnp.zeros_like(v)
    below = jnp.where(row == 0, zero, pltpu.roll(v, 1, 1))
    above = jnp.where(row == lat - 1, zero, pltpu.roll(v, lat - 1, 1))
    return below, above


def dot(a, b):
    return jnp.dot(a, b, preferred_element_type=F32)


def dot_nt(a, b):
    return lax.dot_general(a, b, NT, preferred_element_type=F32)


def put_three(ref, index, v, adjoint):
    channels = v.shape[0]
    below, above = neighbours(v)
    if adjoint:
        below, above = above, below
    ref[index, 0:channels, :] = below.astype(BF16)
    ref[index, channels : 2 * channels, :] = v.astype(BF16)
    ref[index, 2 * channels :, :] = above.astype(BF16)


def prepare(k_ref, forward_ref, adjoint_ref):
    c = k_ref.shape[-1]
    for p in range(3):
        if forward_ref is not None:
            forward_ref[p * c : (p + 1) * c, :] = jnp.concatenate(
                [k_ref[p, q].astype(F32) for q in range(3)], axis=1
            ).astype(BF16)
        adjoint_ref[p * c : (p + 1) * c, :] = jnp.concatenate(
            [k_ref[p, q].astype(F32).T for q in range(3)], axis=1
        ).astype(BF16)


def spread(i, x, e, metric, x3, e3, s3):
    put_three(x3, i, x, False)
    put_three(e3, i, e, True)
    scaled = (metric * e).astype(BF16).astype(F32)
    put_three(s3, i, scaled, True)


def products(i, w1, w2a, x3, e3, s3, y, z):
    c = x3.shape[1] // 3
    y[i] = dot(w1[...], x3[i])
    z[i, c : 2 * c, :] = dot(w2a[c : 2 * c, :], e3[i])
    sides = dot(jnp.concatenate([w2a[0:c, :], w2a[2 * c :, :]], axis=0), s3[i])
    z[i, 0:c, :] = sides[0:c]
    z[i, 2 * c :, :] = sides[c:]


def middle(i, metric, y, z):
    c = y.shape[1] // 3
    u = y[i, c : 2 * c, :] + metric * (y[i - 1, 0:c, :] + y[i + 1, 2 * c :, :])
    hidden, slope = gelu_pair(u)
    grad = z[i, c : 2 * c, :] + (z[i + 1, 0:c, :] + z[i - 1, 2 * c :, :])
    delta = (grad * slope).astype(BF16).astype(F32)
    return hidden.astype(BF16).astype(F32), delta, (metric * delta).astype(BF16).astype(F32)


def three_rows(plain, scaled, j):
    c = plain.shape[1] // 3
    mid = slice(c, 2 * c)
    return jnp.concatenate(
        [scaled[j + 1, mid, :], plain[j, mid, :], scaled[j - 1, mid, :]], axis=0
    )


def scatter_out(ref, value):
    c, n, lat = value.shape
    value = value.astype(F32).reshape(c * n, lat)
    for k in range(lat // 128):
        ref[k * c * n : (k + 1) * c * n, :] = value[:, k * 128 : (k + 1) * 128]


def strided(ref, i, c, n):
    count = ref.shape[0] // (c * n)
    return [(k, pl.ds(k * c * n + i, c, stride=n)) for k in range(count)]


def column(ref, i, c, n):
    return jnp.concatenate([ref[at, :] for _, at in strided(ref, i, c, n)], axis=1)


def interior_kernel(
    x_ref, e_ref, k1_ref, k2_ref, m_ref,
    g1_ref, g2_ref, d_ref, s_ref, w1_ref, w1a_ref, w2a_ref,
    xf, ef, x3, e3, s3, y, z, h3,
):
    c, n, lat = x_ref.shape
    metric = m_ref[...]
    prepare(k1_ref, w1_ref, w1a_ref)
    prepare(k2_ref, None, w2a_ref)
    scatter_out(xf, x_ref[...])
    scatter_out(ef, e_ref[...])

    def first_pass(i, carry):
        spread(i, column(xf, i, c, n), column(ef, i, c, n), metric, x3, e3, s3)
        products(i, w1_ref, w2a_ref, x3, e3, s3, y, z)
        return carry

    lax.fori_loop(0, n, first_pass, 0, unroll=2)

    blank = jnp.zeros((c, lat), BF16)
    for i in (0, n - 1):
        d_ref[i] = blank
        s_ref[i] = blank

    def second_pass(i, carry):
        hidden, delta, scaled = middle(i, metric, y, z)
        put_three(h3, i, hidden, False)
        d_ref[i] = delta.astype(BF16)
        s_ref[i] = scaled.astype(BF16)
        return carry

    lax.fori_loop(1, n - 1, second_pass, 0, unroll=2)

    g2_ref[...] = jnp.zeros_like(g2_ref)
    g1_ref[...] = jnp.zeros_like(g1_ref)
    for j in (0, n - 1):
        inner = 1 if j == 0 else n - 2
        rows = slice(0, c) if j == 0 else slice(2 * c, 3 * c)
        g1_ref[rows, :] += dot_nt(s_ref[inner], x3[j])

    def third_pass(j, carry):
        g2_ref[...] += dot_nt(three_rows(e3, s3, j), h3[j])
        left = jnp.concatenate([s_ref[j + 1], d_ref[j], s_ref[j - 1]], axis=0)
        g1_ref[...] += dot_nt(left, x3[j])
        return carry

    lax.fori_loop(1, n - 1, third_pass, 0, unroll=2)


def edge_kernel(
    before_ref, first_ref, last_ref, after_ref, m_ref, w1_ref, w2a_ref, g1_in, g2_in,
    g1_ref, g2_ref, d_ref, s_ref,
    x3, e3, s3, y, z, h3,
):
    metric = m_ref[...]
    c = before_ref.shape[2]
    total1, total2 = g1_in[...], g2_in[...]
    for side, pair in ((0, (before_ref, first_ref)), (1, (last_ref, after_ref))):
        base = 4 * side
        for k in range(4):
            source = pair[k // 2]
            spread(
                base + k, source[0, k % 2].astype(F32), source[1, k % 2].astype(F32), metric, x3, e3, s3
            )
            products(base + k, w1_ref, w2a_ref, x3, e3, s3, y, z)
        own = 2 if side == 0 else 1
        for k in (1, 2):
            hidden, delta, scaled = middle(base + k, metric, y, z)
            d_ref[2 * side + k - 1] = delta.astype(BF16)
            s_ref[2 * side + k - 1] = scaled.astype(BF16)
            if k == own:
                put_three(h3, side, hidden, False)
        j = base + own
        total2 = total2 + dot_nt(three_rows(e3, s3, j), h3[side])
        delta, scaled = d_ref[2 * side + own - 1], s_ref[2 * side + own - 1]
        total1 = total1 + jnp.concatenate(
            [dot_nt(scaled, x3[j - 1]), dot_nt(delta, x3[j]), dot_nt(scaled, x3[j + 1])], axis=0
        )
    for ref, total in ((g1_ref, total1), (g2_ref, total2)):
        half = total.shape[0] // 2
        tail = total[:, 2 * c :]
        ref[0 : 2 * half, :] = total[:, 0 : 2 * c].astype(BF16)
        ref[2 * half :, :] = jnp.concatenate([tail[0:half], tail[half:]], axis=1).astype(BF16)


def field_kernel(
    e_ref, d_in, s_in, de_ref, se_ref, w1a_ref, out_ref,
    d3, s3, zm, zs, ef,
):
    c, n, lat = e_ref.shape
    for place, edge in ((0, 0), (1, 1), (n, 2), (n + 1, 3)):
        put_three(d3, place, de_ref[edge].astype(F32), True)
        put_three(s3, place, se_ref[edge].astype(F32), True)

    def fill(i, carry):
        put_three(d3, i + 1, d_in[i].astype(F32), True)
        put_three(s3, i + 1, s_in[i].astype(F32), True)
        return carry

    lax.fori_loop(1, n - 1, fill, 0, unroll=2)

    sides = jnp.concatenate([w1a_ref[0:c, :], w1a_ref[2 * c :, :]], axis=0)

    def multiply(i, carry):
        zm[i] = dot(w1a_ref[c : 2 * c, :], d3[i])
        zs[i] = dot(sides, s3[i])
        return carry

    lax.fori_loop(0, n + 2, multiply, 0, unroll=2)
    scatter_out(ef, e_ref[...])

    def add(i, carry):
        place = i + 1
        grad = zm[place] + (zs[place + 1, 0:c, :] + zs[place - 1, c:, :])
        for k, at in strided(ef, i, c, n):
            ef[at, :] = ef[at, :] + grad[:, k * 128 : (k + 1) * 128]
        return carry

    lax.fori_loop(0, n, add, 0, unroll=2)
    for k in range(lat // 128):
        part = ef[k * c * n : (k + 1) * c * n, :].reshape(c, n, 128)
        out_ref[:, :, k * 128 : (k + 1) * 128] = part.astype(BF16)


def final_kernel(one_ref, two_ref, out1_ref, out2_ref):
    c = out1_ref.shape[-1]
    half = (one_ref.shape[0] // 3)
    for ref, out in ((one_ref, out1_ref), (two_ref, out2_ref)):
        for p in range(3):
            rows = slice(p * c, (p + 1) * c)
            out[p, 0] = ref[rows, 0:c]
            out[p, 1] = ref[rows, c : 2 * c]
        tail = ref[2 * half :, :]
        tail = jnp.concatenate([tail[:, 0:c], tail[:, c:]], axis=0)
        for p in range(3):
            out[p, 2] = tail[p * c : (p + 1) * c]


def vmem(count):
    return [pl.BlockSpec(memory_space=pltpu.VMEM)] * count


def call(kernel, outs, scratch, *args, flops=0):
    return pl.pallas_call(
        kernel,
        out_shape=[jax.ShapeDtypeStruct(s, d) for s, d in outs],
        in_specs=vmem(len(args)),
        out_specs=vmem(len(outs)),
        scratch_shapes=[pltpu.VMEM(s, d) for s, d in scratch],
        compiler_params=pltpu.CompilerParams(vmem_limit_bytes=56 * 2**20),
    )(*args)


def exchange(value, pairs):
    return lax.ppermute(value, ("dp", "lon"), pairs)


def one_sample(x, e, kernel_first, kernel_second, metric):
    c, n, lat = x.shape
    wide = 3 * c
    size = lax.axis_size("lon")
    up = [(i, (i + 1) % size) for i in range(size)]
    down = [(j, i) for i, j in up]
    both = jnp.stack((x, e))
    first = jnp.swapaxes(both[:, :, 0:2], 1, 2)
    last = jnp.swapaxes(both[:, :, n - 2 :], 1, 2)
    before = lax.ppermute(last, "lon", up)
    after = lax.ppermute(first, "lon", down)
    three = (wide, lat)
    g1, g2, d, s, w1, w1a, w2a = call(
        interior_kernel,
        [((wide, wide), F32)] * 2 + [((n, c, lat), BF16)] * 2 + [((wide, wide), BF16)] * 3,
        [((c * n * lat // 128, 128), F32)] * 2
        + [((n,) + three, BF16)] * 3
        + [((n,) + three, F32)] * 2
        + [((n,) + three, BF16)],
        x, e, kernel_first, kernel_second, metric,
    )
    packed = ((3 * wide // 2, 2 * c), BF16)
    p1, p2, de, se = call(
        edge_kernel,
        [packed] * 2 + [((4, c, lat), BF16)] * 2,
        [((8,) + three, BF16)] * 3 + [((8,) + three, F32)] * 2 + [((2,) + three, BF16)],
        before, first, last, after, metric, w1, w2a, g1, g2,
    )
    return p1, p2, (d, s, de, se, w1a)


def field_part(e, parts):
    c, n, lat = e.shape
    d, s, de, se, w1a = parts
    (out,) = call(
        field_kernel,
        [((c, n, lat), BF16)],
        [((n + 2, 3 * c, lat), BF16)] * 2
        + [((n + 2, c, lat), F32), ((n + 2, 2 * c, lat), F32), ((c * n * lat // 128, 128), F32)],
        e, d, s, de, se, w1a,
    )
    return out


def sum_everywhere(one, two, factor):
    dp, lon = lax.axis_size("dp"), lax.axis_size("lon")
    count = dp * lon
    if (dp & (dp - 1)) or (lon & (lon - 1)) or lon < 2:
        one, two = lax.psum((one.astype(F32), two.astype(F32)), ("dp", "lon"))
        return (one * factor).astype(BF16), (two * factor).astype(BF16)
    odd = lax.axis_index("lon") % 2 == 1
    swap = [(i, i ^ 1) for i in range(count)]
    kept = jnp.where(odd, two, one)
    got = exchange(jnp.where(odd, one, two), swap)
    total = kept.astype(F32) + got.astype(F32)
    inner = [1 << k for k in range(1, lon.bit_length() - 1)]
    outer = [lon << k for k in range(dp.bit_length() - 1)]
    bits = []
    while inner or outer:
        if outer:
            bits.append(outer.pop(0))
        if inner:
            bits.append(inner.pop())
    other = list(bits)
    for k in range(0, len(bits) - 1, 2):
        other[k], other[k + 1] = bits[k + 1], bits[k]
    for even_bit, odd_bit in zip(bits, other):
        sent = total.astype(BF16)
        got = exchange(sent, [(i, i ^ (odd_bit if i & 1 else even_bit)) for i in range(count)])
        total = sent.astype(F32) + got.astype(F32)
    mine = (total * factor).astype(BF16)
    theirs = exchange(mine, swap)
    return jnp.where(odd, theirs, mine), jnp.where(odd, mine, theirs)


def per_device(fields, cotangent, kernel_first, kernel_second, metric):
    samples, c, n, lat = fields.shape
    counted = (
        float(samples * lax.axis_size("dp")) * float(n * lax.axis_size("lon")) * float(lat)
    )
    factor = jnp.float32(1.0 / counted**0.5)
    row = metric.reshape(1, lat)
    one = two = None
    later = []
    for b in range(samples):
        p1, p2, parts = one_sample(fields[b], cotangent[b], kernel_first, kernel_second, row)
        later.append(parts)
        one = p1 if one is None else (one.astype(F32) + p1.astype(F32)).astype(BF16)
        two = p2 if two is None else (two.astype(F32) + p2.astype(F32)).astype(BF16)
    one, two = sum_everywhere(one, two, factor)
    field_grad = jnp.stack([field_part(cotangent[b], later[b]) for b in range(samples)])
    grad_first, grad_second = call(
        final_kernel, [((3, 3, c, c), BF16)] * 2, [], one, two
    )
    return field_grad, grad_first, grad_second


def solution(mesh):
    placed = (P("dp", None, "lon", None), P("dp", None, "lon", None), P(), P(), P())
    return jax.shard_map(
        per_device,
        mesh=mesh,
        in_specs=placed,
        out_specs=(P("dp", None, "lon", None), P(), P()),
        check_vma=False,
    )
```

time: 194 us -> 58.7 us (0.30)
  waiting for transfers between devices: 126 us -> 16 us
  matrix products: 37.8 us -> 0 us
  Pallas kernels: 0 us -> 26.4 us
  between operations: 14.4 us -> 0.78 us
  starting transfers between devices: 4.64 us -> 9.51 us
  other arithmetic: 6.37 us -> 2.61 us
    psum x1 -> x0, waiting for transfers between devices: 123 us -> none  [per_device(): first, second = lax.psum((first, second), ('dp', 'lon'))]
    dot_general x45 -> x0, matrix products: 37.8 us -> none  [the longest x18 23 us: stencil_adjoint(): jnp.einsum('oc,boij->bcij', taps[p, q], source[:, :, 2 - p:2 - p + column...]
    pallas_call x0 -> x4, Pallas kernels: none -> 26.4 us  [call(): pl.pallas_call(kernel, out_shape=[jax.ShapeDtypeStruct(s, d) for s, d in...]
    ppermute x2 -> x8, waiting for transfers between devices: 3.32 us -> 16 us  [the longest x6 16 us: exchange(): return lax.ppermute(value, ('dp', 'lon'), pairs)]
    ppermute x2 -> x8, starting transfers between devices: 4.61 us -> 9.51 us  [the longest x6 4.97 us: exchange(): return lax.ppermute(value, ('dp', 'lon'), pairs)]
    convert_element_type x4 -> x5, other arithmetic: 4.56 us -> 1.02 us  [the longest x4 0.99 us: sum_everywhere(): sent = total.astype(BF16)]
  transfers between devices with their start and end apart: 3 -> 8, of which waited for: 2 -> 5; matrix products, arithmetic and copies ran while one was open for 4% -> 1% of each run, Pallas kernels for 0% -> 35%
where the time goes in v1:
time: 58.7 us; the launch traced here: 58.3 us
  Pallas kernels  26.4 us (45%)
  waiting for transfers between devices  16 us (27%)
  starting transfers between devices  9.51 us (16%)
  local copies, waits for them, and re-layouts  3 us (5%)
  other arithmetic  2.61 us (4%)
  between operations  0.78 us (1%)
    pallas_call x4, Pallas kernels, call(): pl.pallas_call(kernel, out_shape=[jax.ShapeDtypeStruct(s, d) for s, d in...  26.4 us
    ppermute x6, waiting for transfers between devices, exchange(): return lax.ppermute(value, ('dp', 'lon'), pairs)  16 us
    ppermute x6, starting transfers between devices, exchange(): return lax.ppermute(value, ('dp', 'lon'), pairs)  4.97 us
    ppermute x1, starting transfers between devices, one_sample(): after = lax.ppermute(first, 'lon', down)  4.54 us
    unnamed x13, local copies, waits for them, and re-layouts  2.13 us
  transfers between devices with their start and end apart: 8, of which 5 were waited for; matrix products, arithmetic and copies ran while one was open for 1% of the time, Pallas kernels for 35%

profile of v1, /device:TPU:0, one launch (start us, length us, event | category | flops | bytes accessed | tf_op | source)
XLA Modules:
  0.0 58.3 jit_solution(2303869244900780253)
XLA Ops:
  0.6 0.0 copy-start
  0.6 1.4 %copy_dynamic-update-slice_fusion.1 = bf16[2,64,16,384]{3,1,2,0:T(8,128)(2,1)S(1)} fusion(bf16[1,64,16,384]{3,2,1,0:T(8,128)(2,1)} %param.5), kind=kLoop, calls=%fused_computation.1 | loop fusion | bytes 1572864
  2.0 0.0 copy-done
  2.0 0.0 copy-start.5
  2.1 0.3 copy_dynamic-update-slice_fusion
  2.4 0.0 copy-start.1
  2.4 0.0 copy-start.2
  2.4 4.5 %collective-permute-start.1 = (bf16[2,2,64,384]{3,2,1,0:T(8,128)(2,1)S(1)}, bf16[2,2,64,384]{3,2,1,0:T(8,128)(2,1)S(1)}, u32[]{:S(2)}, u32[]{:S(2)}) collective-permute-start(bf16[2,2,64,384]{3,2,1,0:T(8,128)(2,1)S(1)} %get-tuple-element.29.first_ref), channel_id=1, source_target_pairs={{1,0},{2,1},{3,2},{4,3},{5,4},{6,5},{7,6},{0,7},{9,8},{10,9},{11,1... | collective-permute-start | bytes 589832 | tf_op jit(solution)/shard_map/ppermute | solution.py:280
  6.9 0.0 collective-permute-start
  6.9 0.0 copy-done.5
  6.9 0.6 reshape.9.m_ref
  7.5 12.6 %shard_map.76 = (f32[192,192]{1,0:T(8,128)}, f32[192,192]{1,0:T(8,128)}, bf16[16,64,384]{2,1,0:T(8,128)(2,1)}, bf16[16,64,384]{2,1,0:T(8,128)(2,1)}, bf16[192,19...) custom-call(bf16[64,16,384]{2,1,0:T(8,128)(2,1)} %bitcast.9, bf16[64,16,384]{2,1,0:T(8,128)(2,1)} %bitcast.7, ...), custom_call_target="tpu_custom_call" | custom-call | tf_op jit(solution)/shard_map/pallas_call | solution.py:256
  20.1 0.0 collective-permute-done.1.after_ref
  20.1 0.0 copy-start.3
  20.1 0.0 collective-permute-done.before_ref
  20.1 0.0 copy-start.4
  20.1 0.0 copy-done.1
  20.1 0.0 copy-done.2
  20.2 0.6 %copy-done.3 = bf16[2,2,64,384]{3,2,1,0:T(8,128)(2,1)} copy-done((bf16[2,2,64,384]{3,2,1,0:T(8,128)(2,1)}, bf16[2,2,64,384]{3,2,1,0:T(8,128)(2,1)S(1)}, u32[]{:S(2)}) %copy-start.3) | copy-done | bytes 196632
  20.8 0.1 copy-done.4
  20.9 4.0 %shard_map.77 = (bf16[288,128]{1,0:T(8,128)(2,1)}, bf16[288,128]{1,0:T(8,128)(2,1)}, bf16[4,64,384]{2,1,0:T(8,128)(2,1)}, bf16[4,64,384]{2,1,0:T(8,128)(2,1)}) custom-call(bf16[2,2,64,384]{3,2,1,0:T(8,128)(2,1)} %copy-done.4, bf16[2,2,64,384]{3,2,1,0:T(8,128)(2,1)} %copy-done.1, bf16[2,2,64,384]{3,2,1,0:T(8,128)(2,1)} %copy-done.2, ...), custom_call_target="tpu_custom_call" | custom-call | tf_op jit(solution)/shard_map/pallas_call | solution.py:256
  24.9 0.9 %broadcast_select_fusion.2 = bf16[288,128]{1,0:T(8,128)(2,1)S(1)} fusion(bf16[288,128]{1,0:T(8,128)(2,1)} %get-tuple-element.26, bf16[288,128]{1,0:T(8,128)(2,1)} %get-tuple-element.25, pred[]{:T(512)S(6)} %eq.5), kind=kLoop, calls=%fused_computation.11 | loop fusion | flops 36864 | bytes 221185 | tf_op jit(solution)/shard_map/jit(_where)/select_n | solution.py:323
  25.8 0.1 collective-permute-start.2
  25.9 1.3 %collective-permute-done.2 = bf16[288,128]{1,0:T(8,128)(2,1)S(1)} collective-permute-done((bf16[288,128]{1,0:T(8,128)(2,1)S(1)}, bf16[288,128]{1,0:T(8,128)(2,1)S(1)}, u32[]{:S(2)}, u32[]{:S(2)}) %collective-permute-start.2) | collective-permute-done | bytes 73760 | tf_op jit(solution)/shard_map/ppermute | solution.py:267
  27.1 0.9 %add_convert_fusion.3 = bf16[288,128]{1,0:T(8,128)(2,1)S(1)} fusion(bf16[288,128]{1,0:T(8,128)(2,1)S(1)} %collective-permute-done.2, bf16[288,128]{1,0:T(8,128)(2,1)} %get-tuple-element.25, bf16[288,128]{1,0:T(8,128)(2,1)} %get-tuple-element.26, pred[]{:T(512)S(6)} %eq.5), kind=kLoop, calls=%fused_computation.8 | loop fusion | flops 184320 | bytes 294913 | tf_op jit(solution)/shard_map/convert_element_type | solution.py:337
  28.1 1.6 %collective-permute-start.3 = (bf16[288,128]{1,0:T(8,128)(2,1)S(1)}, bf16[288,128]{1,0:T(8,128)(2,1)S(1)}, u32[]{:S(2)}, u32[]{:S(2)}) collective-permute-start(bf16[288,128]{1,0:T(8,128)(2,1)S(1)} %add_convert_fusion.3), channel_id=1, source_target_pairs={{0,8},{1,5},{2,10},{3,7},{4,12},{5,1},{6,14},{7,3},{8,0},{9,13},{1... | collective-permute-start | bytes 221192 | tf_op jit(solution)/shard_map/ppermute | solution.py:267
  29.6 2.9 %collective-permute-done.3 = bf16[288,128]{1,0:T(8,128)(2,1)S(1)} collective-permute-done((bf16[288,128]{1,0:T(8,128)(2,1)S(1)}, bf16[288,128]{1,0:T(8,128)(2,1)S(1)}, u32[]{:S(2)}, u32[]{:S(2)}) %collective-permute-start.3) | collective-permute-done | bytes 73760 | tf_op jit(solution)/shard_map/ppermute | solution.py:267
  32.5 1.0 %collective-permute-start.4 = (bf16[288,128]{1,0:T(8,128)(2,1)S(1)}, bf16[288,128]{1,0:T(8,128)(2,1)S(1)}, u32[]{:S(2)}, u32[]{:S(2)}) collective-permute-start(bf16[288,128]{1,0:T(8,128)(2,1)S(1)} %add_convert_fusion.2), channel_id=1, source_target_pairs={{0,4},{1,9},{2,6},{3,11},{4,0},{5,13},{6,2},{7,15},{8,12},{9,1},{1... | collective-permute-start | bytes 221192 | tf_op jit(solution)/shard_map/ppermute | solution.py:267
  33.5 5.2 %collective-permute-done.4 = bf16[288,128]{1,0:T(8,128)(2,1)S(1)} collective-permute-done((bf16[288,128]{1,0:T(8,128)(2,1)S(1)}, bf16[288,128]{1,0:T(8,128)(2,1)S(1)}, u32[]{:S(2)}, u32[]{:S(2)}) %collective-permute-start.4) | collective-permute-done | bytes 73760 | tf_op jit(solution)/shard_map/ppermute | solution.py:267
  38.7 1.6 %collective-permute-start.5 = (bf16[288,128]{1,0:T(8,128)(2,1)S(1)}, bf16[288,128]{1,0:T(8,128)(2,1)S(1)}, u32[]{:S(2)}, u32[]{:S(2)}) collective-permute-start(bf16[288,128]{1,0:T(8,128)(2,1)S(1)} %add_convert_fusion.1), channel_id=1, source_target_pairs={{0,16},{1,3},{2,18},{3,1},{4,20},{5,7},{6,22},{7,5},{8,24},{9,11},... | collective-permute-start | bytes 221192 | tf_op jit(solution)/shard_map/ppermute | solution.py:267
  40.3 2.9 %collective-permute-done.5 = bf16[288,128]{1,0:T(8,128)(2,1)S(1)} collective-permute-done((bf16[288,128]{1,0:T(8,128)(2,1)S(1)}, bf16[288,128]{1,0:T(8,128)(2,1)S(1)}, u32[]{:S(2)}, u32[]{:S(2)}) %collective-permute-start.5) | collective-permute-done | bytes 73760 | tf_op jit(solution)/shard_map/ppermute | solution.py:267
  43.3 0.7 %collective-permute-start.6 = (bf16[288,128]{1,0:T(8,128)(2,1)S(1)}, bf16[288,128]{1,0:T(8,128)(2,1)S(1)}, u32[]{:S(2)}, u32[]{:S(2)}) collective-permute-start(bf16[288,128]{1,0:T(8,128)(2,1)S(1)} %add_convert_fusion), channel_id=1, source_target_pairs={{0,2},{1,17},{2,0},{3,19},{4,6},{5,21},{6,4},{7,23},{8,10},{9,25},... | collective-permute-start | bytes 221192 | tf_op jit(solution)/shard_map/ppermute | solution.py:267
  44.0 3.7 %collective-permute-done.6 = bf16[288,128]{1,0:T(8,128)(2,1)S(1)} collective-permute-done((bf16[288,128]{1,0:T(8,128)(2,1)S(1)}, bf16[288,128]{1,0:T(8,128)(2,1)S(1)}, u32[]{:S(2)}, u32[]{:S(2)}) %collective-permute-start.6) | collective-permute-done | bytes 73760 | tf_op jit(solution)/shard_map/ppermute | solution.py:267
  47.7 0.1 collective-permute-start.7
  47.8 8.0 %shard_map.78 = bf16[64,16,384]{2,1,0:T(8,128)(2,1)} custom-call(bf16[64,16,384]{2,1,0:T(8,128)(2,1)} %bitcast.8, bf16[16,64,384]{2,1,0:T(8,128)(2,1)} %get-tuple-element.16.d_in, bf16[16,64,384]{2,1,0:T(8,128)(2,1)} %get-tuple-element.17.s_in, bf16[4,64,384]{2,1,0:T(8,128)(2,1)} %get-tuple-element.22.de_ref, bf16[4,64,384]{2,1,0:T(8,128)(2,1)} %get-tuple-element.23.se_ref, ...), custom_call_target="tpu_custom_call" | custom-call | tf_op jit(solution)/shard_map/pallas_call | solution.py:256
  55.9 0.0 collective-permute-done.7
  55.9 0.7 %broadcast_select_fusion = (bf16[288,128]{1,0:T(8,128)(2,1)}, bf16[288,128]{1,0:T(8,128)(2,1)}) fusion(bf16[288,128]{1,0:T(8,128)(2,1)S(1)} %multiply_convert_fusion, bf16[288,128]{1,0:T(8,128)(2,1)S(1)} %collective-permute-done.7, pred[]{:T(512)S(6)} %eq.5), kind=kLoop, calls=%fused_computation.9 | loop fusion | flops 73728 | bytes 294913 | tf_op jit(solution)/shard_map/jit(_where)/select_n | solution.py:342
  56.5 1.7 %shard_map.79 = (bf16[3,3,64,64]{3,2,1,0:T(8,128)(2,1)}, bf16[3,3,64,64]{3,2,1,0:T(8,128)(2,1)}) custom-call(bf16[288,128]{1,0:T(8,128)(2,1)} %get-tuple-element.32.one_ref, bf16[288,128]{1,0:T(8,128)(2,1)} %get-tuple-element.31.two_ref), custom_call_target="tpu_custom_call" | custom-call | tf_op jit(solution)/shard_map/pallas_call | solution.py:256
  (5 shorter events, 0.1 us)
Async XLA Ops:
  0.6 1.4 %copy-start = (bf16[1,64,16,384]{3,2,1,0:T(8,128)(2,1)S(1)}, bf16[1,64,16,384]{3,2,1,0:T(8,128)(2,1)}, u32[]{:S(2)}) copy-start(bf16[1,64,16,384]{3,2,1,0:T(8,128)(2,1)} %param.6) | copy-start | bytes 2359300
  2.0 4.9 %copy-start.5 = (f32[384]{0:T(512)S(1)}, f32[384]{0:T(512)}, u32[]{:S(2)}) copy-start(f32[384]{0:T(512)} %param.9) | copy-start | bytes 4612
  2.4 17.8 %copy-start.1 = (bf16[2,2,64,384]{3,2,1,0:T(8,128)(2,1)}, bf16[2,2,64,384]{3,2,1,0:T(8,128)(2,1)S(1)}, u32[]{:S(2)}) copy-start(bf16[2,2,64,384]{3,2,1,0:T(8,128)(2,1)S(1)} %get-tuple-element.29.first_ref) | copy-start | bytes 589828
  2.4 17.8 %copy-start.2 = (bf16[2,2,64,384]{3,2,1,0:T(8,128)(2,1)}, bf16[2,2,64,384]{3,2,1,0:T(8,128)(2,1)S(1)}, u32[]{:S(2)}) copy-start(bf16[2,2,64,384]{3,2,1,0:T(8,128)(2,1)S(1)} %get-tuple-element.30.last_ref) | copy-start | bytes 589828
  2.4 17.7 %collective-permute-start.1 = (bf16[2,2,64,384]{3,2,1,0:T(8,128)(2,1)S(1)}, bf16[2,2,64,384]{3,2,1,0:T(8,128)(2,1)S(1)}, u32[]{:S(2)}, u32[]{:S(2)}) collective-permute-start(bf16[2,2,64,384]{3,2,1,0:T(8,128)(2,1)S(1)} %get-tuple-element.29.first_ref), channel_id=1, source_target_pairs={{1,0},{2,1},{3,2},{4,3},{5,4},{6,5},{7,6},{0,7},{9,8},{10,9},{11,1... | collective-permute-start | bytes 589832 | tf_op jit(solution)/shard_map/ppermute | solution.py:280
  6.9 13.2 %collective-permute-start = (bf16[2,2,64,384]{3,2,1,0:T(8,128)(2,1)S(1)}, bf16[2,2,64,384]{3,2,1,0:T(8,128)(2,1)S(1)}, u32[]{:S(2)}, u32[]{:S(2)}) collective-permute-start(bf16[2,2,64,384]{3,2,1,0:T(8,128)(2,1)S(1)} %get-tuple-element.30.last_ref), channel_id=1, source_target_pairs={{0,1},{1,2},{2,3},{3,4},{4,5},{5,6},{6,7},{7,0},{8,9},{9,10},{10,1... | collective-permute-start | bytes 589832 | tf_op jit(solution)/shard_map/ppermute | solution.py:279
  20.1 0.7 %copy-start.3 = (bf16[2,2,64,384]{3,2,1,0:T(8,128)(2,1)}, bf16[2,2,64,384]{3,2,1,0:T(8,128)(2,1)S(1)}, u32[]{:S(2)}) copy-start(bf16[2,2,64,384]{3,2,1,0:T(8,128)(2,1)S(1)} %collective-permute-done.1.after_ref) | copy-start | bytes 589828
  20.1 0.8 %copy-start.4 = (bf16[2,2,64,384]{3,2,1,0:T(8,128)(2,1)}, bf16[2,2,64,384]{3,2,1,0:T(8,128)(2,1)S(1)}, u32[]{:S(2)}) copy-start(bf16[2,2,64,384]{3,2,1,0:T(8,128)(2,1)S(1)} %collective-permute-done.before_ref) | copy-start | bytes 589828
  25.8 1.3 %collective-permute-start.2 = (bf16[288,128]{1,0:T(8,128)(2,1)S(1)}, bf16[288,128]{1,0:T(8,128)(2,1)S(1)}, u32[]{:S(2)}, u32[]{:S(2)}) collective-permute-start(bf16[288,128]{1,0:T(8,128)(2,1)S(1)} %broadcast_select_fusion.2), channel_id=1, source_target_pairs={{0,1},{1,0},{2,3},{3,2},{4,5},{5,4},{6,7},{7,6},{8,9},{9,8},{10,11... | collective-permute-start | bytes 221192 | tf_op jit(solution)/shard_map/ppermute | solution.py:267
  28.1 4.4 %collective-permute-start.3 = (bf16[288,128]{1,0:T(8,128)(2,1)S(1)}, bf16[288,128]{1,0:T(8,128)(2,1)S(1)}, u32[]{:S(2)}, u32[]{:S(2)}) collective-permute-start(bf16[288,128]{1,0:T(8,128)(2,1)S(1)} %add_convert_fusion.3), channel_id=1, source_target_pairs={{0,8},{1,5},{2,10},{3,7},{4,12},{5,1},{6,14},{7,3},{8,0},{9,13},{1... | collective-permute-start | bytes 221192 | tf_op jit(solution)/shard_map/ppermute | solution.py:267
  32.5 6.2 %collective-permute-start.4 = (bf16[288,128]{1,0:T(8,128)(2,1)S(1)}, bf16[288,128]{1,0:T(8,128)(2,1)S(1)}, u32[]{:S(2)}, u32[]{:S(2)}) collective-permute-start(bf16[288,128]{1,0:T(8,128)(2,1)S(1)} %add_convert_fusion.2), channel_id=1, source_target_pairs={{0,4},{1,9},{2,6},{3,11},{4,0},{5,13},{6,2},{7,15},{8,12},{9,1},{1... | collective-permute-start | bytes 221192 | tf_op jit(solution)/shard_map/ppermute | solution.py:267
  38.7 4.5 %collective-permute-start.5 = (bf16[288,128]{1,0:T(8,128)(2,1)S(1)}, bf16[288,128]{1,0:T(8,128)(2,1)S(1)}, u32[]{:S(2)}, u32[]{:S(2)}) collective-permute-start(bf16[288,128]{1,0:T(8,128)(2,1)S(1)} %add_convert_fusion.1), channel_id=1, source_target_pairs={{0,16},{1,3},{2,18},{3,1},{4,20},{5,7},{6,22},{7,5},{8,24},{9,11},... | collective-permute-start | bytes 221192 | tf_op jit(solution)/shard_map/ppermute | solution.py:267
  43.3 4.4 %collective-permute-start.6 = (bf16[288,128]{1,0:T(8,128)(2,1)S(1)}, bf16[288,128]{1,0:T(8,128)(2,1)S(1)}, u32[]{:S(2)}, u32[]{:S(2)}) collective-permute-start(bf16[288,128]{1,0:T(8,128)(2,1)S(1)} %add_convert_fusion), channel_id=1, source_target_pairs={{0,2},{1,17},{2,0},{3,19},{4,6},{5,21},{6,4},{7,23},{8,10},{9,25},... | collective-permute-start | bytes 221192 | tf_op jit(solution)/shard_map/ppermute | solution.py:267
  47.7 8.1 %collective-permute-start.7 = (bf16[288,128]{1,0:T(8,128)(2,1)S(1)}, bf16[288,128]{1,0:T(8,128)(2,1)S(1)}, u32[]{:S(2)}, u32[]{:S(2)}) collective-permute-start(bf16[288,128]{1,0:T(8,128)(2,1)S(1)} %multiply_convert_fusion), channel_id=1, source_target_pairs={{0,1},{1,0},{2,3},{3,2},{4,5},{5,4},{6,7},{7,6},{8,9},{9,8},{10,11... | collective-permute-start | bytes 221192 | tf_op jit(solution)/shard_map/ppermute | solution.py:267

commit v2 on v1

v2 whole, which is shorter than its diff:
```python
import functools
import math

import jax
import jax.numpy as jnp
from jax import lax
from jax.experimental import pallas as pl
from jax.experimental.pallas import tpu as pltpu
from jax.sharding import PartitionSpec as P

gelu_coef = 0.7978845608
F32 = jnp.float32
BF16 = jnp.bfloat16
NT = (((1,), (1,)), ((), ()))


def gelu_pair(u):
    inner = jnp.tanh(gelu_coef * (u + 0.044715 * u * u * u))
    value = 0.5 * u * (1.0 + inner)
    slope = 0.5 * (1.0 + inner) + 0.5 * u * (1.0 - inner * inner) * gelu_coef * (
        1.0 + 3.0 * 0.044715 * u * u
    )
    return value, slope


def neighbours(v):
    lat = v.shape[-1]
    row = lax.broadcasted_iota(jnp.int32, v.shape, 1)
    zero = jnp.zeros_like(v)
    below = jnp.where(row == 0, zero, pltpu.roll(v, 1, 1))
    above = jnp.where(row == lat - 1, zero, pltpu.roll(v, lat - 1, 1))
    return below, above


def dot(a, b):
    return jnp.dot(a, b, preferred_element_type=F32)


def dot_nt(a, b):
    return lax.dot_general(a, b, NT, preferred_element_type=F32)


def put_three(ref, index, v, adjoint):
    channels = v.shape[0]
    v = v.astype(BF16)
    below, above = neighbours(v)
    if adjoint:
        below, above = above, below
    ref[index, 0:channels, :] = below
    ref[index, channels : 2 * channels, :] = v
    ref[index, 2 * channels :, :] = above


def prepare(k_ref, forward_ref, adjoint_ref):
    c = k_ref.shape[-1]
    for p in range(3):
        if forward_ref is not None:
            forward_ref[p * c : (p + 1) * c, :] = jnp.concatenate(
                [k_ref[p, q].astype(F32) for q in range(3)], axis=1
            ).astype(BF16)
        adjoint_ref[p * c : (p + 1) * c, :] = jnp.concatenate(
            [k_ref[p, q].astype(F32).T for q in range(3)], axis=1
        ).astype(BF16)


def spread(i, x, e, metric, x3, e3, s3):
    put_three(x3, i, x, False)
    put_three(e3, i, e, True)
    scaled = (metric * e).astype(BF16).astype(F32)
    put_three(s3, i, scaled, True)


def products(i, w1, w2a, x3, e3, s3, y, z):
    c = x3.shape[1] // 3
    y[i] = dot(w1[...], x3[i])
    z[i, c : 2 * c, :] = dot(w2a[c : 2 * c, :], e3[i])
    sides = dot(jnp.concatenate([w2a[0:c, :], w2a[2 * c :, :]], axis=0), s3[i])
    z[i, 0:c, :] = sides[0:c]
    z[i, 2 * c :, :] = sides[c:]


def middle(i, metric, y, z):
    c = y.shape[1] // 3
    u = y[i, c : 2 * c, :] + metric * (y[i - 1, 0:c, :] + y[i + 1, 2 * c :, :])
    hidden, slope = gelu_pair(u)
    grad = z[i, c : 2 * c, :] + (z[i + 1, 0:c, :] + z[i - 1, 2 * c :, :])
    delta = (grad * slope).astype(BF16).astype(F32)
    return hidden.astype(BF16).astype(F32), delta, (metric * delta).astype(BF16).astype(F32)


def three_rows(plain, scaled, j):
    c = plain.shape[1] // 3
    mid = slice(c, 2 * c)
    return jnp.concatenate(
        [scaled[j + 1, mid, :], plain[j, mid, :], scaled[j - 1, mid, :]], axis=0
    )


def scatter_out(ref, value):
    c, n, lat = value.shape
    value = value.astype(F32).reshape(c * n, lat)
    for k in range(lat // 128):
        ref[k * c * n : (k + 1) * c * n, :] = value[:, k * 128 : (k + 1) * 128]


def strided(ref, i, c, n):
    count = ref.shape[0] // (c * n)
    return [(k, pl.ds(k * c * n + i, c, stride=n)) for k in range(count)]


def column(ref, i, c, n):
    return jnp.concatenate([ref[at, :] for _, at in strided(ref, i, c, n)], axis=1)


def interior_kernel(
    x_ref, e_ref, k1_ref, k2_ref, m_ref,
    g1_ref, g2_ref, d_ref, s_ref, w1_ref, w1a_ref, w2a_ref,
    xf, ef, x3, e3, s3, y, z, h3,
):
    c, n, lat = x_ref.shape
    metric = m_ref[...]
    prepare(k1_ref, w1_ref, w1a_ref)
    prepare(k2_ref, None, w2a_ref)
    scatter_out(xf, x_ref[...])
    scatter_out(ef, e_ref[...])

    blank = jnp.zeros((c, lat), BF16)
    for i in (0, n - 1):
        d_ref[i] = blank
        s_ref[i] = blank
    g1_ref[...] = jnp.zeros_like(g1_ref)
    g2_ref[...] = jnp.zeros_like(g2_ref)

    def second_terms(columns):
        left = jnp.concatenate([three_rows(e3, s3, j) for j in columns], axis=1)
        g2_ref[...] += dot_nt(left, jnp.concatenate([h3[j] for j in columns], axis=1))

    def first_terms(columns):
        left = [
            jnp.concatenate([s_ref[j + 1], d_ref[j], s_ref[j - 1]], axis=0) for j in columns
        ]
        right = jnp.concatenate([x3[j] for j in columns], axis=1)
        g1_ref[...] += dot_nt(jnp.concatenate(left, axis=1), right)

    inner = list(range(1, n - 1))
    groups = [inner[k : k + 7] for k in range(0, n - 2, 7)]
    second_todo, first_todo = list(groups), list(groups)
    for i in range(n + 1):
        if i < n:
            spread(i, column(xf, i, c, n), column(ef, i, c, n), metric, x3, e3, s3)
            products(i, w1_ref, w2a_ref, x3, e3, s3, y, z)
        if 1 <= i - 1 < n - 1:
            hidden, delta, scaled = middle(i - 1, metric, y, z)
            put_three(h3, i - 1, hidden, False)
            d_ref[i - 1] = delta.astype(BF16)
            s_ref[i - 1] = scaled.astype(BF16)
        if i == 3:
            g1_ref[0:c, :] += dot_nt(s_ref[1], x3[0])
        ready = i - 2 if i < n else n - 2
        if second_todo and second_todo[0][-1] <= ready:
            second_terms(second_todo.pop(0))
        if first_todo and first_todo[0][-1] <= (ready - 1 if i < n else ready):
            first_terms(first_todo.pop(0))
    for columns in second_todo:
        second_terms(columns)
    for columns in first_todo:
        first_terms(columns)
    g1_ref[2 * c :, :] += dot_nt(s_ref[n - 2], x3[n - 1])


def edge_kernel(
    before_ref, first_ref, last_ref, after_ref, m_ref, w1_ref, w2a_ref, g1_in, g2_in,
    kept_ref, sent_ref, d_ref, s_ref,
    x3, e3, s3, y, z, h3,
):
    metric = m_ref[...]
    c = before_ref.shape[2]
    total1, total2 = g1_in[...], g2_in[...]
    for side, pair in ((0, (before_ref, first_ref)), (1, (last_ref, after_ref))):
        base = 4 * side
        for k in range(4):
            source = pair[k // 2]
            spread(
                base + k, source[0, k % 2].astype(F32), source[1, k % 2].astype(F32), metric, x3, e3, s3
            )
            products(base + k, w1_ref, w2a_ref, x3, e3, s3, y, z)
        own = 2 if side == 0 else 1
        for k in (1, 2):
            hidden, delta, scaled = middle(base + k, metric, y, z)
            d_ref[2 * side + k - 1] = delta.astype(BF16)
            s_ref[2 * side + k - 1] = scaled.astype(BF16)
            if k == own:
                put_three(h3, side, hidden, False)
        j = base + own
        total2 = total2 + dot_nt(three_rows(e3, s3, j), h3[side])
        delta, scaled = d_ref[2 * side + own - 1], s_ref[2 * side + own - 1]
        total1 = total1 + jnp.concatenate(
            [dot_nt(scaled, x3[j - 1]), dot_nt(delta, x3[j]), dot_nt(scaled, x3[j + 1])], axis=0
        )
    odd = lax.axis_index("lon") % 2 == 1
    for ref, total in (
        (kept_ref, jnp.where(odd, total2, total1)),
        (sent_ref, jnp.where(odd, total1, total2)),
    ):
        half = total.shape[0] // 2
        tail = total[:, 2 * c :]
        ref[0 : 2 * half, :] = total[:, 0 : 2 * c].astype(ref.dtype)
        ref[2 * half :, :] = jnp.concatenate([tail[0:half], tail[half:]], axis=1).astype(ref.dtype)


def field_kernel(d_in, s_in, de_ref, se_ref, w1a_ref, out_ref, d3, s3, zm, zs, *, start):
    c, n = d_in.shape[1], d_in.shape[0]
    count = out_ref.shape[0]
    sides = jnp.concatenate([w1a_ref[0:c, :], w1a_ref[2 * c :, :]], axis=0)
    edges = {-1: 0, 0: 1, n - 1: 2, n: 3}
    for place in range(count + 2):
        i = start + place - 1
        d, s = (de_ref[edges[i]], se_ref[edges[i]]) if i in edges else (d_in[i], s_in[i])
        put_three(d3, place, d, True)
        put_three(s3, place, s, True)
        zm[place] = dot(w1a_ref[c : 2 * c, :], d3[place])
        zs[place] = dot(sides, s3[place])
        if place >= 2:
            out_ref[place - 2] = zm[place - 1] + (zs[place, 0:c, :] + zs[place - 2, c:, :])


def assemble_kernel(*refs):
    e_ref, parts, out_ref, ef = refs[0], refs[1:-2], refs[-2], refs[-1]
    c, n, lat = e_ref.shape
    scatter_out(ef, e_ref[...])
    i = 0
    for part in parts:
        for k in range(part.shape[0]):
            grad = part[k]
            for t, at in strided(ef, i, c, n):
                ef[at, :] = ef[at, :] + grad[:, t * 128 : (t + 1) * 128]
            i += 1
    for k in range(lat // 128):
        part = ef[k * c * n : (k + 1) * c * n, :].reshape(c, n, 128)
        out_ref[:, :, k * 128 : (k + 1) * 128] = part.astype(BF16)


def final_kernel(mine_ref, theirs_ref, out1_ref, out2_ref):
    c = out1_ref.shape[-1]
    odd = lax.axis_index("lon") % 2 == 1
    mine, theirs = mine_ref[...], theirs_ref[...]
    for out, packed in (
        (out1_ref, jnp.where(odd, theirs, mine)),
        (out2_ref, jnp.where(odd, mine, theirs)),
    ):
        tail = packed[3 * c :]
        tail = jnp.concatenate([tail[:, 0:c], tail[:, c:]], axis=0)
        for p in range(3):
            rows = slice(p * c, (p + 1) * c)
            out[p, 0] = packed[rows, 0:c]
            out[p, 1] = packed[rows, c:]
            out[p, 2] = tail[rows]


def vmem(count):
    return [pl.BlockSpec(memory_space=pltpu.VMEM)] * count


def size_of(shapes):
    return sum(math.prod(s) * jnp.dtype(d).itemsize for s, d in shapes)


def call(kernel, outs, scratch, *args):
    mib = 2**20
    limit = size_of(scratch) + size_of(outs) + size_of([(a.shape, a.dtype) for a in args])
    return pl.pallas_call(
        kernel,
        out_shape=[jax.ShapeDtypeStruct(s, d) for s, d in outs],
        in_specs=vmem(len(args)),
        out_specs=vmem(len(outs)),
        scratch_shapes=[pltpu.VMEM(s, d) for s, d in scratch],
        compiler_params=pltpu.CompilerParams(vmem_limit_bytes=(limit // mib + 6) * mib),
    )(*args)


def exchange(value, pairs):
    return lax.ppermute(value, ("dp", "lon"), pairs)


def one_sample(x, e, kernel_first, kernel_second, metric):
    c, n, lat = x.shape
    wide = 3 * c
    size = lax.axis_size("lon")
    up = [(i, (i + 1) % size) for i in range(size)]
    down = [(j, i) for i, j in up]
    first = jnp.swapaxes(jnp.stack((x[:, 0:2], e[:, 0:2])), 1, 2)
    last = jnp.swapaxes(jnp.stack((x[:, n - 2 :], e[:, n - 2 :])), 1, 2)
    before = lax.ppermute(last, "lon", up)
    after = lax.ppermute(first, "lon", down)
    three = (wide, lat)
    g1, g2, d, s, w1, w1a, w2a = call(
        interior_kernel,
        [((wide, wide), F32)] * 2 + [((n, c, lat), BF16)] * 2 + [((wide, wide), BF16)] * 3,
        [((c * n * lat // 128, 128), F32)] * 2
        + [((n,) + three, BF16)] * 3
        + [((n,) + three, F32)] * 2
        + [((n,) + three, BF16)],
        x, e, kernel_first, kernel_second, metric,
    )
    packed = (3 * wide // 2, 2 * c)
    kept, sent, de, se = call(
        edge_kernel,
        [(packed, F32), (packed, BF16)] + [((4, c, lat), BF16)] * 2,
        [((8,) + three, BF16)] * 3 + [((8,) + three, F32)] * 2 + [((2,) + three, BF16)],
        before, first, last, after, metric, w1, w2a, g1, g2,
    )
    return kept, sent, (d, s, de, se, w1a)


def field_parts(parts, pieces):
    n, c, lat = parts[0].shape
    wide = 3 * c
    made, start = [], 0
    for k in range(pieces):
        stop = n * (k + 1) // pieces
        count = stop - start
        made.append(
            functools.partial(
                call,
                functools.partial(field_kernel, start=start),
                [((count, c, lat), F32)],
                [((count + 2, wide, lat), BF16)] * 2
                + [((count + 2, c, lat), F32), ((count + 2, 2 * c, lat), F32)],
                *parts,
            )
        )
        start = stop
    return made


def assemble(e, grads):
    c, n, lat = e.shape
    return call(
        assemble_kernel, [((c, n, lat), BF16)], [((c * n * lat // 128, 128), F32)], e, *grads
    )[0]


def sum_everywhere(kept, sent, factor, jobs):
    dp, lon = lax.axis_size("dp"), lax.axis_size("lon")
    count = dp * lon
    swap = [(i, i ^ 1) for i in range(count)]
    total = kept + exchange(sent, swap).astype(F32)
    inner = [1 << k for k in range(1, lon.bit_length() - 1)]
    outer = [lon << k for k in range(dp.bit_length() - 1)]
    bits = []
    while inner or outer:
        if outer:
            bits.append(outer.pop(0))
        if inner:
            bits.append(inner.pop())
    other = list(bits)
    for k in range(0, len(bits) - 1, 2):
        other[k], other[k + 1] = bits[k + 1], bits[k]
    results = []
    for even_bit, odd_bit in zip(bits, other):
        sent = total.astype(BF16)
        got = exchange(sent, [(i, i ^ (odd_bit if i & 1 else even_bit)) for i in range(count)])
        if jobs:
            sent, job_args = lax.optimization_barrier((sent, jobs[0][1](results)))
            results.append(jobs.pop(0)[0](*job_args))
            got, results[-1] = lax.optimization_barrier((got, results[-1]))
        total = sent.astype(F32) + got.astype(F32)
    for job in jobs:
        results.append(job[0](*job[1](results)))
    mine = (total * factor).astype(BF16)
    return mine, exchange(mine, swap), results


def per_device(fields, cotangent, kernel_first, kernel_second, metric):
    samples, c, n, lat = fields.shape
    counted = (
        float(samples * lax.axis_size("dp")) * float(n * lax.axis_size("lon")) * float(lat)
    )
    factor = jnp.float32(1.0 / counted**0.5)
    row = metric.reshape(1, lat)
    kept = sent = None
    jobs = []
    pieces = 2
    for b in range(samples):
        k, t, parts = one_sample(fields[b], cotangent[b], kernel_first, kernel_second, row)
        kept = k if kept is None else kept + k
        sent = t if sent is None else (sent.astype(F32) + t.astype(F32)).astype(BF16)
        for job in field_parts(parts, pieces):
            jobs.append((lambda *args, job=job: job.func(*job.args[:3], *args)[0], lambda done, job=job: job.args[3:]))
        jobs.append((
            lambda *args: assemble(args[0], args[1:]),
            lambda done, b=b: (cotangent[b],) + tuple(done[-pieces:]),
        ))
    mine, theirs, results = sum_everywhere(kept, sent, factor, jobs)
    field_grad = jnp.stack(results[pieces :: pieces + 1])
    grad_first, grad_second = call(
        final_kernel, [((3, 3, c, c), BF16)] * 2, [], mine, theirs
    )
    return field_grad, grad_first, grad_second


def solution(mesh):
    placed = (P("dp", None, "lon", None), P("dp", None, "lon", None), P(), P(), P())
    return jax.shard_map(
        per_device,
        mesh=mesh,
        in_specs=placed,
        out_specs=(P("dp", None, "lon", None), P(), P()),
        check_vma=False,
    )
```

time: 58.7 us -> 39.6 us (0.67)
  Pallas kernels: 26.4 us -> 11.7 us
  other arithmetic: 2.61 us -> 0.67 us
  starting transfers between devices: 9.51 us -> 8.03 us
    pallas_call x4 -> x6, Pallas kernels: 26.4 us -> 11.7 us  [call(): pl.pallas_call(kernel, out_shape=[jax.ShapeDtypeStruct(s, d) for s, d in...]
    select_n x2 -> x0, other arithmetic: 1.59 us -> none  [the longest x1 0.9 us: sum_everywhere(): got = exchange(jnp.where(odd, one, two), swap)]
    ppermute x6, starting transfers between devices: 4.97 us -> 3.43 us  [exchange(): return lax.ppermute(value, ('dp', 'lon'), pairs)]
    unnamed x13 -> x10, local copies, waits for them, and re-layouts: 2.13 us -> 0.66 us
    another operation x1, local copies, waits for them, and re-layouts: 0.26 us -> 1.71 us  [one_sample(): first = jnp.swapaxes(jnp.stack((x[:, 0:2], e[:, 0:2])), 1, 2)]
    ppermute x6, waiting for transfers between devices: 16 us -> 14.7 us  [exchange(): return lax.ppermute(value, ('dp', 'lon'), pairs)]
    ppermute x1, waiting for transfers between devices: 0.01 us -> 0.99 us  [one_sample(): before = lax.ppermute(last, 'lon', up)]
    convert_element_type x4, other arithmetic: 0.99 us -> 0.09 us  [sum_everywhere(): sent = total.astype(BF16)]
  transfers between devices with their start and end apart: 8 -> 8, of which waited for: 5 -> 7; matrix products, arithmetic and copies ran while one was open for 1% -> 1% of each run, Pallas kernels for 35% -> 23%
where the time goes in v2:
time: 39.6 us; the launch traced here: 39.4 us
  waiting for transfers between devices  15.7 us (40%)
  Pallas kernels  11.7 us (30%)
  starting transfers between devices  8.03 us (20%)
  local copies, waits for them, and re-layouts  2.47 us (6%)
  between operations  0.83 us (2%)
  other arithmetic  0.67 us (2%)
    ppermute x6, waiting for transfers between devices, exchange(): return lax.ppermute(value, ('dp', 'lon'), pairs)  14.7 us
    pallas_call x6, Pallas kernels, call(): pl.pallas_call(kernel, out_shape=[jax.ShapeDtypeStruct(s, d) for s, d in...  11.7 us
    ppermute x1, starting transfers between devices, one_sample(): after = lax.ppermute(first, 'lon', down)  4.54 us
    ppermute x6, starting transfers between devices, exchange(): return lax.ppermute(value, ('dp', 'lon'), pairs)  3.43 us
    another operation x1, local copies, waits for them, and re-layouts, one_sample(): first = jnp.swapaxes(jnp.stack((x[:, 0:2], e[:, 0:2])), 1, 2)  1.71 us
    ppermute x1, waiting for transfers between devices, one_sample(): before = lax.ppermute(last, 'lon', up)  0.99 us
  transfers between devices with their start and end apart: 8, of which 7 were waited for; matrix products, arithmetic and copies ran while one was open for 1% of the time, Pallas kernels for 23%

profile of v2, /device:TPU:0, one launch (start us, length us, event | category | flops | bytes accessed | tf_op | source)
XLA Modules:
  0.0 39.4 jit_solution(11201598532699732050)
XLA Ops:
  0.6 0.0 copy-start.2
  0.6 0.0 copy-start.3
  0.7 1.7 %slice_bitcast_fusion = (bf16[1,64,2,384]{3,2,1,0:T(2,128)(2,1)S(1)}, bf16[1,64,2,384]{3,2,1,0:T(2,128)(2,1)S(1)}, bf16[1,64,2,384]{3,2,1,0:T(2,128)(2,1)S(1)}, bf16[1,64,2,384]{3,2,1,0:T(2,128)(2,1)S(1)}) fusion(bf16[64,16,384]{2,1,0:T(8,128)(2,1)} %bitcast.15, bf16[64,16,384]{2,1,0:T(8,128)(2,1)} %bitcast.18), kind=kLoop, calls=%fused_computation.7 | loop fusion | bytes 786432 | tf_op jit(solution)/shard_map/stack | solution.py:291
  2.4 0.0 copy-start
  2.4 0.0 copy-start.1
  2.4 0.3 maximum_bitcast_fusion.1
  2.7 4.5 %collective-permute-start.1 = (bf16[2,2,64,384]{3,1,2,0:T(2,128)(2,1)S(1)}, bf16[2,2,64,384]{3,1,2,0:T(2,128)(2,1)S(1)}, u32[]{:S(2)}, u32[]{:S(2)}) collective-permute-start(bf16[2,2,64,384]{3,1,2,0:T(2,128)(2,1)S(1)} %maximum_bitcast_fusion.1), channel_id=1, source_target_pairs={{1,0},{2,1},{3,2},{4,3},{5,4},{6,5},{7,6},{0,7},{9,8},{10,9},{11,1... | collective-permute-start | bytes 589832 | tf_op jit(solution)/shard_map/ppermute | solution.py:294
  7.2 0.3 maximum_bitcast_fusion
  7.5 0.1 collective-permute-start
  7.6 0.0 copy-start.4
  7.6 0.6 %copy-done.4 = f32[384]{0:T(512)S(1)} copy-done((f32[384]{0:T(512)S(1)}, f32[384]{0:T(512)}, u32[]{:S(2)}) %copy-start.4) | copy-done | bytes 1560
  8.3 0.0 copy-done.2
  8.3 0.0 copy-done.3
  8.3 0.0 copy-done
  8.3 0.0 copy-done.1
  8.3 5.1 %shard_map.76 = (f32[192,192]{1,0:T(8,128)S(1)}, f32[192,192]{1,0:T(8,128)S(1)}, bf16[16,64,384]{2,1,0:T(8,128)(2,1)S(1)}, bf16[16,64,384]{2,1,0:T(8,128)(2,1)S(...) custom-call(bf16[64,16,384]{2,1,0:T(8,128)(2,1)S(1)} %bitcast.19, ...), custom_call_target="tpu_custom_call" | custom-call | tf_op jit(solution)/shard_map/pallas_call | solution.py:271
  13.4 0.0 collective-permute-done.1
  13.4 1.0 %collective-permute-done = bf16[2,2,64,384]{3,1,2,0:T(2,128)(2,1)S(1)} collective-permute-done((bf16[2,2,64,384]{3,1,2,0:T(2,128)(2,1)S(1)}, bf16[2,2,64,384]{3,1,2,0:T(2,128)(2,1)S(1)}, u32[]{:S(2)}, u32[]{:S(2)}) %collective-permute-start) | collective-permute-done | bytes 196640 | tf_op jit(solution)/shard_map/ppermute | solution.py:293
  14.5 1.9 %shard_map.77 = (f32[288,128]{1,0:T(8,128)S(1)}, bf16[288,128]{1,0:T(8,128)(2,1)S(1)}, bf16[4,64,384]{2,1,0:T(8,128)(2,1)S(1)}, bf16[4,64,384]{2,1,0:T(8,128)(2,1)S(1)}) custom-call(bf16[2,2,64,384]{3,2,1,0:T(8,128)(2,1)S(1)} %copy.8.before_ref, bf16[2,2,64,384]{3,2,1,0:T(8,128)(2,1)S(1)} %copy.9.first_ref, bf16[2,2,64,384]{3,2,1,0:T(8,128)(2,1)S(1)} %copy.10.last_ref, ...), custom_call_target="tpu_custom_call" | custom-call | tf_op jit(solution)/shard_map/pallas_call | solution.py:271
  16.4 0.1 collective-permute-start.2
  16.5 1.3 %collective-permute-done.2 = bf16[288,128]{1,0:T(8,128)(2,1)S(1)} collective-permute-done((bf16[288,128]{1,0:T(8,128)(2,1)S(1)}, bf16[288,128]{1,0:T(8,128)(2,1)S(1)}, u32[]{:S(2)}, u32[]{:S(2)}) %collective-permute-start.2) | collective-permute-done | bytes 73760 | tf_op jit(solution)/shard_map/ppermute | solution.py:282
  17.8 1.6 %collective-permute-start.3 = (bf16[288,128]{1,0:T(8,128)(2,1)S(1)}, bf16[288,128]{1,0:T(8,128)(2,1)S(1)}, u32[]{:S(2)}, u32[]{:S(2)}) collective-permute-start(bf16[288,128]{1,0:T(8,128)(2,1)S(1)} %add_convert_fusion.3), channel_id=1, source_target_pairs={{0,8},{1,5},{2,10},{3,7},{4,12},{5,1},{6,14},{7,3},{8,0},{9,13},{1... | collective-permute-start | bytes 221192 | tf_op jit(solution)/shard_map/ppermute | solution.py:282
  19.3 0.9 %shard_map.78.refs_1_ = f32[8,64,384]{2,1,0:T(8,128)S(1)} custom-call(bf16[16,64,384]{2,1,0:T(8,128)(2,1)S(1)} %get-tuple-element.57.d_in, bf16[16,64,384]{2,1,0:T(8,128)(2,1)S(1)} %get-tuple-element.58.s_in, bf16[4,64,384]{2,1,0:T(8,128)(2,1)S(1)} %get-tuple-element.59.de_ref, bf16[4,64,384]{2,1,0:T(8,128)(2,1)S(1)} %get-tuple-element.60.se_ref, ...), custom_call_target="tpu_custom_call" | custom-call | tf_op jit(solution)/shard_map/pallas_call | solution.py:271
  20.3 1.9 %collective-permute-done.3 = bf16[288,128]{1,0:T(8,128)(2,1)S(1)} collective-permute-done((bf16[288,128]{1,0:T(8,128)(2,1)S(1)}, bf16[288,128]{1,0:T(8,128)(2,1)S(1)}, u32[]{:S(2)}, u32[]{:S(2)}) %collective-permute-start.3) | collective-permute-done | bytes 73760 | tf_op jit(solution)/shard_map/ppermute | solution.py:282
  22.2 0.1 collective-permute-start.4
  22.3 0.9 %shard_map.79.refs_2_ = f32[8,64,384]{2,1,0:T(8,128)S(1)} custom-call(bf16[16,64,384]{2,1,0:T(8,128)(2,1)S(1)} %get-tuple-element.57.d_in, bf16[16,64,384]{2,1,0:T(8,128)(2,1)S(1)} %get-tuple-element.58.s_in, bf16[4,64,384]{2,1,0:T(8,128)(2,1)S(1)} %get-tuple-element.59.de_ref, bf16[4,64,384]{2,1,0:T(8,128)(2,1)S(1)} %get-tuple-element.60.se_ref, ...), custom_call_target="tpu_custom_call" | custom-call | tf_op jit(solution)/shard_map/pallas_call | solution.py:271
  23.2 4.8 %collective-permute-done.4 = bf16[288,128]{1,0:T(8,128)(2,1)S(1)} collective-permute-done((bf16[288,128]{1,0:T(8,128)(2,1)S(1)}, bf16[288,128]{1,0:T(8,128)(2,1)S(1)}, u32[]{:S(2)}, u32[]{:S(2)}) %collective-permute-start.4) | collective-permute-done | bytes 73760 | tf_op jit(solution)/shard_map/ppermute | solution.py:282
  28.0 1.6 %collective-permute-start.5 = (bf16[288,128]{1,0:T(8,128)(2,1)S(1)}, bf16[288,128]{1,0:T(8,128)(2,1)S(1)}, u32[]{:S(2)}, u32[]{:S(2)}) collective-permute-start(bf16[288,128]{1,0:T(8,128)(2,1)S(1)} %add_convert_fusion.1), channel_id=1, source_target_pairs={{0,16},{1,3},{2,18},{3,1},{4,20},{5,7},{6,22},{7,5},{8,24},{9,11},... | collective-permute-start | bytes 221192 | tf_op jit(solution)/shard_map/ppermute | solution.py:282
  29.6 2.0 %shard_map.80 = bf16[64,16,384]{2,1,0:T(8,128)(2,1)} custom-call(bf16[64,16,384]{2,1,0:T(8,128)(2,1)S(1)} %bitcast.17, f32[8,64,384]{2,1,0:T(8,128)S(1)} %shard_map.78.refs_1_, f32[8,64,384]{2,1,0:T(8,128)S(1)} %shard_map.79.refs_2_), custom_call_target="tpu_custom_call" | custom-call | tf_op jit(solution)/shard_map/pallas_call | solution.py:271
  31.6 1.2 %collective-permute-done.5 = bf16[288,128]{1,0:T(8,128)(2,1)S(1)} collective-permute-done((bf16[288,128]{1,0:T(8,128)(2,1)S(1)}, bf16[288,128]{1,0:T(8,128)(2,1)S(1)}, u32[]{:S(2)}, u32[]{:S(2)}) %collective-permute-start.5) | collective-permute-done | bytes 73760 | tf_op jit(solution)/shard_map/ppermute | solution.py:282
  32.8 0.1 collective-permute-start.6
  32.9 4.3 %collective-permute-done.6 = bf16[288,128]{1,0:T(8,128)(2,1)S(1)} collective-permute-done((bf16[288,128]{1,0:T(8,128)(2,1)S(1)}, bf16[288,128]{1,0:T(8,128)(2,1)S(1)}, u32[]{:S(2)}, u32[]{:S(2)}) %collective-permute-start.6) | collective-permute-done | bytes 73760 | tf_op jit(solution)/shard_map/ppermute | solution.py:282
  37.3 0.1 collective-permute-start.7
  37.3 1.3 %collective-permute-done.7.theirs_ref = bf16[288,128]{1,0:T(8,128)(2,1)S(1)} collective-permute-done((bf16[288,128]{1,0:T(8,128)(2,1)S(1)}, bf16[288,128]{1,0:T(8,128)(2,1)S(1)}, u32[]{:S(2)}, u32[]{:S(2)}) %collective-permute-start.7) | collective-permute-done | bytes 73760 | tf_op jit(solution)/shard_map/ppermute | solution.py:282
  38.6 0.8 %shard_map.81 = (bf16[3,3,64,64]{3,2,1,0:T(8,128)(2,1)}, bf16[3,3,64,64]{3,2,1,0:T(8,128)(2,1)}) custom-call(bf16[288,128]{1,0:T(8,128)(2,1)S(1)} %multiply_convert_fusion.mine_ref, bf16[288,128]{1,0:T(8,128)(2,1)S(1)} %collective-permute-done.7.theirs_ref), custom_call_target="tpu_custom_call" | custom-call | tf_op jit(solution)/shard_map/pallas_call | solution.py:271
  (10 shorter events, 0.2 us)
Async XLA Ops:
  0.6 7.6 %copy-start.2 = (bf16[3,3,64,64]{3,2,1,0:T(8,128)(2,1)S(1)}, bf16[3,3,64,64]{3,2,1,0:T(8,128)(2,1)}, u32[]{:S(2)}) copy-start(bf16[3,3,64,64]{3,2,1,0:T(8,128)(2,1)} %k1_ref.1) | copy-start | bytes 221188
  0.6 7.6 %copy-start.3 = (bf16[3,3,64,64]{3,2,1,0:T(8,128)(2,1)S(1)}, bf16[3,3,64,64]{3,2,1,0:T(8,128)(2,1)}, u32[]{:S(2)}) copy-start(bf16[3,3,64,64]{3,2,1,0:T(8,128)(2,1)} %k2_ref.1) | copy-start | bytes 221188
  2.4 5.9 %copy-start = (bf16[1,64,16,384]{3,2,1,0:T(8,128)(2,1)S(1)}, bf16[1,64,16,384]{3,2,1,0:T(8,128)(2,1)}, u32[]{:S(2)}) copy-start(bf16[1,64,16,384]{3,2,1,0:T(8,128)(2,1)} %param.6) | copy-start | bytes 2359300
  2.4 5.9 %copy-start.1 = (bf16[1,64,16,384]{3,2,1,0:T(8,128)(2,1)S(1)}, bf16[1,64,16,384]{3,2,1,0:T(8,128)(2,1)}, u32[]{:S(2)}) copy-start(bf16[1,64,16,384]{3,2,1,0:T(8,128)(2,1)} %param.5) | copy-start | bytes 2359300
  2.7 10.7 %collective-permute-start.1 = (bf16[2,2,64,384]{3,1,2,0:T(2,128)(2,1)S(1)}, bf16[2,2,64,384]{3,1,2,0:T(2,128)(2,1)S(1)}, u32[]{:S(2)}, u32[]{:S(2)}) collective-permute-start(bf16[2,2,64,384]{3,1,2,0:T(2,128)(2,1)S(1)} %maximum_bitcast_fusion.1), channel_id=1, source_target_pairs={{1,0},{2,1},{3,2},{4,3},{5,4},{6,5},{7,6},{0,7},{9,8},{10,9},{11,1... | collective-permute-start | bytes 589832 | tf_op jit(solution)/shard_map/ppermute | solution.py:294
  7.5 6.9 %collective-permute-start = (bf16[2,2,64,384]{3,1,2,0:T(2,128)(2,1)S(1)}, bf16[2,2,64,384]{3,1,2,0:T(2,128)(2,1)S(1)}, u32[]{:S(2)}, u32[]{:S(2)}) collective-permute-start(bf16[2,2,64,384]{3,1,2,0:T(2,128)(2,1)S(1)} %maximum_bitcast_fusion), channel_id=1, source_target_pairs={{0,1},{1,2},{2,3},{3,4},{4,5},{5,6},{6,7},{7,0},{8,9},{9,10},{10,1... | collective-permute-start | bytes 589832 | tf_op jit(solution)/shard_map/ppermute | solution.py:293
  7.6 0.7 %copy-start.4 = (f32[384]{0:T(512)S(1)}, f32[384]{0:T(512)}, u32[]{:S(2)}) copy-start(f32[384]{0:T(512)} %param.9) | copy-start | bytes 4612
  16.4 1.3 %collective-permute-start.2 = (bf16[288,128]{1,0:T(8,128)(2,1)S(1)}, bf16[288,128]{1,0:T(8,128)(2,1)S(1)}, u32[]{:S(2)}, u32[]{:S(2)}) collective-permute-start(bf16[288,128]{1,0:T(8,128)(2,1)S(1)} %get-tuple-element.43), channel_id=1, source_target_pairs={{0,1},{1,0},{2,3},{3,2},{4,5},{5,4},{6,7},{7,6},{8,9},{9,8},{10,11... | collective-permute-start | bytes 221192 | tf_op jit(solution)/shard_map/ppermute | solution.py:282
  17.8 4.4 %collective-permute-start.3 = (bf16[288,128]{1,0:T(8,128)(2,1)S(1)}, bf16[288,128]{1,0:T(8,128)(2,1)S(1)}, u32[]{:S(2)}, u32[]{:S(2)}) collective-permute-start(bf16[288,128]{1,0:T(8,128)(2,1)S(1)} %add_convert_fusion.3), channel_id=1, source_target_pairs={{0,8},{1,5},{2,10},{3,7},{4,12},{5,1},{6,14},{7,3},{8,0},{9,13},{1... | collective-permute-start | bytes 221192 | tf_op jit(solution)/shard_map/ppermute | solution.py:282
  22.2 5.8 %collective-permute-start.4 = (bf16[288,128]{1,0:T(8,128)(2,1)S(1)}, bf16[288,128]{1,0:T(8,128)(2,1)S(1)}, u32[]{:S(2)}, u32[]{:S(2)}) collective-permute-start(bf16[288,128]{1,0:T(8,128)(2,1)S(1)} %add_convert_fusion.2), channel_id=1, source_target_pairs={{0,4},{1,9},{2,6},{3,11},{4,0},{5,13},{6,2},{7,15},{8,12},{9,1},{1... | collective-permute-start | bytes 221192 | tf_op jit(solution)/shard_map/ppermute | solution.py:282
  28.0 4.8 %collective-permute-start.5 = (bf16[288,128]{1,0:T(8,128)(2,1)S(1)}, bf16[288,128]{1,0:T(8,128)(2,1)S(1)}, u32[]{:S(2)}, u32[]{:S(2)}) collective-permute-start(bf16[288,128]{1,0:T(8,128)(2,1)S(1)} %add_convert_fusion.1), channel_id=1, source_target_pairs={{0,16},{1,3},{2,18},{3,1},{4,20},{5,7},{6,22},{7,5},{8,24},{9,11},... | collective-permute-start | bytes 221192 | tf_op jit(solution)/shard_map/ppermute | solution.py:282
  32.8 4.4 %collective-permute-start.6 = (bf16[288,128]{1,0:T(8,128)(2,1)S(1)}, bf16[288,128]{1,0:T(8,128)(2,1)S(1)}, u32[]{:S(2)}, u32[]{:S(2)}) collective-permute-start(bf16[288,128]{1,0:T(8,128)(2,1)S(1)} %add_convert_fusion), channel_id=1, source_target_pairs={{0,2},{1,17},{2,0},{3,19},{4,6},{5,21},{6,4},{7,23},{8,10},{9,25},... | collective-permute-start | bytes 221192 | tf_op jit(solution)/shard_map/ppermute | solution.py:282
  37.3 1.3 %collective-permute-start.7 = (bf16[288,128]{1,0:T(8,128)(2,1)S(1)}, bf16[288,128]{1,0:T(8,128)(2,1)S(1)}, u32[]{:S(2)}, u32[]{:S(2)}) collective-permute-start(bf16[288,128]{1,0:T(8,128)(2,1)S(1)} %multiply_convert_fusion.mine_ref), channel_id=1, source_target_pairs={{0,1},{1,0},{2,3},{3,2},{4,5},{5,4},{6,7},{7,6},{8,9},{9,8},{10,11... | collective-permute-start | bytes 221192 | tf_op jit(solution)/shard_map/ppermute | solution.py:282

commit v3 on v2

--- a/solution.py
+++ b/solution.py
@@ -63,15 +63,36 @@
         ).astype(BF16)
 
 
+class Columns:
+    def __init__(self, place):
+        self.place = place
+
+    def __getitem__(self, at):
+        i, rest = (at[0], at[1:]) if isinstance(at, tuple) else (at, ())
+        ref, k = self.place[i]
+        return ref[(k,) + rest]
+
+    def __setitem__(self, at, value):
+        i, rest = (at[0], at[1:]) if isinstance(at, tuple) else (at, ())
+        ref, k = self.place[i]
+        ref[(k,) + rest] = value
+
+
+def split(outside, edges, inside):
+    return Columns(
+        {i: (outside, edges.index(i)) if i in edges else (inside, i) for i in range(inside.shape[0])}
+    )
+
+
 def spread(i, x, e, metric, x3, e3, s3):
     put_three(x3, i, x, False)
     put_three(e3, i, e, True)
-    scaled = (metric * e).astype(BF16).astype(F32)
+    scaled = (metric * e).astype(BF16)
     put_three(s3, i, scaled, True)
 
 
 def products(i, w1, w2a, x3, e3, s3, y, z):
-    c = x3.shape[1] // 3
+    c = w1.shape[0] // 3
     y[i] = dot(w1[...], x3[i])
     z[i, c : 2 * c, :] = dot(w2a[c : 2 * c, :], e3[i])
     sides = dot(jnp.concatenate([w2a[0:c, :], w2a[2 * c :, :]], axis=0), s3[i])
@@ -80,27 +101,29 @@
 
 
 def middle(i, metric, y, z):
-    c = y.shape[1] // 3
+    c = z[i].shape[0] // 3
     u = y[i, c : 2 * c, :] + metric * (y[i - 1, 0:c, :] + y[i + 1, 2 * c :, :])
     hidden, slope = gelu_pair(u)
     grad = z[i, c : 2 * c, :] + (z[i + 1, 0:c, :] + z[i - 1, 2 * c :, :])
-    delta = (grad * slope).astype(BF16).astype(F32)
-    return hidden.astype(BF16).astype(F32), delta, (metric * delta).astype(BF16).astype(F32)
+    delta = (grad * slope).astype(BF16)
+    return hidden.astype(BF16), delta, (metric * delta.astype(F32)).astype(BF16)
 
 
 def three_rows(plain, scaled, j):
-    c = plain.shape[1] // 3
+    c = plain[j].shape[0] // 3
     mid = slice(c, 2 * c)
     return jnp.concatenate(
         [scaled[j + 1, mid, :], plain[j, mid, :], scaled[j - 1, mid, :]], axis=0
     )
 
 
-def scatter_out(ref, value):
+def scatter_out(ref, value, first=0):
     c, n, lat = value.shape
     value = value.astype(F32).reshape(c * n, lat)
+    whole = ref.shape[0] * 128 // lat
     for k in range(lat // 128):
-        ref[k * c * n : (k + 1) * c * n, :] = value[:, k * 128 : (k + 1) * 128]
+        at = k * whole + first
+        ref[at : at + c * n, :] = value[:, k * 128 : (k + 1) * 128]
 
 
 def strided(ref, i, c, n):
@@ -112,18 +135,51 @@
     return jnp.concatenate([ref[at, :] for _, at in strided(ref, i, c, n)], axis=1)
 
 
+def pack_kernel(
+    x_hbm, e_hbm, m_hbm, xf, ef, mate_ref, outer_ref, row_ref, xs, es, ms, sems, row_sem
+):
+    c, n, lat = x_hbm.shape
+    chunks = sems.shape[1]
+    w = c // chunks
+    copies = []
+    for k in range(chunks):
+        for a, (src, dst) in enumerate(((x_hbm, xs), (e_hbm, es))):
+            rows = pl.ds(k * w, w)
+            copies.append(pltpu.make_async_copy(src.at[rows], dst.at[rows], sems.at[a, k]))
+            copies[-1].start()
+    row_copy = pltpu.make_async_copy(m_hbm, ms, row_sem)
+    row_copy.start()
+    for k in range(chunks):
+        for a, (src, dst) in enumerate(((xs, xf), (es, ef))):
+            copies[2 * k + a].wait()
+            scatter_out(dst, src[k * w : (k + 1) * w], k * w * n)
+    odd = lax.axis_index("lon") % 2 == 1
+    for a, source in enumerate((xf, ef)):
+        for k in range(2):
+            low = column(source, k, c, n).astype(BF16)
+            high = column(source, n - 2 + k, c, n).astype(BF16)
+            mate_ref[a, k] = jnp.where(odd, low, high)
+            outer_ref[a, k] = jnp.where(odd, high, low)
+    row_copy.wait()
+    row_ref[...] = ms[...].reshape(1, lat)
+
+
 def interior_kernel(
-    x_ref, e_ref, k1_ref, k2_ref, m_ref,
-    g1_ref, g2_ref, d_ref, s_ref, w1_ref, w1a_ref, w2a_ref,
-    xf, ef, x3, e3, s3, y, z, h3,
+    xf, ef, k1_ref, k2_ref, m_ref,
+    g1_ref, g2_ref, d_ref, s_ref, w1_ref, w1a_ref, w2a_ref, x3_out, e3_out, s3_out, y_out, z_out,
+    x3_in, e3_in, s3_in, y_in, z_in, h3,
 ):
-    c, n, lat = x_ref.shape
+    n, c, lat = d_ref.shape
     metric = m_ref[...]
     prepare(k1_ref, w1_ref, w1a_ref)
     prepare(k2_ref, None, w2a_ref)
-    scatter_out(xf, x_ref[...])
-    scatter_out(ef, e_ref[...])
-
+    edges = (0, 1, n - 2, n - 1)
+    x3, e3, s3, y, z = (
+        split(outside, edges, inside)
+        for outside, inside in (
+            (x3_out, x3_in), (e3_out, e3_in), (s3_out, s3_in), (y_out, y_in), (z_out, z_in)
+        )
+    )
     blank = jnp.zeros((c, lat), BF16)
     for i in (0, n - 1):
         d_ref[i] = blank
@@ -152,8 +208,8 @@
         if 1 <= i - 1 < n - 1:
             hidden, delta, scaled = middle(i - 1, metric, y, z)
             put_three(h3, i - 1, hidden, False)
-            d_ref[i - 1] = delta.astype(BF16)
-            s_ref[i - 1] = scaled.astype(BF16)
+            d_ref[i - 1] = delta
+            s_ref[i - 1] = scaled
         if i == 3:
             g1_ref[0:c, :] += dot_nt(s_ref[1], x3[0])
         ready = i - 2 if i < n else n - 2
@@ -168,39 +224,74 @@
     g1_ref[2 * c :, :] += dot_nt(s_ref[n - 2], x3[n - 1])
 
 
+def parity():
+    place = lax.axis_index("dp") * lax.axis_size("lon") + lax.axis_index("lon")
+    total, left = 0, lax.axis_size("dp") * lax.axis_size("lon") - 1
+    while left:
+        total, place, left = total + place % 2, place // 2, left // 2
+    return total % 2
+
+
 def edge_kernel(
-    before_ref, first_ref, last_ref, after_ref, m_ref, w1_ref, w2a_ref, g1_in, g2_in,
+    to_mate, to_outer, from_mate, from_outer, m_ref, w1, w2a, g1_in, g2_in, x3_own, e3_own, s3_own, y_own, z_own,
     kept_ref, sent_ref, d_ref, s_ref,
-    x3, e3, s3, y, z, h3,
+    x3_far, e3_far, s3_far, y_far, z_far, h3,
 ):
     metric = m_ref[...]
-    c = before_ref.shape[2]
+    c = to_mate.shape[2]
+    odd = lax.axis_index("lon") % 2 == 1
+    low, mid, high = slice(0, c), slice(c, 2 * c), slice(2 * c, 3 * c)
+    far, own = (0, 1, 6, 7), (2, 3, 4, 5)
+
+    def both(outside, inside):
+        places = {i: (outside, k) for k, i in enumerate(far)}
+        places.update({i: (inside, k) for k, i in enumerate(own)})
+        return Columns(places)
+
+    x3, e3, s3, y, z = (
+        both(*pair)
+        for pair in (
+            (x3_far, x3_own), (e3_far, e3_own), (s3_far, s3_own), (y_far, y_own), (z_far, z_own)
+        )
+    )
     total1, total2 = g1_in[...], g2_in[...]
-    for side, pair in ((0, (before_ref, first_ref)), (1, (last_ref, after_ref))):
+    for side in range(2):
         base = 4 * side
-        for k in range(4):
-            source = pair[k // 2]
-            spread(
-                base + k, source[0, k % 2].astype(F32), source[1, k % 2].astype(F32), metric, x3, e3, s3
+        for k in range(2):
+            i = base + 2 * side + k
+            x, e = (
+                jnp.where(odd, from_outer[a, k], from_mate[a, k])
+                if side
+                else jnp.where(odd, from_mate[a, k], from_outer[a, k])
+                for a in range(2)
             )
-            products(base + k, w1_ref, w2a_ref, x3, e3, s3, y, z)
-        own = 2 if side == 0 else 1
+            put_three(x3, i, x, False)
+            scaled = (metric * e.astype(F32)).astype(BF16)
+            put_three(s3, i, scaled, True)
+            near = k != side
+            one, two = (high, low) if side else (low, high)
+            y[i, one, :] = dot(w1[one, :], x3[i])
+            z[i, two, :] = dot(w2a[two, :], s3[i])
+            if near:
+                put_three(e3, i, e, True)
+                y[i, mid, :] = dot(w1[mid, :], x3[i])
+                z[i, mid, :] = dot(w2a[mid, :], e3[i])
         for k in (1, 2):
             hidden, delta, scaled = middle(base + k, metric, y, z)
-            d_ref[2 * side + k - 1] = delta.astype(BF16)
-            s_ref[2 * side + k - 1] = scaled.astype(BF16)
-            if k == own:
+            d_ref[2 * side + k - 1] = delta
+            s_ref[2 * side + k - 1] = scaled
+            if k == 2 - side:
                 put_three(h3, side, hidden, False)
-        j = base + own
-        total2 = total2 + dot_nt(three_rows(e3, s3, j), h3[side])
-        delta, scaled = d_ref[2 * side + own - 1], s_ref[2 * side + own - 1]
-        total1 = total1 + jnp.concatenate(
-            [dot_nt(scaled, x3[j - 1]), dot_nt(delta, x3[j]), dot_nt(scaled, x3[j + 1])], axis=0
-        )
-    odd = lax.axis_index("lon") % 2 == 1
+                j = base + k
+                total2 = total2 + dot_nt(three_rows(e3, s3, j), h3[side])
+                total1 = total1 + jnp.concatenate(
+                    [dot_nt(scaled, x3[j - 1]), dot_nt(delta, x3[j]), dot_nt(scaled, x3[j + 1])],
+                    axis=0,
+                )
+    keeps_second = parity() == 1
     for ref, total in (
-        (kept_ref, jnp.where(odd, total2, total1)),
-        (sent_ref, jnp.where(odd, total1, total2)),
+        (kept_ref, jnp.where(keeps_second, total2, total1)),
+        (sent_ref, jnp.where(keeps_second, total1, total2)),
     ):
         half = total.shape[0] // 2
         tail = total[:, 2 * c :]
@@ -226,14 +317,13 @@
 
 def assemble_kernel(*refs):
     e_ref, parts, out_ref, ef = refs[0], refs[1:-2], refs[-2], refs[-1]
-    c, n, lat = e_ref.shape
-    scatter_out(ef, e_ref[...])
+    c, n, lat = out_ref.shape
     i = 0
     for part in parts:
         for k in range(part.shape[0]):
             grad = part[k]
             for t, at in strided(ef, i, c, n):
-                ef[at, :] = ef[at, :] + grad[:, t * 128 : (t + 1) * 128]
+                ef[at, :] = e_ref[at, :] + grad[:, t * 128 : (t + 1) * 128]
             i += 1
     for k in range(lat // 128):
         part = ef[k * c * n : (k + 1) * c * n, :].reshape(c, n, 128)
@@ -242,7 +332,7 @@
 
 def final_kernel(mine_ref, theirs_ref, out1_ref, out2_ref):
     c = out1_ref.shape[-1]
-    odd = lax.axis_index("lon") % 2 == 1
+    odd = parity() == 1
     mine, theirs = mine_ref[...], theirs_ref[...]
     for out, packed in (
         (out1_ref, jnp.where(odd, theirs, mine)),
@@ -265,15 +355,16 @@
     return sum(math.prod(s) * jnp.dtype(d).itemsize for s, d in shapes)
 
 
-def call(kernel, outs, scratch, *args):
+def call(kernel, outs, scratch, *args, specs=None):
     mib = 2**20
-    limit = size_of(scratch) + size_of(outs) + size_of([(a.shape, a.dtype) for a in args])
+    buffers = [s for s in scratch if isinstance(s, tuple)]
+    limit = size_of(buffers) + size_of(outs) + size_of([(a.shape, a.dtype) for a in args])
     return pl.pallas_call(
         kernel,
         out_shape=[jax.ShapeDtypeStruct(s, d) for s, d in outs],
-        in_specs=vmem(len(args)),
+        in_specs=specs or vmem(len(args)),
         out_specs=vmem(len(outs)),
-        scratch_shapes=[pltpu.VMEM(s, d) for s, d in scratch],
+        scratch_shapes=[pltpu.VMEM(*s) if isinstance(s, tuple) else s for s in scratch],
         compiler_params=pltpu.CompilerParams(vmem_limit_bytes=(limit // mib + 6) * mib),
     )(*args)
 
@@ -285,31 +376,43 @@
 def one_sample(x, e, kernel_first, kernel_second, metric):
     c, n, lat = x.shape
     wide = 3 * c
-    size = lax.axis_size("lon")
-    up = [(i, (i + 1) % size) for i in range(size)]
-    down = [(j, i) for i, j in up]
-    first = jnp.swapaxes(jnp.stack((x[:, 0:2], e[:, 0:2])), 1, 2)
-    last = jnp.swapaxes(jnp.stack((x[:, n - 2 :], e[:, n - 2 :])), 1, 2)
-    before = lax.ppermute(last, "lon", up)
-    after = lax.ppermute(first, "lon", down)
-    three = (wide, lat)
-    g1, g2, d, s, w1, w1a, w2a = call(
+    chunks = 4
+    count = lax.axis_size("dp") * lax.axis_size("lon")
+    lon = lax.axis_size("lon")
+    mates = [(i, i ^ 1) for i in range(count)]
+    outers = [
+        (i, i // lon * lon + (i % lon + (1 if i % lon % 2 else -1)) % lon) for i in range(count)
+    ]
+    strided_form = ((c * n * lat // 128, 128), F32)
+    column = (wide, lat)
+    halo = ((2, 2, c, lat), BF16)
+    copied = [pl.BlockSpec(memory_space=pltpu.HBM)] * 3
+    xf, ef, to_mate, to_outer, row = call(
+        pack_kernel,
+        [strided_form] * 2 + [halo] * 2 + [((1, lat), F32)],
+        [((c, n, lat), BF16)] * 2
+        + [((lat,), F32), pltpu.SemaphoreType.DMA((2, chunks)), pltpu.SemaphoreType.DMA],
+        *(pltpu.with_memory_space_constraint(a, pltpu.HBM) for a in (x, e, metric)),
+        specs=copied,
+    )
+    from_mate = exchange(to_mate, mates)
+    from_outer = exchange(to_outer, outers)
+    four = [((4,) + column, BF16)] * 3 + [((4,) + column, F32)] * 2
+    square = (wide, wide)
+    g1, g2, d, s, w1, w1a, w2a, *own = call(
         interior_kernel,
-        [((wide, wide), F32)] * 2 + [((n, c, lat), BF16)] * 2 + [((wide, wide), BF16)] * 3,
-        [((c * n * lat // 128, 128), F32)] * 2
-        + [((n,) + three, BF16)] * 3
-        + [((n,) + three, F32)] * 2
-        + [((n,) + three, BF16)],
-        x, e, kernel_first, kernel_second, metric,
+        [(square, F32)] * 2 + [((n, c, lat), BF16)] * 2 + [(square, BF16)] * 3 + four,
+        [((n,) + column, BF16)] * 3 + [((n,) + column, F32)] * 2 + [((n,) + column, BF16)],
+        xf, ef, kernel_first, kernel_second, row,
     )
     packed = (3 * wide // 2, 2 * c)
     kept, sent, de, se = call(
         edge_kernel,
         [(packed, F32), (packed, BF16)] + [((4, c, lat), BF16)] * 2,
-        [((8,) + three, BF16)] * 3 + [((8,) + three, F32)] * 2 + [((2,) + three, BF16)],
-        before, first, last, after, metric, w1, w2a, g1, g2,
-    )
-    return kept, sent, (d, s, de, se, w1a)
+        four + [((2,) + column, BF16)],
+        to_mate, to_outer, from_mate, from_outer, row, w1, w2a, g1, g2, *own,
+    )
+    return kept, sent, (d, s, de, se, w1a), ef
 
 
 def field_parts(parts, pieces):
@@ -334,7 +437,8 @@
 
 
 def assemble(e, grads):
-    c, n, lat = e.shape
+    n = sum(g.shape[0] for g in grads)
+    _, c, lat = grads[0].shape
     return call(
         assemble_kernel, [((c, n, lat), BF16)], [((c * n * lat // 128, 128), F32)], e, *grads
     )[0]
@@ -359,7 +463,9 @@
     results = []
     for even_bit, odd_bit in zip(bits, other):
         sent = total.astype(BF16)
-        got = exchange(sent, [(i, i ^ (odd_bit if i & 1 else even_bit)) for i in range(count)])
+        got = exchange(
+            sent, [(i, i ^ 1 ^ (odd_bit if i.bit_count() & 1 else even_bit)) for i in range(count)]
+        )
         if jobs:
             sent, job_args = lax.optimization_barrier((sent, jobs[0][1](results)))
             results.append(jobs.pop(0)[0](*job_args))
@@ -377,19 +483,18 @@
         float(samples * lax.axis_size("dp")) * float(n * lax.axis_size("lon")) * float(lat)
     )
     factor = jnp.float32(1.0 / counted**0.5)
-    row = metric.reshape(1, lat)
     kept = sent = None
     jobs = []
     pieces = 2
     for b in range(samples):
-        k, t, parts = one_sample(fields[b], cotangent[b], kernel_first, kernel_second, row)
+        k, t, parts, ef = one_sample(fields[b], cotangent[b], kernel_first, kernel_second, metric)
         kept = k if kept is None else kept + k
         sent = t if sent is None else (sent.astype(F32) + t.astype(F32)).astype(BF16)
         for job in field_parts(parts, pieces):
             jobs.append((lambda *args, job=job: job.func(*job.args[:3], *args)[0], lambda done, job=job: job.args[3:]))
         jobs.append((
             lambda *args: assemble(args[0], args[1:]),
-            lambda done, b=b: (cotangent[b],) + tuple(done[-pieces:]),
+            lambda done, ef=ef: (ef,) + tuple(done[-pieces:]),
         ))
     mine, theirs, results = sum_everywhere(kept, sent, factor, jobs)
     field_grad = jnp.stack(results[pieces :: pieces + 1])

time: 39.6 us -> 35.3 us (0.89)
  waiting for transfers between devices: 15.7 us -> 12.8 us
  local copies, waits for them, and re-layouts: 2.47 us -> 0.01 us
  Pallas kernels: 11.7 us -> 13.1 us
  other arithmetic: 0.67 us -> 0.12 us
    ppermute x6 -> x8, starting transfers between devices: 3.43 us -> 8.37 us  [exchange(): return lax.ppermute(value, ('dp', 'lon'), pairs)]
    ppermute x2 -> x0, starting transfers between devices: 4.6 us -> none  [the longest x1 4.54 us: one_sample(): after = lax.ppermute(first, 'lon', down)]
    ppermute x6 -> x8, waiting for transfers between devices: 14.7 us -> 12.8 us  [exchange(): return lax.ppermute(value, ('dp', 'lon'), pairs)]
    another operation x1 -> x0, local copies, waits for them, and re-layouts: 1.71 us -> none  [one_sample(): first = jnp.swapaxes(jnp.stack((x[:, 0:2], e[:, 0:2])), 1, 2)]
    pallas_call x6 -> x7, Pallas kernels: 11.7 us -> 13.1 us  [call(): pl.pallas_call(kernel, out_shape=[jax.ShapeDtypeStruct(s, d) for s, d in...]
    ppermute x2 -> x0, waiting for transfers between devices: 0.99 us -> none  [the longest x1 0.99 us: one_sample(): before = lax.ppermute(last, 'lon', up)]
    unnamed x10 -> x4, local copies, waits for them, and re-layouts: 0.66 us -> 0.01 us
    transpose x2 -> x0, other arithmetic: 0.55 us -> none  [the longest x1 0.28 us: one_sample(): first = jnp.swapaxes(jnp.stack((x[:, 0:2], e[:, 0:2])), 1, 2)]
  transfers between devices with their start and end apart: 8 -> 8, of which waited for: 7 -> 6; matrix products, arithmetic and copies ran while one was open for 1% -> 0% of each run, Pallas kernels for 23% -> 25%
where the time goes in v3:
time: 35.3 us; the launch traced here: 35.2 us
  Pallas kernels  13.1 us (37%)
  waiting for transfers between devices  12.8 us (36%)
  starting transfers between devices  8.37 us (24%)
  between operations  0.74 us (2%)
    pallas_call x7, Pallas kernels, call(): pl.pallas_call(kernel, out_shape=[jax.ShapeDtypeStruct(s, d) for s, d in...  13.1 us
    ppermute x8, waiting for transfers between devices, exchange(): return lax.ppermute(value, ('dp', 'lon'), pairs)  12.8 us
    ppermute x8, starting transfers between devices, exchange(): return lax.ppermute(value, ('dp', 'lon'), pairs)  8.37 us
  transfers between devices with their start and end apart: 8, of which 6 were waited for; matrix products, arithmetic and copies ran while one was open for 0% of the time, Pallas kernels for 25%

profile of v3, /device:TPU:0, one launch (start us, length us, event | category | flops | bytes accessed | tf_op | source)
XLA Modules:
  0.0 35.2 jit_solution(8954348341411075431)
XLA Ops:
  0.6 0.0 copy-start
  0.6 0.0 copy-start.1
  0.7 1.9 %shard_map.76 = (f32[3072,128]{1,0:T(8,128)S(1)}, f32[3072,128]{1,0:T(8,128)S(1)}, bf16[2,2,64,384]{3,2,1,0:T(8,128)(2,1)S(1)}, bf16[2,2,64,384]{3,2,1,0:T(8,128)(2,1)S(1)}, f32[1,384]{1,0:T(1,128)S(1)}) custom-call(bf16[64,16,384]{2,1,0:T(8,128)(2,1)} %bitcast.3, bf16[64,16,384]{2,1,0:T(8,128)(2,1)} %bitcast.4, f32[384]{0:T(512)} %m_hbm.1), custom_call_target="tpu_custom_call" | custom-call | tf_op jit(solution)/shard_map/pallas_call | solution.py:362
  2.5 0.5 %collective-permute-start = (bf16[2,2,64,384]{3,2,1,0:T(8,128)(2,1)S(1)}, bf16[2,2,64,384]{3,2,1,0:T(8,128)(2,1)S(1)}, u32[]{:S(2)}, u32[]{:S(2)}) collective-permute-start(bf16[2,2,64,384]{3,2,1,0:T(8,128)(2,1)S(1)} %get-tuple-element.48.to_mate), channel_id=1, source_target_pairs={{0,1},{1,0},{2,3},{3,2},{4,5},{5,4},{6,7},{7,6},{8,9},{9,8},{10,11... | collective-permute-start | bytes 589832 | tf_op jit(solution)/shard_map/ppermute | solution.py:373
  3.1 4.7 %collective-permute-start.1 = (bf16[2,2,64,384]{3,2,1,0:T(8,128)(2,1)S(1)}, bf16[2,2,64,384]{3,2,1,0:T(8,128)(2,1)S(1)}, u32[]{:S(2)}, u32[]{:S(2)}) collective-permute-start(bf16[2,2,64,384]{3,2,1,0:T(8,128)(2,1)S(1)} %get-tuple-element.49.to_outer), channel_id=1, source_target_pairs={{0,7},{1,2},{2,1},{3,4},{4,3},{5,6},{6,5},{7,0},{8,15},{9,10},{10,... | collective-permute-start | bytes 589832 | tf_op jit(solution)/shard_map/ppermute | solution.py:373
  7.8 0.0 copy-done
  7.8 0.0 copy-done.1
  7.8 5.1 %shard_map.77 = (f32[192,192]{1,0:T(8,128)S(1)}, f32[192,192]{1,0:T(8,128)S(1)}, bf16[16,64,384]{2,1,0:T(8,128)(2,1)S(1)}, bf16[16,64,384]{2,1,0:T(8,128)(2,1)S(...) custom-call(f32[3072,128]{1,0:T(8,128)S(1)} %get-tuple-element.51.xf, ...), custom_call_target="tpu_custom_call" | custom-call | tf_op jit(solution)/shard_map/pallas_call | solution.py:362
  12.9 0.0 collective-permute-done.from_mate
  12.9 0.0 collective-permute-done.1.from_outer
  12.9 1.5 %shard_map.78 = (f32[288,128]{1,0:T(8,128)S(1)}, bf16[288,128]{1,0:T(8,128)(2,1)S(1)}, bf16[4,64,384]{2,1,0:T(8,128)(2,1)S(1)}, bf16[4,64,384]{2,1,0:T(8,128)(2,1)S(1)}) custom-call(bf16[2,2,64,384]{3,2,1,0:T(8,128)(2,1)S(1)} %get-tuple-element.48.to_mate, bf16[2,2,64,384]{3,2,1,0:T(8,128)(2,1)S(1)} %get-tuple-element.49.to_outer, ...), custom_call_target="tpu_custom_call" | custom-call | tf_op jit(solution)/shard_map/pallas_call | solution.py:362
  14.4 0.1 collective-permute-start.2
  14.5 1.3 %collective-permute-done.2 = bf16[288,128]{1,0:T(8,128)(2,1)S(1)} collective-permute-done((bf16[288,128]{1,0:T(8,128)(2,1)S(1)}, bf16[288,128]{1,0:T(8,128)(2,1)S(1)}, u32[]{:S(2)}, u32[]{:S(2)}) %collective-permute-start.2) | collective-permute-done | bytes 73760 | tf_op jit(solution)/shard_map/ppermute | solution.py:373
  15.8 1.3 %collective-permute-start.3 = (bf16[288,128]{1,0:T(8,128)(2,1)S(1)}, bf16[288,128]{1,0:T(8,128)(2,1)S(1)}, u32[]{:S(2)}, u32[]{:S(2)}) collective-permute-start(bf16[288,128]{1,0:T(8,128)(2,1)S(1)} %add_convert_fusion.3), channel_id=1, source_target_pairs={{0,9},{1,4},{2,7},{3,10},{4,1},{5,12},{6,15},{7,2},{8,13},{9,0},{1... | collective-permute-start | bytes 221192 | tf_op jit(solution)/shard_map/ppermute | solution.py:373
  17.1 0.9 %shard_map.79.refs_1_ = f32[8,64,384]{2,1,0:T(8,128)S(1)} custom-call(bf16[16,64,384]{2,1,0:T(8,128)(2,1)S(1)} %get-tuple-element.77.d_in, bf16[16,64,384]{2,1,0:T(8,128)(2,1)S(1)} %get-tuple-element.78.s_in, bf16[4,64,384]{2,1,0:T(8,128)(2,1)S(1)} %get-tuple-element.79.de_ref, bf16[4,64,384]{2,1,0:T(8,128)(2,1)S(1)} %get-tuple-element.80.se_ref, ...), custom_call_target="tpu_custom_call" | custom-call | tf_op jit(solution)/shard_map/pallas_call | solution.py:362
  18.0 1.6 %collective-permute-done.3 = bf16[288,128]{1,0:T(8,128)(2,1)S(1)} collective-permute-done((bf16[288,128]{1,0:T(8,128)(2,1)S(1)}, bf16[288,128]{1,0:T(8,128)(2,1)S(1)}, u32[]{:S(2)}, u32[]{:S(2)}) %collective-permute-start.3) | collective-permute-done | bytes 73760 | tf_op jit(solution)/shard_map/ppermute | solution.py:373
  19.6 0.7 %collective-permute-start.4 = (bf16[288,128]{1,0:T(8,128)(2,1)S(1)}, bf16[288,128]{1,0:T(8,128)(2,1)S(1)}, u32[]{:S(2)}, u32[]{:S(2)}) collective-permute-start(bf16[288,128]{1,0:T(8,128)(2,1)S(1)} %add_convert_fusion.2), channel_id=1, source_target_pairs={{0,5},{1,8},{2,11},{3,6},{4,13},{5,0},{6,3},{7,14},{8,1},{9,12},{1... | collective-permute-start | bytes 221192 | tf_op jit(solution)/shard_map/ppermute | solution.py:373
  20.3 0.9 %shard_map.80.refs_2_ = f32[8,64,384]{2,1,0:T(8,128)S(1)} custom-call(bf16[16,64,384]{2,1,0:T(8,128)(2,1)S(1)} %get-tuple-element.77.d_in, bf16[16,64,384]{2,1,0:T(8,128)(2,1)S(1)} %get-tuple-element.78.s_in, bf16[4,64,384]{2,1,0:T(8,128)(2,1)S(1)} %get-tuple-element.79.de_ref, bf16[4,64,384]{2,1,0:T(8,128)(2,1)S(1)} %get-tuple-element.80.se_ref, ...), custom_call_target="tpu_custom_call" | custom-call | tf_op jit(solution)/shard_map/pallas_call | solution.py:362
  21.2 3.9 %collective-permute-done.4 = bf16[288,128]{1,0:T(8,128)(2,1)S(1)} collective-permute-done((bf16[288,128]{1,0:T(8,128)(2,1)S(1)}, bf16[288,128]{1,0:T(8,128)(2,1)S(1)}, u32[]{:S(2)}, u32[]{:S(2)}) %collective-permute-start.4) | collective-permute-done | bytes 73760 | tf_op jit(solution)/shard_map/ppermute | solution.py:373
  25.2 0.8 %collective-permute-start.5 = (bf16[288,128]{1,0:T(8,128)(2,1)S(1)}, bf16[288,128]{1,0:T(8,128)(2,1)S(1)}, u32[]{:S(2)}, u32[]{:S(2)}) collective-permute-start(bf16[288,128]{1,0:T(8,128)(2,1)S(1)} %add_convert_fusion.1), channel_id=1, source_target_pairs={{0,17},{1,2},{2,1},{3,18},{4,7},{5,20},{6,23},{7,4},{8,11},{9,24},... | collective-permute-start | bytes 221192 | tf_op jit(solution)/shard_map/ppermute | solution.py:373
  26.1 1.9 %shard_map.81 = bf16[64,16,384]{2,1,0:T(8,128)(2,1)} custom-call(f32[3072,128]{1,0:T(8,128)S(1)} %get-tuple-element.85.ef.refs_0_, f32[8,64,384]{2,1,0:T(8,128)S(1)} %shard_map.79.refs_1_, f32[8,64,384]{2,1,0:T(8,128)S(1)} %shard_map.80.refs_2_), custom_call_target="tpu_custom_call" | custom-call | tf_op jit(solution)/shard_map/pallas_call | solution.py:362
  28.0 1.1 %collective-permute-done.5 = bf16[288,128]{1,0:T(8,128)(2,1)S(1)} collective-permute-done((bf16[288,128]{1,0:T(8,128)(2,1)S(1)}, bf16[288,128]{1,0:T(8,128)(2,1)S(1)}, u32[]{:S(2)}, u32[]{:S(2)}) %collective-permute-start.5) | collective-permute-done | bytes 73760 | tf_op jit(solution)/shard_map/ppermute | solution.py:373
  29.1 0.1 collective-permute-start.6
  29.2 3.8 %collective-permute-done.6 = bf16[288,128]{1,0:T(8,128)(2,1)S(1)} collective-permute-done((bf16[288,128]{1,0:T(8,128)(2,1)S(1)}, bf16[288,128]{1,0:T(8,128)(2,1)S(1)}, u32[]{:S(2)}, u32[]{:S(2)}) %collective-permute-start.6) | collective-permute-done | bytes 73760 | tf_op jit(solution)/shard_map/ppermute | solution.py:373
  33.0 0.2 collective-permute-start.7
  33.1 1.2 %collective-permute-done.7.theirs_ref = bf16[288,128]{1,0:T(8,128)(2,1)S(1)} collective-permute-done((bf16[288,128]{1,0:T(8,128)(2,1)S(1)}, bf16[288,128]{1,0:T(8,128)(2,1)S(1)}, u32[]{:S(2)}, u32[]{:S(2)}) %collective-permute-start.7) | collective-permute-done | bytes 73760 | tf_op jit(solution)/shard_map/ppermute | solution.py:373
  34.3 0.9 %shard_map.82 = (bf16[3,3,64,64]{3,2,1,0:T(8,128)(2,1)}, bf16[3,3,64,64]{3,2,1,0:T(8,128)(2,1)}) custom-call(bf16[288,128]{1,0:T(8,128)(2,1)S(1)} %multiply_convert_fusion.mine_ref, bf16[288,128]{1,0:T(8,128)(2,1)S(1)} %collective-permute-done.7.theirs_ref), custom_call_target="tpu_custom_call" | custom-call | tf_op jit(solution)/shard_map/pallas_call | solution.py:362
  (5 shorter events, 0.1 us)
Async XLA Ops:
  0.6 7.1 %copy-start = (bf16[3,3,64,64]{3,2,1,0:T(8,128)(2,1)S(1)}, bf16[3,3,64,64]{3,2,1,0:T(8,128)(2,1)}, u32[]{:S(2)}) copy-start(bf16[3,3,64,64]{3,2,1,0:T(8,128)(2,1)} %k1_ref.1) | copy-start | bytes 221188
  0.6 7.1 %copy-start.1 = (bf16[3,3,64,64]{3,2,1,0:T(8,128)(2,1)S(1)}, bf16[3,3,64,64]{3,2,1,0:T(8,128)(2,1)}, u32[]{:S(2)}) copy-start(bf16[3,3,64,64]{3,2,1,0:T(8,128)(2,1)} %k2_ref.1) | copy-start | bytes 221188
  2.5 10.4 %collective-permute-start = (bf16[2,2,64,384]{3,2,1,0:T(8,128)(2,1)S(1)}, bf16[2,2,64,384]{3,2,1,0:T(8,128)(2,1)S(1)}, u32[]{:S(2)}, u32[]{:S(2)}) collective-permute-start(bf16[2,2,64,384]{3,2,1,0:T(8,128)(2,1)S(1)} %get-tuple-element.48.to_mate), channel_id=1, source_target_pairs={{0,1},{1,0},{2,3},{3,2},{4,5},{5,4},{6,7},{7,6},{8,9},{9,8},{10,11... | collective-permute-start | bytes 589832 | tf_op jit(solution)/shard_map/ppermute | solution.py:373
  3.1 9.8 %collective-permute-start.1 = (bf16[2,2,64,384]{3,2,1,0:T(8,128)(2,1)S(1)}, bf16[2,2,64,384]{3,2,1,0:T(8,128)(2,1)S(1)}, u32[]{:S(2)}, u32[]{:S(2)}) collective-permute-start(bf16[2,2,64,384]{3,2,1,0:T(8,128)(2,1)S(1)} %get-tuple-element.49.to_outer), channel_id=1, source_target_pairs={{0,7},{1,2},{2,1},{3,4},{4,3},{5,6},{6,5},{7,0},{8,15},{9,10},{10,... | collective-permute-start | bytes 589832 | tf_op jit(solution)/shard_map/ppermute | solution.py:373
  14.4 1.3 %collective-permute-start.2 = (bf16[288,128]{1,0:T(8,128)(2,1)S(1)}, bf16[288,128]{1,0:T(8,128)(2,1)S(1)}, u32[]{:S(2)}, u32[]{:S(2)}) collective-permute-start(bf16[288,128]{1,0:T(8,128)(2,1)S(1)} %get-tuple-element.63), channel_id=1, source_target_pairs={{0,1},{1,0},{2,3},{3,2},{4,5},{5,4},{6,7},{7,6},{8,9},{9,8},{10,11... | collective-permute-start | bytes 221192 | tf_op jit(solution)/shard_map/ppermute | solution.py:373
  15.8 3.8 %collective-permute-start.3 = (bf16[288,128]{1,0:T(8,128)(2,1)S(1)}, bf16[288,128]{1,0:T(8,128)(2,1)S(1)}, u32[]{:S(2)}, u32[]{:S(2)}) collective-permute-start(bf16[288,128]{1,0:T(8,128)(2,1)S(1)} %add_convert_fusion.3), channel_id=1, source_target_pairs={{0,9},{1,4},{2,7},{3,10},{4,1},{5,12},{6,15},{7,2},{8,13},{9,0},{1... | collective-permute-start | bytes 221192 | tf_op jit(solution)/shard_map/ppermute | solution.py:373
  19.6 5.5 %collective-permute-start.4 = (bf16[288,128]{1,0:T(8,128)(2,1)S(1)}, bf16[288,128]{1,0:T(8,128)(2,1)S(1)}, u32[]{:S(2)}, u32[]{:S(2)}) collective-permute-start(bf16[288,128]{1,0:T(8,128)(2,1)S(1)} %add_convert_fusion.2), channel_id=1, source_target_pairs={{0,5},{1,8},{2,11},{3,6},{4,13},{5,0},{6,3},{7,14},{8,1},{9,12},{1... | collective-permute-start | bytes 221192 | tf_op jit(solution)/shard_map/ppermute | solution.py:373
  25.2 3.8 %collective-permute-start.5 = (bf16[288,128]{1,0:T(8,128)(2,1)S(1)}, bf16[288,128]{1,0:T(8,128)(2,1)S(1)}, u32[]{:S(2)}, u32[]{:S(2)}) collective-permute-start(bf16[288,128]{1,0:T(8,128)(2,1)S(1)} %add_convert_fusion.1), channel_id=1, source_target_pairs={{0,17},{1,2},{2,1},{3,18},{4,7},{5,20},{6,23},{7,4},{8,11},{9,24},... | collective-permute-start | bytes 221192 | tf_op jit(solution)/shard_map/ppermute | solution.py:373
  29.1 3.8 %collective-permute-start.6 = (bf16[288,128]{1,0:T(8,128)(2,1)S(1)}, bf16[288,128]{1,0:T(8,128)(2,1)S(1)}, u32[]{:S(2)}, u32[]{:S(2)}) collective-permute-start(bf16[288,128]{1,0:T(8,128)(2,1)S(1)} %add_convert_fusion), channel_id=1, source_target_pairs={{0,3},{1,16},{2,19},{3,0},{4,21},{5,6},{6,5},{7,22},{8,25},{9,10},... | collective-permute-start | bytes 221192 | tf_op jit(solution)/shard_map/ppermute | solution.py:373
  33.0 1.3 %collective-permute-start.7 = (bf16[288,128]{1,0:T(8,128)(2,1)S(1)}, bf16[288,128]{1,0:T(8,128)(2,1)S(1)}, u32[]{:S(2)}, u32[]{:S(2)}) collective-permute-start(bf16[288,128]{1,0:T(8,128)(2,1)S(1)} %multiply_convert_fusion.mine_ref), channel_id=1, source_target_pairs={{0,1},{1,0},{2,3},{3,2},{4,5},{5,4},{6,7},{7,6},{8,9},{9,8},{10,11... | collective-permute-start | bytes 221192 | tf_op jit(solution)/shard_map/ppermute | solution.py:373

commit v4 on v3

--- a/solution.py
+++ b/solution.py
@@ -15,21 +15,24 @@
 
 
 def gelu_pair(u):
-    inner = jnp.tanh(gelu_coef * (u + 0.044715 * u * u * u))
-    value = 0.5 * u * (1.0 + inner)
-    slope = 0.5 * (1.0 + inner) + 0.5 * u * (1.0 - inner * inner) * gelu_coef * (
-        1.0 + 3.0 * 0.044715 * u * u
-    )
-    return value, slope
+    square = u * u
+    inner = jnp.tanh(u * (gelu_coef + (gelu_coef * 0.044715) * square))
+    a = 0.5 + 0.5 * inner
+    value = u * a
+    twice = 2.0 * gelu_coef + (6.0 * gelu_coef * 0.044715) * square
+    return value, a + (value - value * a) * twice
 
 
 def neighbours(v):
-    lat = v.shape[-1]
-    row = lax.broadcasted_iota(jnp.int32, v.shape, 1)
-    zero = jnp.zeros_like(v)
-    below = jnp.where(row == 0, zero, pltpu.roll(v, 1, 1))
-    above = jnp.where(row == lat - 1, zero, pltpu.roll(v, lat - 1, 1))
-    return below, above
+    lanes = 128
+    tiles = [v[:, k : k + lanes] for k in range(0, v.shape[-1], lanes)]
+    lane = lax.broadcasted_iota(jnp.int32, tiles[0].shape, 1)
+    zero = jnp.zeros_like(tiles[0])
+    up = [zero] + [pltpu.roll(t, 1, 1) for t in tiles]
+    down = [pltpu.roll(t, lanes - 1, 1) for t in tiles] + [zero]
+    below = [jnp.where(lane == 0, up[k], up[k + 1]) for k in range(len(tiles))]
+    above = [jnp.where(lane == lanes - 1, down[k + 1], down[k]) for k in range(len(tiles))]
+    return jnp.concatenate(below, axis=1), jnp.concatenate(above, axis=1)
 
 
 def dot(a, b):
@@ -136,19 +139,30 @@
 
 
 def pack_kernel(
-    x_hbm, e_hbm, m_hbm, xf, ef, mate_ref, outer_ref, row_ref, xs, es, ms, sems, row_sem
+    x_hbm, e_hbm, m_hbm, k1_hbm, k2_hbm,
+    xf, ef, mate_ref, outer_ref, row_ref, w1_ref, w1a_ref, w2a_ref,
+    xs, es, ms, k1s, k2s, sems, small_sems,
 ):
     c, n, lat = x_hbm.shape
     chunks = sems.shape[1]
     w = c // chunks
+    small = [
+        pltpu.make_async_copy(src, dst, small_sems.at[k])
+        for k, (src, dst) in enumerate(((k1_hbm, k1s), (k2_hbm, k2s), (m_hbm, ms)))
+    ]
+    for copy in small:
+        copy.start()
     copies = []
     for k in range(chunks):
         for a, (src, dst) in enumerate(((x_hbm, xs), (e_hbm, es))):
             rows = pl.ds(k * w, w)
             copies.append(pltpu.make_async_copy(src.at[rows], dst.at[rows], sems.at[a, k]))
             copies[-1].start()
-    row_copy = pltpu.make_async_copy(m_hbm, ms, row_sem)
-    row_copy.start()
+    for copy in small:
+        copy.wait()
+    row_ref[...] = ms[...].reshape(1, lat)
+    prepare(k1s, w1_ref, w1a_ref)
+    prepare(k2s, None, w2a_ref)
     for k in range(chunks):
         for a, (src, dst) in enumerate(((xs, xf), (es, ef))):
             copies[2 * k + a].wait()
@@ -160,19 +174,15 @@
             high = column(source, n - 2 + k, c, n).astype(BF16)
             mate_ref[a, k] = jnp.where(odd, low, high)
             outer_ref[a, k] = jnp.where(odd, high, low)
-    row_copy.wait()
-    row_ref[...] = ms[...].reshape(1, lat)
 
 
 def interior_kernel(
-    xf, ef, k1_ref, k2_ref, m_ref,
-    g1_ref, g2_ref, d_ref, s_ref, w1_ref, w1a_ref, w2a_ref, x3_out, e3_out, s3_out, y_out, z_out,
+    xf, ef, w1_ref, w2a_ref, m_ref,
+    g1_ref, g2_ref, d_ref, s_ref, x3_out, e3_out, s3_out, y_out, z_out,
     x3_in, e3_in, s3_in, y_in, z_in, h3,
 ):
     n, c, lat = d_ref.shape
     metric = m_ref[...]
-    prepare(k1_ref, w1_ref, w1a_ref)
-    prepare(k2_ref, None, w2a_ref)
     edges = (0, 1, n - 2, n - 1)
     x3, e3, s3, y, z = (
         split(outside, edges, inside)
@@ -233,7 +243,7 @@
 
 
 def edge_kernel(
-    to_mate, to_outer, from_mate, from_outer, m_ref, w1, w2a, g1_in, g2_in, x3_own, e3_own, s3_own, y_own, z_own,
+    from_outer, from_mate, to_mate, to_outer, m_ref, w1, w2a, g1_in, g2_in, x3_own, e3_own, s3_own, y_own, z_own,
     kept_ref, sent_ref, d_ref, s_ref,
     x3_far, e3_far, s3_far, y_far, z_far, h3,
 ):
@@ -376,7 +386,7 @@
 def one_sample(x, e, kernel_first, kernel_second, metric):
     c, n, lat = x.shape
     wide = 3 * c
-    chunks = 4
+    chunks = 1
     count = lax.axis_size("dp") * lax.axis_size("lon")
     lon = lax.axis_size("lon")
     mates = [(i, i ^ 1) for i in range(count)]
@@ -386,31 +396,33 @@
     strided_form = ((c * n * lat // 128, 128), F32)
     column = (wide, lat)
     halo = ((2, 2, c, lat), BF16)
-    copied = [pl.BlockSpec(memory_space=pltpu.HBM)] * 3
-    xf, ef, to_mate, to_outer, row = call(
+    square = (wide, wide)
+    inputs = (x, e, metric, kernel_first, kernel_second)
+    xf, ef, to_mate, to_outer, row, w1, w1a, w2a = call(
         pack_kernel,
-        [strided_form] * 2 + [halo] * 2 + [((1, lat), F32)],
+        [strided_form] * 2 + [halo] * 2 + [((1, lat), F32)] + [(square, BF16)] * 3,
         [((c, n, lat), BF16)] * 2
-        + [((lat,), F32), pltpu.SemaphoreType.DMA((2, chunks)), pltpu.SemaphoreType.DMA],
-        *(pltpu.with_memory_space_constraint(a, pltpu.HBM) for a in (x, e, metric)),
-        specs=copied,
-    )
+        + [((lat,), F32)]
+        + [((3, 3, c, c), BF16)] * 2
+        + [pltpu.SemaphoreType.DMA((2, chunks)), pltpu.SemaphoreType.DMA((3,))],
+        *(pltpu.with_memory_space_constraint(a, pltpu.HBM) for a in inputs),
+        specs=[pl.BlockSpec(memory_space=pltpu.HBM)] * len(inputs),
+    )
+    from_outer = exchange(to_outer, outers)
     from_mate = exchange(to_mate, mates)
-    from_outer = exchange(to_outer, outers)
     four = [((4,) + column, BF16)] * 3 + [((4,) + column, F32)] * 2
-    square = (wide, wide)
-    g1, g2, d, s, w1, w1a, w2a, *own = call(
+    g1, g2, d, s, *own = call(
         interior_kernel,
-        [(square, F32)] * 2 + [((n, c, lat), BF16)] * 2 + [(square, BF16)] * 3 + four,
+        [(square, F32)] * 2 + [((n, c, lat), BF16)] * 2 + four,
         [((n,) + column, BF16)] * 3 + [((n,) + column, F32)] * 2 + [((n,) + column, BF16)],
-        xf, ef, kernel_first, kernel_second, row,
+        xf, ef, w1, w2a, row,
     )
     packed = (3 * wide // 2, 2 * c)
     kept, sent, de, se = call(
         edge_kernel,
         [(packed, F32), (packed, BF16)] + [((4, c, lat), BF16)] * 2,
         four + [((2,) + column, BF16)],
-        to_mate, to_outer, from_mate, from_outer, row, w1, w2a, g1, g2, *own,
+        from_outer, from_mate, to_mate, to_outer, row, w1, w2a, g1, g2, *own,
     )
     return kept, sent, (d, s, de, se, w1a), ef
 
@@ -448,28 +460,35 @@
     dp, lon = lax.axis_size("dp"), lax.axis_size("lon")
     count = dp * lon
     swap = [(i, i ^ 1) for i in range(count)]
-    total = kept + exchange(sent, swap).astype(F32)
-    inner = [1 << k for k in range(1, lon.bit_length() - 1)]
-    outer = [lon << k for k in range(dp.bit_length() - 1)]
+    results = []
+
+    def beside(sent, got):
+        if jobs:
+            job, arguments = jobs.pop(0)
+            sent, arguments = lax.optimization_barrier((sent, arguments(results)))
+            results.append(job(*arguments))
+            got, results[-1] = lax.optimization_barrier((got, results[-1]))
+        return sent, got
+
+    _, got = beside(sent, exchange(sent, swap))
+    total = kept + got.astype(F32)
+    along_lon = [1 << k for k in range(1, lon.bit_length() - 1)]
+    along_dp = [lon << k for k in range(dp.bit_length() - 1)]
     bits = []
-    while inner or outer:
-        if outer:
-            bits.append(outer.pop(0))
-        if inner:
-            bits.append(inner.pop())
+    while along_lon or along_dp:
+        if along_dp:
+            bits.append(along_dp.pop(0))
+        if along_lon:
+            bits.append(along_lon.pop())
     other = list(bits)
     for k in range(0, len(bits) - 1, 2):
         other[k], other[k + 1] = bits[k + 1], bits[k]
-    results = []
     for even_bit, odd_bit in zip(bits, other):
         sent = total.astype(BF16)
         got = exchange(
             sent, [(i, i ^ 1 ^ (odd_bit if i.bit_count() & 1 else even_bit)) for i in range(count)]
         )
-        if jobs:
-            sent, job_args = lax.optimization_barrier((sent, jobs[0][1](results)))
-            results.append(jobs.pop(0)[0](*job_args))
-            got, results[-1] = lax.optimization_barrier((got, results[-1]))
+        sent, got = beside(sent, got)
         total = sent.astype(F32) + got.astype(F32)
     for job in jobs:
         results.append(job[0](*job[1](results)))

time: 35.3 us -> 34.7 us (0.983)
  waiting for transfers between devices: 12.8 us -> 10.5 us
  starting transfers between devices: 8.37 us -> 10.4 us
    ppermute x8, waiting for transfers between devices: 12.8 us -> 10.5 us  [exchange(): return lax.ppermute(value, ('dp', 'lon'), pairs)]
    ppermute x8, starting transfers between devices: 8.37 us -> 10.4 us  [exchange(): return lax.ppermute(value, ('dp', 'lon'), pairs)]
  transfers between devices with their start and end apart: 8 -> 8, of which waited for: 6 -> 5; matrix products, arithmetic and copies ran while one was open for 0% -> 0% of each run, Pallas kernels for 25% -> 25%
where the time goes in v4:
time: 34.7 us; the launch traced here: 34.5 us
  Pallas kernels  12.8 us (37%)
  waiting for transfers between devices  10.5 us (30%)
  starting transfers between devices  10.4 us (30%)
  between operations  0.73 us (2%)
    pallas_call x7, Pallas kernels, call(): pl.pallas_call(kernel, out_shape=[jax.ShapeDtypeStruct(s, d) for s, d in...  12.8 us
    ppermute x8, waiting for transfers between devices, exchange(): return lax.ppermute(value, ('dp', 'lon'), pairs)  10.5 us
    ppermute x8, starting transfers between devices, exchange(): return lax.ppermute(value, ('dp', 'lon'), pairs)  10.4 us
  transfers between devices with their start and end apart: 8, of which 5 were waited for; matrix products, arithmetic and copies ran while one was open for 0% of the time, Pallas kernels for 25%

profile of v4, /device:TPU:0, one launch (start us, length us, event | category | flops | bytes accessed | tf_op | source)
XLA Modules:
  0.0 34.5 jit_solution(18422192804753988282)
XLA Ops:
  0.6 2.0 %shard_map.76 = (f32[3072,128]{1,0:T(8,128)S(1)}, f32[3072,128]{1,0:T(8,128)S(1)}, bf16[2,2,64,384]{3,2,1,0:T(8,128)(2,1)S(1)}, bf16[2,2,64,384]{3,2,1,0:T(8,128...) custom-call(bf16[64,16,384]{2,1,0:T(8,128)(2,1)} %bitcast.3, ...), custom_call_target="tpu_custom_call" | custom-call | tf_op jit(solution)/shard_map/pallas_call | solution.py:372
  2.6 4.6 %collective-permute-start = (bf16[2,2,64,384]{3,2,1,0:T(8,128)(2,1)S(1)}, bf16[2,2,64,384]{3,2,1,0:T(8,128)(2,1)S(1)}, u32[]{:S(2)}, u32[]{:S(2)}) collective-permute-start(bf16[2,2,64,384]{3,2,1,0:T(8,128)(2,1)S(1)} %get-tuple-element.47.to_outer), channel_id=1, source_target_pairs={{0,7},{1,2},{2,1},{3,4},{4,3},{5,6},{6,5},{7,0},{8,15},{9,10},{10,... | collective-permute-start | bytes 589832 | tf_op jit(solution)/shard_map/ppermute | solution.py:383
  7.2 0.0 collective-permute-start.1
  7.2 4.8 %shard_map.77 = (f32[192,192]{1,0:T(8,128)S(1)}, f32[192,192]{1,0:T(8,128)S(1)}, bf16[16,64,384]{2,1,0:T(8,128)(2,1)S(1)}, bf16[16,64,384]{2,1,0:T(8,128)(2,1)S(...) custom-call(f32[3072,128]{1,0:T(8,128)S(1)} %get-tuple-element.52.xf, ...), custom_call_target="tpu_custom_call" | custom-call | tf_op jit(solution)/shard_map/pallas_call | solution.py:372
  12.0 0.0 collective-permute-done.from_outer
  12.0 0.0 collective-permute-done.1.from_mate
  12.0 1.4 %shard_map.78 = (f32[288,128]{1,0:T(8,128)S(1)}, bf16[288,128]{1,0:T(8,128)(2,1)S(1)}, bf16[4,64,384]{2,1,0:T(8,128)(2,1)S(1)}, bf16[4,64,384]{2,1,0:T(8,128)(2,1)S(1)}) custom-call(bf16[2,2,64,384]{3,2,1,0:T(8,128)(2,1)S(1)} %collective-permute-done.from_outer, bf16[2,2,64,384]{3,2,1,0:T(8,128)(2,1)S(1)} %collective-permute-done.1.from_mate, ...), custom_call_target="tpu_custom_call" | custom-call | tf_op jit(solution)/shard_map/pallas_call | solution.py:372
  13.4 0.6 %collective-permute-start.2 = (bf16[288,128]{1,0:T(8,128)(2,1)S(1)}, bf16[288,128]{1,0:T(8,128)(2,1)S(1)}, u32[]{:S(2)}, u32[]{:S(2)}) collective-permute-start(bf16[288,128]{1,0:T(8,128)(2,1)S(1)} %get-tuple-element.62), channel_id=1, source_target_pairs={{0,1},{1,0},{2,3},{3,2},{4,5},{5,4},{6,7},{7,6},{8,9},{9,8},{10,11... | collective-permute-start | bytes 221192 | tf_op jit(solution)/shard_map/ppermute | solution.py:383
  14.0 0.9 %shard_map.79.refs_1_ = f32[8,64,384]{2,1,0:T(8,128)S(1)} custom-call(bf16[16,64,384]{2,1,0:T(8,128)(2,1)S(1)} %get-tuple-element.75.d_in, bf16[16,64,384]{2,1,0:T(8,128)(2,1)S(1)} %get-tuple-element.76.s_in, bf16[4,64,384]{2,1,0:T(8,128)(2,1)S(1)} %get-tuple-element.77.de_ref, bf16[4,64,384]{2,1,0:T(8,128)(2,1)S(1)} %get-tuple-element.78.se_ref, ...), custom_call_target="tpu_custom_call" | custom-call | tf_op jit(solution)/shard_map/pallas_call | solution.py:372
  14.9 0.0 collective-permute-done.2
  15.0 2.0 %collective-permute-start.3 = (bf16[288,128]{1,0:T(8,128)(2,1)S(1)}, bf16[288,128]{1,0:T(8,128)(2,1)S(1)}, u32[]{:S(2)}, u32[]{:S(2)}) collective-permute-start(bf16[288,128]{1,0:T(8,128)(2,1)S(1)} %add_convert_fusion.3), channel_id=1, source_target_pairs={{0,9},{1,4},{2,7},{3,10},{4,1},{5,12},{6,15},{7,2},{8,13},{9,0},{1... | collective-permute-start | bytes 221192 | tf_op jit(solution)/shard_map/ppermute | solution.py:383
  17.0 0.9 %shard_map.80.refs_2_ = f32[8,64,384]{2,1,0:T(8,128)S(1)} custom-call(bf16[16,64,384]{2,1,0:T(8,128)(2,1)S(1)} %get-tuple-element.75.d_in, bf16[16,64,384]{2,1,0:T(8,128)(2,1)S(1)} %get-tuple-element.76.s_in, bf16[4,64,384]{2,1,0:T(8,128)(2,1)S(1)} %get-tuple-element.77.de_ref, bf16[4,64,384]{2,1,0:T(8,128)(2,1)S(1)} %get-tuple-element.78.se_ref, ...), custom_call_target="tpu_custom_call" | custom-call | tf_op jit(solution)/shard_map/pallas_call | solution.py:372
  17.9 1.1 %collective-permute-done.3 = bf16[288,128]{1,0:T(8,128)(2,1)S(1)} collective-permute-done((bf16[288,128]{1,0:T(8,128)(2,1)S(1)}, bf16[288,128]{1,0:T(8,128)(2,1)S(1)}, u32[]{:S(2)}, u32[]{:S(2)}) %collective-permute-start.3) | collective-permute-done | bytes 73760 | tf_op jit(solution)/shard_map/ppermute | solution.py:383
  19.0 1.7 %collective-permute-start.4 = (bf16[288,128]{1,0:T(8,128)(2,1)S(1)}, bf16[288,128]{1,0:T(8,128)(2,1)S(1)}, u32[]{:S(2)}, u32[]{:S(2)}) collective-permute-start(bf16[288,128]{1,0:T(8,128)(2,1)S(1)} %add_convert_fusion.2), channel_id=1, source_target_pairs={{0,5},{1,8},{2,11},{3,6},{4,13},{5,0},{6,3},{7,14},{8,1},{9,12},{1... | collective-permute-start | bytes 221192 | tf_op jit(solution)/shard_map/ppermute | solution.py:383
  20.7 1.9 %shard_map.81 = bf16[64,16,384]{2,1,0:T(8,128)(2,1)} custom-call(f32[3072,128]{1,0:T(8,128)S(1)} %get-tuple-element.83.ef.refs_0_, f32[8,64,384]{2,1,0:T(8,128)S(1)} %shard_map.79.refs_1_, f32[8,64,384]{2,1,0:T(8,128)S(1)} %shard_map.80.refs_2_), custom_call_target="tpu_custom_call" | custom-call | tf_op jit(solution)/shard_map/pallas_call | solution.py:372
  22.6 2.0 %collective-permute-done.4 = bf16[288,128]{1,0:T(8,128)(2,1)S(1)} collective-permute-done((bf16[288,128]{1,0:T(8,128)(2,1)S(1)}, bf16[288,128]{1,0:T(8,128)(2,1)S(1)}, u32[]{:S(2)}, u32[]{:S(2)}) %collective-permute-start.4) | collective-permute-done | bytes 73760 | tf_op jit(solution)/shard_map/ppermute | solution.py:383
  24.6 1.3 %collective-permute-start.5 = (bf16[288,128]{1,0:T(8,128)(2,1)S(1)}, bf16[288,128]{1,0:T(8,128)(2,1)S(1)}, u32[]{:S(2)}, u32[]{:S(2)}) collective-permute-start(bf16[288,128]{1,0:T(8,128)(2,1)S(1)} %add_convert_fusion.1), channel_id=1, source_target_pairs={{0,17},{1,2},{2,1},{3,18},{4,7},{5,20},{6,23},{7,4},{8,11},{9,24},... | collective-permute-start | bytes 221192 | tf_op jit(solution)/shard_map/ppermute | solution.py:383
  25.9 2.5 %collective-permute-done.5 = bf16[288,128]{1,0:T(8,128)(2,1)S(1)} collective-permute-done((bf16[288,128]{1,0:T(8,128)(2,1)S(1)}, bf16[288,128]{1,0:T(8,128)(2,1)S(1)}, u32[]{:S(2)}, u32[]{:S(2)}) %collective-permute-start.5) | collective-permute-done | bytes 73760 | tf_op jit(solution)/shard_map/ppermute | solution.py:383
  28.5 0.1 collective-permute-start.6
  28.5 3.8 %collective-permute-done.6 = bf16[288,128]{1,0:T(8,128)(2,1)S(1)} collective-permute-done((bf16[288,128]{1,0:T(8,128)(2,1)S(1)}, bf16[288,128]{1,0:T(8,128)(2,1)S(1)}, u32[]{:S(2)}, u32[]{:S(2)}) %collective-permute-start.6) | collective-permute-done | bytes 73760 | tf_op jit(solution)/shard_map/ppermute | solution.py:383
  32.3 0.2 collective-permute-start.7
  32.5 1.2 %collective-permute-done.7.theirs_ref = bf16[288,128]{1,0:T(8,128)(2,1)S(1)} collective-permute-done((bf16[288,128]{1,0:T(8,128)(2,1)S(1)}, bf16[288,128]{1,0:T(8,128)(2,1)S(1)}, u32[]{:S(2)}, u32[]{:S(2)}) %collective-permute-start.7) | collective-permute-done | bytes 73760 | tf_op jit(solution)/shard_map/ppermute | solution.py:383
  33.7 0.9 %shard_map.82 = (bf16[3,3,64,64]{3,2,1,0:T(8,128)(2,1)}, bf16[3,3,64,64]{3,2,1,0:T(8,128)(2,1)}) custom-call(bf16[288,128]{1,0:T(8,128)(2,1)S(1)} %multiply_convert_fusion.mine_ref, bf16[288,128]{1,0:T(8,128)(2,1)S(1)} %collective-permute-done.7.theirs_ref), custom_call_target="tpu_custom_call" | custom-call | tf_op jit(solution)/shard_map/pallas_call | solution.py:372
  (5 shorter events, 0.1 us)
Async XLA Ops:
  2.6 9.4 %collective-permute-start = (bf16[2,2,64,384]{3,2,1,0:T(8,128)(2,1)S(1)}, bf16[2,2,64,384]{3,2,1,0:T(8,128)(2,1)S(1)}, u32[]{:S(2)}, u32[]{:S(2)}) collective-permute-start(bf16[2,2,64,384]{3,2,1,0:T(8,128)(2,1)S(1)} %get-tuple-element.47.to_outer), channel_id=1, source_target_pairs={{0,7},{1,2},{2,1},{3,4},{4,3},{5,6},{6,5},{7,0},{8,15},{9,10},{10,... | collective-permute-start | bytes 589832 | tf_op jit(solution)/shard_map/ppermute | solution.py:383
  7.2 4.8 %collective-permute-start.1 = (bf16[2,2,64,384]{3,2,1,0:T(8,128)(2,1)S(1)}, bf16[2,2,64,384]{3,2,1,0:T(8,128)(2,1)S(1)}, u32[]{:S(2)}, u32[]{:S(2)}) collective-permute-start(bf16[2,2,64,384]{3,2,1,0:T(8,128)(2,1)S(1)} %get-tuple-element.48.to_mate), channel_id=1, source_target_pairs={{0,1},{1,0},{2,3},{3,2},{4,5},{5,4},{6,7},{7,6},{8,9},{9,8},{10,11... | collective-permute-start | bytes 589832 | tf_op jit(solution)/shard_map/ppermute | solution.py:383
  13.4 1.5 %collective-permute-start.2 = (bf16[288,128]{1,0:T(8,128)(2,1)S(1)}, bf16[288,128]{1,0:T(8,128)(2,1)S(1)}, u32[]{:S(2)}, u32[]{:S(2)}) collective-permute-start(bf16[288,128]{1,0:T(8,128)(2,1)S(1)} %get-tuple-element.62), channel_id=1, source_target_pairs={{0,1},{1,0},{2,3},{3,2},{4,5},{5,4},{6,7},{7,6},{8,9},{9,8},{10,11... | collective-permute-start | bytes 221192 | tf_op jit(solution)/shard_map/ppermute | solution.py:383
  15.0 4.0 %collective-permute-start.3 = (bf16[288,128]{1,0:T(8,128)(2,1)S(1)}, bf16[288,128]{1,0:T(8,128)(2,1)S(1)}, u32[]{:S(2)}, u32[]{:S(2)}) collective-permute-start(bf16[288,128]{1,0:T(8,128)(2,1)S(1)} %add_convert_fusion.3), channel_id=1, source_target_pairs={{0,9},{1,4},{2,7},{3,10},{4,1},{5,12},{6,15},{7,2},{8,13},{9,0},{1... | collective-permute-start | bytes 221192 | tf_op jit(solution)/shard_map/ppermute | solution.py:383
  19.0 5.5 %collective-permute-start.4 = (bf16[288,128]{1,0:T(8,128)(2,1)S(1)}, bf16[288,128]{1,0:T(8,128)(2,1)S(1)}, u32[]{:S(2)}, u32[]{:S(2)}) collective-permute-start(bf16[288,128]{1,0:T(8,128)(2,1)S(1)} %add_convert_fusion.2), channel_id=1, source_target_pairs={{0,5},{1,8},{2,11},{3,6},{4,13},{5,0},{6,3},{7,14},{8,1},{9,12},{1... | collective-permute-start | bytes 221192 | tf_op jit(solution)/shard_map/ppermute | solution.py:383
  24.6 3.8 %collective-permute-start.5 = (bf16[288,128]{1,0:T(8,128)(2,1)S(1)}, bf16[288,128]{1,0:T(8,128)(2,1)S(1)}, u32[]{:S(2)}, u32[]{:S(2)}) collective-permute-start(bf16[288,128]{1,0:T(8,128)(2,1)S(1)} %add_convert_fusion.1), channel_id=1, source_target_pairs={{0,17},{1,2},{2,1},{3,18},{4,7},{5,20},{6,23},{7,4},{8,11},{9,24},... | collective-permute-start | bytes 221192 | tf_op jit(solution)/shard_map/ppermute | solution.py:383
  28.5 3.8 %collective-permute-start.6 = (bf16[288,128]{1,0:T(8,128)(2,1)S(1)}, bf16[288,128]{1,0:T(8,128)(2,1)S(1)}, u32[]{:S(2)}, u32[]{:S(2)}) collective-permute-start(bf16[288,128]{1,0:T(8,128)(2,1)S(1)} %add_convert_fusion), channel_id=1, source_target_pairs={{0,3},{1,16},{2,19},{3,0},{4,21},{5,6},{6,5},{7,22},{8,25},{9,10},... | collective-permute-start | bytes 221192 | tf_op jit(solution)/shard_map/ppermute | solution.py:383
  32.3 1.3 %collective-permute-start.7 = (bf16[288,128]{1,0:T(8,128)(2,1)S(1)}, bf16[288,128]{1,0:T(8,128)(2,1)S(1)}, u32[]{:S(2)}, u32[]{:S(2)}) collective-permute-start(bf16[288,128]{1,0:T(8,128)(2,1)S(1)} %multiply_convert_fusion.mine_ref), channel_id=1, source_target_pairs={{0,1},{1,0},{2,3},{3,2},{4,5},{5,4},{6,7},{7,6},{8,9},{9,8},{10,11... | collective-permute-start | bytes 221192 | tf_op jit(solution)/shard_map/ppermute | solution.py:383

commit v5 on v4

v5 whole, which is shorter than its diff:
```python
import functools
import math

import jax
import jax.numpy as jnp
from jax import lax
from jax.experimental import pallas as pl
from jax.experimental.pallas import tpu as pltpu
from jax.sharding import PartitionSpec as P

gelu_coef = 0.7978845608
F32 = jnp.float32
BF16 = jnp.bfloat16
NT = (((1,), (1,)), ((), ()))


def gelu_pair(u):
    square = u * u
    inner = jnp.tanh(u * (gelu_coef + (gelu_coef * 0.044715) * square))
    a = 0.5 + 0.5 * inner
    value = u * a
    twice = 2.0 * gelu_coef + (6.0 * gelu_coef * 0.044715) * square
    return value, a + (value - value * a) * twice


def neighbours(v):
    lanes = 128
    tiles = [v[:, k : k + lanes] for k in range(0, v.shape[-1], lanes)]
    lane = lax.broadcasted_iota(jnp.int32, tiles[0].shape, 1)
    zero = jnp.zeros_like(tiles[0])
    up = [zero] + [pltpu.roll(t, 1, 1) for t in tiles]
    down = [pltpu.roll(t, lanes - 1, 1) for t in tiles] + [zero]
    below = [jnp.where(lane == 0, up[k], up[k + 1]) for k in range(len(tiles))]
    above = [jnp.where(lane == lanes - 1, down[k + 1], down[k]) for k in range(len(tiles))]
    return jnp.concatenate(below, axis=1), jnp.concatenate(above, axis=1)


def dot(a, b):
    return jnp.dot(a, b, preferred_element_type=F32)


def dot_nt(a, b):
    return lax.dot_general(a, b, NT, preferred_element_type=F32)


def three(v, adjoint):
    below, above = neighbours(v)
    return jnp.concatenate([above, v, below] if adjoint else [below, v, above], axis=0)


def prepare(k_ref, forward_ref, adjoint_ref):
    c = k_ref.shape[-1]
    for p in range(3):
        if forward_ref is not None:
            forward_ref[p * c : (p + 1) * c, :] = jnp.concatenate(
                [k_ref[p, q].astype(F32) for q in range(3)], axis=1
            ).astype(BF16)
        adjoint_ref[p * c : (p + 1) * c, :] = jnp.concatenate(
            [k_ref[p, q].astype(F32).T for q in range(3)], axis=1
        ).astype(BF16)


def products(i, w1, w2a, x3, e3, s3, y, z):
    c = w1.shape[0] // 3
    y[i] = dot(w1[...], x3)
    z[i, c : 2 * c, :] = dot(w2a[c : 2 * c, :], e3)
    sides = dot(jnp.concatenate([w2a[0:c, :], w2a[2 * c :, :]], axis=0), s3)
    z[i, 0:c, :] = sides[0:c]
    z[i, 2 * c :, :] = sides[c:]


def middle(u, grad, metric):
    hidden, slope = gelu_pair(u)
    delta = (grad * slope).astype(BF16)
    return hidden.astype(BF16), delta, (metric * delta.astype(F32)).astype(BF16)


def edges_term(
    t, fields, upstream, upstream_scaled, near_fields, near_scaled, delta, delta_scaled, hidden
):
    first = t == 0
    rows = []
    for p in range(3):
        left, right = [], []
        for side, (own, inner) in enumerate(((0, 1), (3, 2))):
            if p == 1:
                one, two, three_fields = delta[side], upstream[side], fields[own]
            else:
                one = delta_scaled[side]
                if (p == 0) == (side == 0):
                    two, three_fields = upstream_scaled[side], near_fields[side]
                else:
                    two, three_fields = near_scaled[side], fields[inner]
            left.append(jnp.where(first, one, two))
            right.append(jnp.where(first, three_fields, hidden[side]))
        rows.append(dot_nt(jnp.concatenate(left, axis=1), jnp.concatenate(right, axis=1)))
    return jnp.concatenate(rows, axis=0)


def put_packed(ref, total):
    half = total.shape[0] // 2
    wide = total.shape[1] // 3 * 2
    tail = total[:, wide:]
    ref[0 : 2 * half, :] = total[:, 0:wide].astype(ref.dtype)
    ref[2 * half :, :] = jnp.concatenate([tail[0:half], tail[half:]], axis=1).astype(ref.dtype)


def scatter_out(ref, value, first=0):
    c, n, lat = value.shape
    value = value.astype(F32).reshape(c * n, lat)
    whole = ref.shape[0] * 128 // lat
    for k in range(lat // 128):
        at = k * whole + first
        ref[at : at + c * n, :] = value[:, k * 128 : (k + 1) * 128]


def strided(ref, i, c, n):
    count = ref.shape[0] // (c * n)
    return [(k, pl.ds(k * c * n + i, c, stride=n)) for k in range(count)]


def column(ref, i, c, n):
    return jnp.concatenate([ref[at, :] for _, at in strided(ref, i, c, n)], axis=1)


def pack_kernel(
    x_hbm, e_hbm, m_hbm, k1_hbm, k2_hbm,
    xf, ef, mate_ref, outer_ref, row_ref, w1_ref, w1a_ref, w2a_ref,
    xs, es, ms, k1s, k2s, sems, small_sems,
):
    c, n, lat = x_hbm.shape
    chunks = sems.shape[1]
    w = c // chunks
    small = [
        pltpu.make_async_copy(src, dst, small_sems.at[k])
        for k, (src, dst) in enumerate(((k1_hbm, k1s), (k2_hbm, k2s), (m_hbm, ms)))
    ]
    for copy in small:
        copy.start()
    copies = []
    for k in range(chunks):
        for a, (src, dst) in enumerate(((x_hbm, xs), (e_hbm, es))):
            rows = pl.ds(k * w, w)
            copies.append(pltpu.make_async_copy(src.at[rows], dst.at[rows], sems.at[a, k]))
            copies[-1].start()
    for copy in small:
        copy.wait()
    row_ref[...] = ms[...].reshape(1, lat)
    prepare(k1s, w1_ref, w1a_ref)
    prepare(k2s, None, w2a_ref)
    for k in range(chunks):
        for a, (src, dst) in enumerate(((xs, xf), (es, ef))):
            copies[2 * k + a].wait()
            scatter_out(dst, src[k * w : (k + 1) * w], k * w * n)
    odd = lax.axis_index("lon") % 2 == 1
    for a, source in enumerate((xf, ef)):
        for k in range(2):
            low = column(source, k, c, n).astype(BF16)
            high = column(source, n - 2 + k, c, n).astype(BF16)
            mate_ref[a, k] = jnp.where(odd, low, high)
            outer_ref[a, k] = jnp.where(odd, high, low)


def interior_kernel(
    xf, ef, w1_ref, w2a_ref, m_ref,
    g1_ref, g2_ref, d_ref, s_ref, fields, upstream, upstream_scaled, u_ref, grad_ref, y_ref, z_ref,
    x3, e, es, y, z, h3,
):
    n, c, lat = d_ref.shape
    low, mid, high = slice(0, c), slice(c, 2 * c), slice(2 * c, 3 * c)
    metric = m_ref[...]
    blank = jnp.zeros((c, lat), BF16)
    for i in (0, n - 1):
        d_ref[i] = blank
        s_ref[i] = blank
    g1_ref[...] = jnp.zeros_like(g1_ref)
    g2_ref[...] = jnp.zeros_like(g2_ref)

    def terms(plain, scaled, value, columns):
        left = [jnp.concatenate([scaled[j + 1], plain[j], scaled[j - 1]], axis=0) for j in columns]
        return dot_nt(
            jnp.concatenate(left, axis=1), jnp.concatenate([value[j] for j in columns], axis=1)
        )

    inner = list(range(1, n - 1))
    groups = [inner[k : k + 7] for k in range(0, n - 2, 7)]
    second_todo, first_todo = list(groups), list(groups)
    for i in range(n + 1):
        if i < n:
            x3[i] = three(column(xf, i, c, n).astype(BF16), False)
            wide = column(ef, i, c, n)
            e[i] = wide.astype(BF16)
            es[i] = (metric * wide).astype(BF16)
            products(i, w1_ref, w2a_ref, x3[i], three(e[i], True), three(es[i], True), y, z)
        k = i - 1
        if 0 < k < n - 1:
            u = y[k, mid, :] + metric * (y[k - 1, low, :] + y[k + 1, high, :])
            grad = z[k, mid, :] + (z[k + 1, low, :] + z[k - 1, high, :])
            hidden, delta, scaled = middle(u, grad, metric)
            h3[k] = three(hidden, False)
            d_ref[k] = delta
            s_ref[k] = scaled
        if i == 3:
            g1_ref[0:c, :] += dot_nt(s_ref[1], x3[0])
        ready = i - 2 if i < n else n - 2
        if second_todo and second_todo[0][-1] <= ready:
            g2_ref[...] += terms(e, es, h3, second_todo.pop(0))
        if first_todo and first_todo[0][-1] <= (ready - 1 if i < n else ready):
            g1_ref[...] += terms(d_ref, s_ref, x3, first_todo.pop(0))
    g1_ref[2 * c :, :] += dot_nt(s_ref[n - 2], x3[n - 1])
    for side, own, next_in, one, two in ((0, 0, 1, low, high), (1, n - 1, n - 2, high, low)):
        u_ref[side] = y[own, mid, :] + metric * y[next_in, two, :]
        grad_ref[side] = z[own, mid, :] + z[next_in, one, :]
        y_ref[side] = y[own, two, :]
        z_ref[side] = z[own, one, :]
        upstream[side] = e[own]
        upstream_scaled[side] = es[next_in]
    for k, i in enumerate((0, 1, n - 2, n - 1)):
        fields[k] = x3[i]


def parity():
    place = lax.axis_index("dp") * lax.axis_size("lon") + lax.axis_index("lon")
    total, left = 0, lax.axis_size("dp") * lax.axis_size("lon") - 1
    while left:
        total, place, left = total + place % 2, place // 2, left // 2
    return total % 2


def beyond(odd, from_mate, from_outer, side, array, distance):
    k = distance - 1 if side else 2 - distance
    low_is_mate = jnp.where(odd, from_mate[array, k], from_outer[array, k])
    high_is_mate = jnp.where(odd, from_outer[array, k], from_mate[array, k])
    return high_is_mate if side else low_is_mate


def edge_kernel(
    from_outer, from_mate, m_ref, w1, w2a, g1, g2, fields, upstream, upstream_scaled, u_ref, grad_ref,
    sent_ref, near_fields, near_scaled, delta, delta_scaled, hidden,
):
    metric = m_ref[...]
    c = from_mate.shape[2]
    low, high = slice(0, c), slice(2 * c, 3 * c)
    odd = lax.axis_index("lon") % 2 == 1
    t = 1 - parity()
    for side, one, two in ((0, low, high), (1, high, low)):
        x, e = (beyond(odd, from_mate, from_outer, side, a, 1) for a in range(2))
        near_fields[side] = three(x, False)
        near_scaled[side] = (metric * e.astype(F32)).astype(BF16)
        u = u_ref[side] + metric * dot(w1[one, :], near_fields[side])
        grad = grad_ref[side] + dot(w2a[two, :], three(near_scaled[side], True))
        h, delta[side], delta_scaled[side] = middle(u, grad, metric)
        hidden[side] = three(h, False)
    total = edges_term(
        t, fields, upstream, upstream_scaled, near_fields, near_scaled, delta, delta_scaled, hidden
    )
    put_packed(sent_ref, total + jnp.where(t == 0, g1[...], g2[...]))


def kept_kernel(
    from_outer, from_mate, m_ref, w1, w2a, g1, g2, fields, upstream, upstream_scaled, y_ref, z_ref,
    near_fields, near_scaled, delta, delta_scaled, hidden,
    kept_ref, near_delta, near_delta_scaled,
):
    metric = m_ref[...]
    c = from_mate.shape[2]
    low, mid, high = slice(0, c), slice(c, 2 * c), slice(2 * c, 3 * c)
    odd = lax.axis_index("lon") % 2 == 1
    t = parity()
    total = edges_term(
        t, fields, upstream, upstream_scaled, near_fields, near_scaled, delta, delta_scaled, hidden
    )
    put_packed(kept_ref, total + jnp.where(t == 0, g1[...], g2[...]))
    for side, one, two in ((0, low, high), (1, high, low)):
        x, e = (beyond(odd, from_mate, from_outer, side, a, 2) for a in range(2))
        near_e = beyond(odd, from_mate, from_outer, side, 1, 1)
        scaled = (metric * e.astype(F32)).astype(BF16)
        u = dot(w1[mid, :], near_fields[side]) + metric * (
            dot(w1[one, :], three(x, False)) + y_ref[side]
        )
        grad = dot(w2a[mid, :], three(near_e, True)) + (
            dot(w2a[two, :], three(scaled, True)) + z_ref[side]
        )
        _, near_delta[side], near_delta_scaled[side] = middle(u, grad, metric)


def field_kernel(
    d_in, s_in, delta, delta_scaled, near_delta, near_delta_scaled, w1a_ref, out_ref, zm, zs, *, start
):
    c, n = d_in.shape[1], d_in.shape[0]
    count = out_ref.shape[0]
    sides = jnp.concatenate([w1a_ref[0:c, :], w1a_ref[2 * c :, :]], axis=0)
    edges = {
        -1: (near_delta, near_delta_scaled, 0),
        0: (delta, delta_scaled, 0),
        n - 1: (delta, delta_scaled, 1),
        n: (near_delta, near_delta_scaled, 1),
    }
    for place in range(count + 2):
        i = start + place - 1
        plain, scaled, k = edges.get(i, (d_in, s_in, i))
        if 0 < place < count + 1:
            zm[place] = dot(w1a_ref[c : 2 * c, :], three(plain[k], True))
        zs[place] = dot(sides, three(scaled[k], True))
        if place >= 2:
            out_ref[place - 2] = zm[place - 1] + (zs[place, 0:c, :] + zs[place - 2, c:, :])


def assemble_kernel(*refs):
    e_ref, parts, out_ref, ef = refs[0], refs[1:-2], refs[-2], refs[-1]
    c, n, lat = out_ref.shape
    i = 0
    for part in parts:
        for k in range(part.shape[0]):
            grad = part[k]
            for t, at in strided(ef, i, c, n):
                ef[at, :] = e_ref[at, :] + grad[:, t * 128 : (t + 1) * 128]
            i += 1
    for k in range(lat // 128):
        part = ef[k * c * n : (k + 1) * c * n, :].reshape(c, n, 128)
        out_ref[:, :, k * 128 : (k + 1) * 128] = part.astype(BF16)


def final_kernel(mine_ref, theirs_ref, out1_ref, out2_ref):
    c = out1_ref.shape[-1]
    odd = parity() == 1
    mine, theirs = mine_ref[...], theirs_ref[...]
    for out, packed in (
        (out1_ref, jnp.where(odd, theirs, mine)),
        (out2_ref, jnp.where(odd, mine, theirs)),
    ):
        tail = packed[3 * c :]
        tail = jnp.concatenate([tail[:, 0:c], tail[:, c:]], axis=0)
        for p in range(3):
            rows = slice(p * c, (p + 1) * c)
            out[p, 0] = packed[rows, 0:c]
            out[p, 1] = packed[rows, c:]
            out[p, 2] = tail[rows]


def vmem(count):
    return [pl.BlockSpec(memory_space=pltpu.VMEM)] * count


def size_of(shapes):
    return sum(math.prod(s) * jnp.dtype(d).itemsize for s, d in shapes)


def call(kernel, outs, scratch, *args, specs=None):
    mib = 2**20
    buffers = [s for s in scratch if isinstance(s, tuple)]
    limit = size_of(buffers) + size_of(outs) + size_of([(a.shape, a.dtype) for a in args])
    return pl.pallas_call(
        kernel,
        out_shape=[jax.ShapeDtypeStruct(s, d) for s, d in outs],
        in_specs=specs or vmem(len(args)),
        out_specs=vmem(len(outs)),
        scratch_shapes=[pltpu.VMEM(*s) if isinstance(s, tuple) else s for s in scratch],
        compiler_params=pltpu.CompilerParams(vmem_limit_bytes=(limit // mib + 6) * mib),
    )(*args)


def exchange(value, pairs):
    return lax.ppermute(value, ("dp", "lon"), pairs)


def one_sample(x, e, kernel_first, kernel_second, metric):
    c, n, lat = x.shape
    wide = 3 * c
    chunks = 1
    count = lax.axis_size("dp") * lax.axis_size("lon")
    lon = lax.axis_size("lon")
    mates = [(i, i ^ 1) for i in range(count)]
    outers = [
        (i, i // lon * lon + (i % lon + (1 if i % lon % 2 else -1)) % lon) for i in range(count)
    ]
    strided_form = ((c * n * lat // 128, 128), F32)
    column = (wide, lat)
    halo = ((2, 2, c, lat), BF16)
    square = (wide, wide)
    inputs = (x, e, metric, kernel_first, kernel_second)
    xf, ef, to_mate, to_outer, row, w1, w1a, w2a = call(
        pack_kernel,
        [strided_form] * 2 + [halo] * 2 + [((1, lat), F32)] + [(square, BF16)] * 3,
        [((c, n, lat), BF16)] * 2
        + [((lat,), F32)]
        + [((3, 3, c, c), BF16)] * 2
        + [pltpu.SemaphoreType.DMA((2, chunks)), pltpu.SemaphoreType.DMA((3,))],
        *(pltpu.with_memory_space_constraint(a, pltpu.HBM) for a in inputs),
        specs=[pl.BlockSpec(memory_space=pltpu.HBM)] * len(inputs),
    )
    from_outer = exchange(to_outer, outers)
    from_mate = exchange(to_mate, mates)
    wide_columns = ((n,) + column, F32)
    pair = ((2, c, lat), F32)
    two = ((2, c, lat), BF16)
    two_wide = ((2,) + column, BF16)
    g1, g2, d, s, fields, upstream, upstream_scaled, u, grad, y, z = call(
        interior_kernel,
        [(square, F32)] * 2
        + [((n, c, lat), BF16)] * 2
        + [((4,) + column, BF16)]
        + [two] * 2
        + [pair] * 4,
        [((n,) + column, BF16)]
        + [((n, c, lat), BF16)] * 2
        + [wide_columns] * 2
        + [((n,) + column, BF16)],
        xf, ef, w1, w2a, row,
    )
    packed = (3 * wide // 2, 2 * c)
    common = (from_outer, from_mate, row, w1, w2a, g1, g2, fields, upstream, upstream_scaled)
    sent, *edge = call(
        edge_kernel, [(packed, BF16), two_wide, two, two, two, two_wide], [], *common, u, grad
    )
    near_fields, near_scaled, delta, delta_scaled, hidden = edge

    def keep(done, gate):
        return call(
            kept_kernel, [(packed, F32), two, two], [],
            *common, y, z, near_fields, near_scaled, delta, delta_scaled, gate(hidden),
        )

    def part(done, gate, start, count):
        return call(
            functools.partial(field_kernel, start=start),
            [((count, c, lat), F32)],
            [((count + 2, c, lat), F32), ((count + 2, 2 * c, lat), F32)],
            d, s, delta, delta_scaled, done[0][1], done[0][2], gate(w1a),
        )

    def assemble(done, gate):
        return call(
            assemble_kernel, [((c, n, lat), BF16)], [strided_form],
            ef, done[1][0], gate(done[2][0]),
        )

    half = n // 2
    return sent, [
        keep,
        lambda done, gate: part(done, gate, 0, half),
        lambda done, gate: part(done, gate, half, n - half),
        assemble,
    ]


def sum_everywhere(sent, jobs, factor):
    dp, lon = lax.axis_size("dp"), lax.axis_size("lon")
    count = dp * lon
    swap = [(i, i ^ 1) for i in range(count)]
    jobs, done = list(jobs), []

    def beside(sent, pairs):
        got = exchange(sent, pairs)
        if jobs:
            result = jobs.pop(0)(done, lambda x: lax.optimization_barrier((sent, x))[1])
            got, first = lax.optimization_barrier((got, result[0]))
            done.append([first] + list(result[1:]))
        return got

    got = beside(sent, swap)
    total = done[0][0] + got.astype(F32)
    along_lon = [1 << k for k in range(1, lon.bit_length() - 1)]
    along_dp = [lon << k for k in range(dp.bit_length() - 1)]
    bits = []
    while along_lon or along_dp:
        if along_dp:
            bits.append(along_dp.pop(0))
        if along_lon:
            bits.append(along_lon.pop())
    other = list(bits)
    for k in range(0, len(bits) - 1, 2):
        other[k], other[k + 1] = bits[k + 1], bits[k]
    for even_bit, odd_bit in zip(bits, other):
        sent = total.astype(BF16)
        got = beside(
            sent, [(i, i ^ 1 ^ (odd_bit if i.bit_count() & 1 else even_bit)) for i in range(count)]
        )
        total = sent.astype(F32) + got.astype(F32)
    while jobs:
        done.append(jobs.pop(0)(done, lambda x: x))
    mine = (total * factor).astype(BF16)
    return mine, exchange(mine, swap), done


def per_device(fields, cotangent, kernel_first, kernel_second, metric):
    samples, c, n, lat = fields.shape
    counted = (
        float(samples * lax.axis_size("dp")) * float(n * lax.axis_size("lon")) * float(lat)
    )
    factor = jnp.float32(1.0 / counted**0.5)
    sent, jobs = one_sample(fields[0], cotangent[0], kernel_first, kernel_second, metric)
    mine, theirs, done = sum_everywhere(sent, jobs, factor)
    grad_first, grad_second = call(
        final_kernel, [((3, 3, c, c), BF16)] * 2, [], mine, theirs
    )
    return done[-1][0][None], grad_first, grad_second


def solution(mesh):
    placed = (P("dp", None, "lon", None), P("dp", None, "lon", None), P(), P(), P())
    return jax.shard_map(
        per_device,
        mesh=mesh,
        in_specs=placed,
        out_specs=(P("dp", None, "lon", None), P(), P()),
        check_vma=False,
    )
```

time: 34.7 us -> 34.2 us (0.986)
  waiting for transfers between devices: 10.5 us -> 9.9 us
    ppermute x8, waiting for transfers between devices: 10.5 us -> 9.9 us  [exchange(): return lax.ppermute(value, ('dp', 'lon'), pairs)]
    pallas_call x7 -> x8, Pallas kernels: 12.8 us -> 12.7 us  [call(): pl.pallas_call(kernel, out_shape=[jax.ShapeDtypeStruct(s, d) for s, d in...]
  transfers between devices with their start and end apart: 8 -> 8, of which waited for: 5 -> 6; matrix products, arithmetic and copies ran while one was open for 0% -> 0% of each run, Pallas kernels for 25% -> 26%
where the time goes in v5:
time: 34.2 us; the launch traced here: 34 us
  Pallas kernels  12.7 us (37%)
  starting transfers between devices  10.6 us (31%)
  waiting for transfers between devices  9.9 us (29%)
  between operations  0.72 us (2%)
    pallas_call x8, Pallas kernels, call(): pl.pallas_call(kernel, out_shape=[jax.ShapeDtypeStruct(s, d) for s, d in...  12.7 us
    ppermute x8, starting transfers between devices, exchange(): return lax.ppermute(value, ('dp', 'lon'), pairs)  10.6 us
    ppermute x8, waiting for transfers between devices, exchange(): return lax.ppermute(value, ('dp', 'lon'), pairs)  9.9 us
  transfers between devices with their start and end apart: 8, of which 6 were waited for; matrix products, arithmetic and copies ran while one was open for 0% of the time, Pallas kernels for 26%

profile of v5, /device:TPU:0, one launch (start us, length us, event | category | flops | bytes accessed | tf_op | source)
XLA Modules:
  0.0 34.0 jit_solution(13090730078459309374)
XLA Ops:
  0.6 2.0 %shard_map.76 = (f32[3072,128]{1,0:T(8,128)S(1)}, f32[3072,128]{1,0:T(8,128)S(1)}, bf16[2,2,64,384]{3,2,1,0:T(8,128)(2,1)S(1)}, bf16[2,2,64,384]{3,2,1,0:T(8,128...) custom-call(bf16[64,16,384]{2,1,0:T(8,128)(2,1)} %bitcast.3, ...), custom_call_target="tpu_custom_call" | custom-call | tf_op jit(solution)/shard_map/pallas_call | solution.py:353
  2.6 4.6 %collective-permute-start = (bf16[2,2,64,384]{3,2,1,0:T(8,128)(2,1)S(1)}, bf16[2,2,64,384]{3,2,1,0:T(8,128)(2,1)S(1)}, u32[]{:S(2)}, u32[]{:S(2)}) collective-permute-start(bf16[2,2,64,384]{3,2,1,0:T(8,128)(2,1)S(1)} %get-tuple-element.45), channel_id=1, source_target_pairs={{0,7},{1,2},{2,1},{3,4},{4,3},{5,6},{6,5},{7,0},{8,15},{9,10},{10,... | collective-permute-start | bytes 589832 | tf_op jit(solution)/shard_map/ppermute | solution.py:364
  7.2 0.0 collective-permute-start.1
  7.2 4.6 %shard_map.77 = (f32[192,192]{1,0:T(8,128)S(1)}, f32[192,192]{1,0:T(8,128)S(1)}, bf16[16,64,384]{2,1,0:T(8,128)(2,1)S(1)}, bf16[16,64,384]{2,1,0:T(8,128)(2,1)S(...) custom-call(f32[3072,128]{1,0:T(8,128)S(1)} %get-tuple-element.50.xf, ...), custom_call_target="tpu_custom_call" | custom-call | tf_op jit(solution)/shard_map/pallas_call | solution.py:353
  11.8 0.0 collective-permute-done.from_outer
  11.8 0.0 collective-permute-done.1.from_mate
  11.8 0.9 %shard_map.78 = (bf16[288,128]{1,0:T(8,128)(2,1)S(1)}, bf16[2,192,384]{2,1,0:T(8,128)(2,1)S(1)}, bf16[2,64,384]{2,1,0:T(8,128)(2,1)S(1)}, bf16[2,64,384]{2,1,0:T...) custom-call(bf16[2,2,64,384]{3,2,1,0:T(8,128)(2,1)S(1)} %collective-permute-done.from_outer, ...), custom_call_target="tpu_custom_call" | custom-call | tf_op jit(solution)/shard_map/pallas_call | solution.py:353
  12.8 0.6 %collective-permute-start.2 = (bf16[288,128]{1,0:T(8,128)(2,1)S(1)}, bf16[288,128]{1,0:T(8,128)(2,1)S(1)}, u32[]{:S(2)}, u32[]{:S(2)}) collective-permute-start(bf16[288,128]{1,0:T(8,128)(2,1)S(1)} %get-tuple-element.59), channel_id=1, source_target_pairs={{0,1},{1,0},{2,3},{3,2},{4,5},{5,4},{6,7},{7,6},{8,9},{9,8},{10,11... | collective-permute-start | bytes 221192 | tf_op jit(solution)/shard_map/ppermute | solution.py:364
  13.3 0.7 %shard_map.79 = (f32[288,128]{1,0:T(8,128)S(1)}, bf16[2,64,384]{2,1,0:T(8,128)(2,1)S(1)}, bf16[2,64,384]{2,1,0:T(8,128)(2,1)S(1)}) custom-call(bf16[2,2,64,384]{3,2,1,0:T(8,128)(2,1)S(1)} %collective-permute-done.from_outer, bf16[2,2,64,384]{3,2,1,0:T(8,128)(2,1)S(1)} %collective-permute-done.1.from_mate, f32[1,384]{1,0:T(1,128)S(1)} %get-tuple-element.47.m_ref, ...), custom_call_target="tpu_custom_call" | custom-call | tf_op jit(solution)/shard_map/pallas_call | solution.py:353
  14.1 0.2 collective-permute-done.2
  14.3 2.2 %collective-permute-start.3 = (bf16[288,128]{1,0:T(8,128)(2,1)S(1)}, bf16[288,128]{1,0:T(8,128)(2,1)S(1)}, u32[]{:S(2)}, u32[]{:S(2)}) collective-permute-start(bf16[288,128]{1,0:T(8,128)(2,1)S(1)} %add_convert_fusion.3), channel_id=1, source_target_pairs={{0,9},{1,4},{2,7},{3,10},{4,1},{5,12},{6,15},{7,2},{8,13},{9,0},{1... | collective-permute-start | bytes 221192 | tf_op jit(solution)/shard_map/ppermute | solution.py:364
  16.5 0.8 %shard_map.80.refs_1_ = f32[8,64,384]{2,1,0:T(8,128)S(1)} custom-call(bf16[16,64,384]{2,1,0:T(8,128)(2,1)S(1)} %get-tuple-element.71.d_in, bf16[16,64,384]{2,1,0:T(8,128)(2,1)S(1)} %get-tuple-element.72.s_in, bf16[2,64,384]{2,1,0:T(8,128)(2,1)S(1)} %get-tuple-element.64.delta, bf16[2,64,384]{2,1,0:T(8,128)(2,1)S(1)} %get-tuple-element.65.delta_scaled, ...), custom_call_target="tpu_custom_call" | custom-call | tf_op jit(solution)/shard_map/pallas_call | solution.py:353
  17.3 1.2 %collective-permute-done.3 = bf16[288,128]{1,0:T(8,128)(2,1)S(1)} collective-permute-done((bf16[288,128]{1,0:T(8,128)(2,1)S(1)}, bf16[288,128]{1,0:T(8,128)(2,1)S(1)}, u32[]{:S(2)}, u32[]{:S(2)}) %collective-permute-start.3) | collective-permute-done | bytes 73760 | tf_op jit(solution)/shard_map/ppermute | solution.py:364
  18.5 1.7 %collective-permute-start.4 = (bf16[288,128]{1,0:T(8,128)(2,1)S(1)}, bf16[288,128]{1,0:T(8,128)(2,1)S(1)}, u32[]{:S(2)}, u32[]{:S(2)}) collective-permute-start(bf16[288,128]{1,0:T(8,128)(2,1)S(1)} %add_convert_fusion.2), channel_id=1, source_target_pairs={{0,5},{1,8},{2,11},{3,6},{4,13},{5,0},{6,3},{7,14},{8,1},{9,12},{1... | collective-permute-start | bytes 221192 | tf_op jit(solution)/shard_map/ppermute | solution.py:364
  20.2 0.8 %shard_map.81.refs_2_ = f32[8,64,384]{2,1,0:T(8,128)S(1)} custom-call(bf16[16,64,384]{2,1,0:T(8,128)(2,1)S(1)} %get-tuple-element.71.d_in, bf16[16,64,384]{2,1,0:T(8,128)(2,1)S(1)} %get-tuple-element.72.s_in, bf16[2,64,384]{2,1,0:T(8,128)(2,1)S(1)} %get-tuple-element.64.delta, bf16[2,64,384]{2,1,0:T(8,128)(2,1)S(1)} %get-tuple-element.65.delta_scaled, ...), custom_call_target="tpu_custom_call" | custom-call | tf_op jit(solution)/shard_map/pallas_call | solution.py:353
  21.0 3.0 %collective-permute-done.4 = bf16[288,128]{1,0:T(8,128)(2,1)S(1)} collective-permute-done((bf16[288,128]{1,0:T(8,128)(2,1)S(1)}, bf16[288,128]{1,0:T(8,128)(2,1)S(1)}, u32[]{:S(2)}, u32[]{:S(2)}) %collective-permute-start.4) | collective-permute-done | bytes 73760 | tf_op jit(solution)/shard_map/ppermute | solution.py:364
  24.1 1.3 %collective-permute-start.5 = (bf16[288,128]{1,0:T(8,128)(2,1)S(1)}, bf16[288,128]{1,0:T(8,128)(2,1)S(1)}, u32[]{:S(2)}, u32[]{:S(2)}) collective-permute-start(bf16[288,128]{1,0:T(8,128)(2,1)S(1)} %add_convert_fusion.1), channel_id=1, source_target_pairs={{0,17},{1,2},{2,1},{3,18},{4,7},{5,20},{6,23},{7,4},{8,11},{9,24},... | collective-permute-start | bytes 221192 | tf_op jit(solution)/shard_map/ppermute | solution.py:364
  25.4 1.9 %shard_map.82 = bf16[64,16,384]{2,1,0:T(8,128)(2,1)} custom-call(f32[3072,128]{1,0:T(8,128)S(1)} %get-tuple-element.51.ef.refs_0_, f32[8,64,384]{2,1,0:T(8,128)S(1)} %shard_map.80.refs_1_, f32[8,64,384]{2,1,0:T(8,128)S(1)} %shard_map.81.refs_2_), custom_call_target="tpu_custom_call" | custom-call | tf_op jit(solution)/shard_map/pallas_call | solution.py:353
  27.3 0.6 %collective-permute-done.5 = bf16[288,128]{1,0:T(8,128)(2,1)S(1)} collective-permute-done((bf16[288,128]{1,0:T(8,128)(2,1)S(1)}, bf16[288,128]{1,0:T(8,128)(2,1)S(1)}, u32[]{:S(2)}, u32[]{:S(2)}) %collective-permute-start.5) | collective-permute-done | bytes 73760 | tf_op jit(solution)/shard_map/ppermute | solution.py:364
  28.0 0.1 collective-permute-start.6
  28.0 3.8 %collective-permute-done.6 = bf16[288,128]{1,0:T(8,128)(2,1)S(1)} collective-permute-done((bf16[288,128]{1,0:T(8,128)(2,1)S(1)}, bf16[288,128]{1,0:T(8,128)(2,1)S(1)}, u32[]{:S(2)}, u32[]{:S(2)}) %collective-permute-start.6) | collective-permute-done | bytes 73760 | tf_op jit(solution)/shard_map/ppermute | solution.py:364
  31.8 0.2 collective-permute-start.7
  32.0 1.2 %collective-permute-done.7.theirs_ref = bf16[288,128]{1,0:T(8,128)(2,1)S(1)} collective-permute-done((bf16[288,128]{1,0:T(8,128)(2,1)S(1)}, bf16[288,128]{1,0:T(8,128)(2,1)S(1)}, u32[]{:S(2)}, u32[]{:S(2)}) %collective-permute-start.7) | collective-permute-done | bytes 73760 | tf_op jit(solution)/shard_map/ppermute | solution.py:364
  33.2 0.9 %shard_map.83 = (bf16[3,3,64,64]{3,2,1,0:T(8,128)(2,1)}, bf16[3,3,64,64]{3,2,1,0:T(8,128)(2,1)}) custom-call(bf16[288,128]{1,0:T(8,128)(2,1)S(1)} %multiply_convert_fusion.mine_ref, bf16[288,128]{1,0:T(8,128)(2,1)S(1)} %collective-permute-done.7.theirs_ref), custom_call_target="tpu_custom_call" | custom-call | tf_op jit(solution)/shard_map/pallas_call | solution.py:353
  (5 shorter events, 0.1 us)
Async XLA Ops:
  2.6 9.2 %collective-permute-start = (bf16[2,2,64,384]{3,2,1,0:T(8,128)(2,1)S(1)}, bf16[2,2,64,384]{3,2,1,0:T(8,128)(2,1)S(1)}, u32[]{:S(2)}, u32[]{:S(2)}) collective-permute-start(bf16[2,2,64,384]{3,2,1,0:T(8,128)(2,1)S(1)} %get-tuple-element.45), channel_id=1, source_target_pairs={{0,7},{1,2},{2,1},{3,4},{4,3},{5,6},{6,5},{7,0},{8,15},{9,10},{10,... | collective-permute-start | bytes 589832 | tf_op jit(solution)/shard_map/ppermute | solution.py:364
  7.2 4.7 %collective-permute-start.1 = (bf16[2,2,64,384]{3,2,1,0:T(8,128)(2,1)S(1)}, bf16[2,2,64,384]{3,2,1,0:T(8,128)(2,1)S(1)}, u32[]{:S(2)}, u32[]{:S(2)}) collective-permute-start(bf16[2,2,64,384]{3,2,1,0:T(8,128)(2,1)S(1)} %get-tuple-element.46), channel_id=1, source_target_pairs={{0,1},{1,0},{2,3},{3,2},{4,5},{5,4},{6,7},{7,6},{8,9},{9,8},{10,11... | collective-permute-start | bytes 589832 | tf_op jit(solution)/shard_map/ppermute | solution.py:364
  12.8 1.5 %collective-permute-start.2 = (bf16[288,128]{1,0:T(8,128)(2,1)S(1)}, bf16[288,128]{1,0:T(8,128)(2,1)S(1)}, u32[]{:S(2)}, u32[]{:S(2)}) collective-permute-start(bf16[288,128]{1,0:T(8,128)(2,1)S(1)} %get-tuple-element.59), channel_id=1, source_target_pairs={{0,1},{1,0},{2,3},{3,2},{4,5},{5,4},{6,7},{7,6},{8,9},{9,8},{10,11... | collective-permute-start | bytes 221192 | tf_op jit(solution)/shard_map/ppermute | solution.py:364
  14.3 4.2 %collective-permute-start.3 = (bf16[288,128]{1,0:T(8,128)(2,1)S(1)}, bf16[288,128]{1,0:T(8,128)(2,1)S(1)}, u32[]{:S(2)}, u32[]{:S(2)}) collective-permute-start(bf16[288,128]{1,0:T(8,128)(2,1)S(1)} %add_convert_fusion.3), channel_id=1, source_target_pairs={{0,9},{1,4},{2,7},{3,10},{4,1},{5,12},{6,15},{7,2},{8,13},{9,0},{1... | collective-permute-start | bytes 221192 | tf_op jit(solution)/shard_map/ppermute | solution.py:364
  18.5 5.5 %collective-permute-start.4 = (bf16[288,128]{1,0:T(8,128)(2,1)S(1)}, bf16[288,128]{1,0:T(8,128)(2,1)S(1)}, u32[]{:S(2)}, u32[]{:S(2)}) collective-permute-start(bf16[288,128]{1,0:T(8,128)(2,1)S(1)} %add_convert_fusion.2), channel_id=1, source_target_pairs={{0,5},{1,8},{2,11},{3,6},{4,13},{5,0},{6,3},{7,14},{8,1},{9,12},{1... | collective-permute-start | bytes 221192 | tf_op jit(solution)/shard_map/ppermute | solution.py:364
  24.1 3.8 %collective-permute-start.5 = (bf16[288,128]{1,0:T(8,128)(2,1)S(1)}, bf16[288,128]{1,0:T(8,128)(2,1)S(1)}, u32[]{:S(2)}, u32[]{:S(2)}) collective-permute-start(bf16[288,128]{1,0:T(8,128)(2,1)S(1)} %add_convert_fusion.1), channel_id=1, source_target_pairs={{0,17},{1,2},{2,1},{3,18},{4,7},{5,20},{6,23},{7,4},{8,11},{9,24},... | collective-permute-start | bytes 221192 | tf_op jit(solution)/shard_map/ppermute | solution.py:364
  28.0 3.8 %collective-permute-start.6 = (bf16[288,128]{1,0:T(8,128)(2,1)S(1)}, bf16[288,128]{1,0:T(8,128)(2,1)S(1)}, u32[]{:S(2)}, u32[]{:S(2)}) collective-permute-start(bf16[288,128]{1,0:T(8,128)(2,1)S(1)} %add_convert_fusion), channel_id=1, source_target_pairs={{0,3},{1,16},{2,19},{3,0},{4,21},{5,6},{6,5},{7,22},{8,25},{9,10},... | collective-permute-start | bytes 221192 | tf_op jit(solution)/shard_map/ppermute | solution.py:364
  31.8 1.3 %collective-permute-start.7 = (bf16[288,128]{1,0:T(8,128)(2,1)S(1)}, bf16[288,128]{1,0:T(8,128)(2,1)S(1)}, u32[]{:S(2)}, u32[]{:S(2)}) collective-permute-start(bf16[288,128]{1,0:T(8,128)(2,1)S(1)} %multiply_convert_fusion.mine_ref), channel_id=1, source_target_pairs={{0,1},{1,0},{2,3},{3,2},{4,5},{5,4},{6,7},{7,6},{8,9},{9,8},{10,11... | collective-permute-start | bytes 221192 | tf_op jit(solution)/shard_map/ppermute | solution.py:364

commit v6 on v5

--- a/solution.py
+++ b/solution.py
@@ -105,70 +105,59 @@
     ref[2 * half :, :] = jnp.concatenate([tail[0:half], tail[half:]], axis=1).astype(ref.dtype)
 
 
-def scatter_out(ref, value, first=0):
-    c, n, lat = value.shape
-    value = value.astype(F32).reshape(c * n, lat)
-    whole = ref.shape[0] * 128 // lat
-    for k in range(lat // 128):
-        at = k * whole + first
-        ref[at : at + c * n, :] = value[:, k * 128 : (k + 1) * 128]
-
-
-def strided(ref, i, c, n):
-    count = ref.shape[0] // (c * n)
-    return [(k, pl.ds(k * c * n + i, c, stride=n)) for k in range(count)]
-
-
-def column(ref, i, c, n):
-    return jnp.concatenate([ref[at, :] for _, at in strided(ref, i, c, n)], axis=1)
+def turning(n, back=False, edges=False):
+    shape = (64 if edges else 16 * n, 16 * n)
+    row = lax.broadcasted_iota(jnp.int32, shape, 1 if back else 0)
+    source = lax.broadcasted_iota(jnp.int32, shape, 0 if back else 1)
+    place = lax.shift_right_logical(row, jnp.full_like(row, 4))
+    if edges:
+        place = jnp.where(place < 2, place, place + n - 4)
+    return jnp.where(source == (row & 15) * n + place, 1.0, 0.0).astype(BF16)
+
+
+def turn_columns(turn, source, target):
+    c, n, lat = source.shape
+    for b in range(0, c, 16):
+        turned = dot(turn, source[b : b + 16].reshape(16 * n, lat)).astype(BF16)
+        for i in range(turn.shape[0] // 16):
+            target[i, b : b + 16, :] = turned[16 * i : 16 * (i + 1)]
 
 
 def pack_kernel(
-    x_hbm, e_hbm, m_hbm, k1_hbm, k2_hbm,
-    xf, ef, mate_ref, outer_ref, row_ref, w1_ref, w1a_ref, w2a_ref,
-    xs, es, ms, k1s, k2s, sems, small_sems,
-):
-    c, n, lat = x_hbm.shape
-    chunks = sems.shape[1]
-    w = c // chunks
-    small = [
-        pltpu.make_async_copy(src, dst, small_sems.at[k])
-        for k, (src, dst) in enumerate(((k1_hbm, k1s), (k2_hbm, k2s), (m_hbm, ms)))
+    x_hbm, e_hbm, m_hbm, x_ref, e_ref, mate_ref, outer_ref, row_ref, edges, ms, sems
+):
+    n, lat = x_hbm.shape[1:]
+    copies = [
+        pltpu.make_async_copy(src, dst, sems.at[a])
+        for a, (src, dst) in enumerate(((x_hbm, x_ref), (e_hbm, e_ref), (m_hbm, ms)))
     ]
-    for copy in small:
+    for copy in copies:
         copy.start()
-    copies = []
-    for k in range(chunks):
-        for a, (src, dst) in enumerate(((x_hbm, xs), (e_hbm, es))):
-            rows = pl.ds(k * w, w)
-            copies.append(pltpu.make_async_copy(src.at[rows], dst.at[rows], sems.at[a, k]))
-            copies[-1].start()
-    for copy in small:
-        copy.wait()
+    turn = turning(n, edges=True)
+    odd = lax.axis_index("lon") % 2 == 1
+    for a, source in enumerate((x_ref, e_ref)):
+        copies[a].wait()
+        turn_columns(turn, source, edges)
+        for k in range(2):
+            mate_ref[a, k] = jnp.where(odd, edges[k], edges[2 + k])
+            outer_ref[a, k] = jnp.where(odd, edges[2 + k], edges[k])
+    copies[2].wait()
     row_ref[...] = ms[...].reshape(1, lat)
-    prepare(k1s, w1_ref, w1a_ref)
-    prepare(k2s, None, w2a_ref)
-    for k in range(chunks):
-        for a, (src, dst) in enumerate(((xs, xf), (es, ef))):
-            copies[2 * k + a].wait()
-            scatter_out(dst, src[k * w : (k + 1) * w], k * w * n)
-    odd = lax.axis_index("lon") % 2 == 1
-    for a, source in enumerate((xf, ef)):
-        for k in range(2):
-            low = column(source, k, c, n).astype(BF16)
-            high = column(source, n - 2 + k, c, n).astype(BF16)
-            mate_ref[a, k] = jnp.where(odd, low, high)
-            outer_ref[a, k] = jnp.where(odd, high, low)
 
 
 def interior_kernel(
-    xf, ef, w1_ref, w2a_ref, m_ref,
-    g1_ref, g2_ref, d_ref, s_ref, fields, upstream, upstream_scaled, u_ref, grad_ref, y_ref, z_ref,
-    x3, e, es, y, z, h3,
+    x_ref, e_ref, k1_ref, k2_ref, m_ref,
+    e, w1_ref, w1a_ref, w2a_ref, g1_ref, g2_ref, d_ref, s_ref, fields, upstream, upstream_scaled, u_ref, grad_ref, y_ref, z_ref,
+    x, x3, es, y, z, h3,
 ):
     n, c, lat = d_ref.shape
     low, mid, high = slice(0, c), slice(c, 2 * c), slice(2 * c, 3 * c)
     metric = m_ref[...]
+    turn = turning(n)
+    turn_columns(turn, x_ref, x)
+    turn_columns(turn, e_ref, e)
+    prepare(k1_ref, w1_ref, w1a_ref)
+    prepare(k2_ref, None, w2a_ref)
     blank = jnp.zeros((c, lat), BF16)
     for i in (0, n - 1):
         d_ref[i] = blank
@@ -187,10 +176,8 @@
     second_todo, first_todo = list(groups), list(groups)
     for i in range(n + 1):
         if i < n:
-            x3[i] = three(column(xf, i, c, n).astype(BF16), False)
-            wide = column(ef, i, c, n)
-            e[i] = wide.astype(BF16)
-            es[i] = (metric * wide).astype(BF16)
+            x3[i] = three(x[i], False)
+            es[i] = (metric * e[i].astype(F32)).astype(BF16)
             products(i, w1_ref, w2a_ref, x3[i], three(e[i], True), three(es[i], True), y, z)
         k = i - 1
         if 0 < k < n - 1:
@@ -285,7 +272,7 @@
 
 
 def field_kernel(
-    d_in, s_in, delta, delta_scaled, near_delta, near_delta_scaled, w1a_ref, out_ref, zm, zs, *, start
+    e_ref, d_in, s_in, delta, delta_scaled, near_delta, near_delta_scaled, w1a_ref, out_ref, zm, zs, *, start
 ):
     c, n = d_in.shape[1], d_in.shape[0]
     count = out_ref.shape[0]
@@ -303,22 +290,18 @@
             zm[place] = dot(w1a_ref[c : 2 * c, :], three(plain[k], True))
         zs[place] = dot(sides, three(scaled[k], True))
         if place >= 2:
-            out_ref[place - 2] = zm[place - 1] + (zs[place, 0:c, :] + zs[place - 2, c:, :])
+            grad = zm[place - 1] + (zs[place, 0:c, :] + zs[place - 2, c:, :])
+            out_ref[place - 2] = (e_ref[i - 1].astype(F32) + grad).astype(BF16)
 
 
 def assemble_kernel(*refs):
-    e_ref, parts, out_ref, ef = refs[0], refs[1:-2], refs[-2], refs[-1]
+    parts, out_ref = refs[:-1], refs[-1]
     c, n, lat = out_ref.shape
-    i = 0
-    for part in parts:
-        for k in range(part.shape[0]):
-            grad = part[k]
-            for t, at in strided(ef, i, c, n):
-                ef[at, :] = e_ref[at, :] + grad[:, t * 128 : (t + 1) * 128]
-            i += 1
-    for k in range(lat // 128):
-        part = ef[k * c * n : (k + 1) * c * n, :].reshape(c, n, 128)
-        out_ref[:, :, k * 128 : (k + 1) * 128] = part.astype(BF16)
+    turn = turning(n, back=True)
+    for b in range(0, c, 16):
+        rows = [part[k, b : b + 16, :] for part in parts for k in range(part.shape[0])]
+        turned = dot(turn, jnp.concatenate(rows, axis=0))
+        out_ref[b : b + 16] = turned.astype(BF16).reshape(16, n, lat)
 
 
 def final_kernel(mine_ref, theirs_ref, out1_ref, out2_ref):
@@ -367,25 +350,21 @@
 def one_sample(x, e, kernel_first, kernel_second, metric):
     c, n, lat = x.shape
     wide = 3 * c
-    chunks = 1
     count = lax.axis_size("dp") * lax.axis_size("lon")
     lon = lax.axis_size("lon")
     mates = [(i, i ^ 1) for i in range(count)]
     outers = [
         (i, i // lon * lon + (i % lon + (1 if i % lon % 2 else -1)) % lon) for i in range(count)
     ]
-    strided_form = ((c * n * lat // 128, 128), F32)
+    turned_form = ((n, c, lat), BF16)
     column = (wide, lat)
     halo = ((2, 2, c, lat), BF16)
     square = (wide, wide)
-    inputs = (x, e, metric, kernel_first, kernel_second)
-    xf, ef, to_mate, to_outer, row, w1, w1a, w2a = call(
+    inputs = (x, e, metric)
+    x_here, e_here, to_mate, to_outer, row = call(
         pack_kernel,
-        [strided_form] * 2 + [halo] * 2 + [((1, lat), F32)] + [(square, BF16)] * 3,
-        [((c, n, lat), BF16)] * 2
-        + [((lat,), F32)]
-        + [((3, 3, c, c), BF16)] * 2
-        + [pltpu.SemaphoreType.DMA((2, chunks)), pltpu.SemaphoreType.DMA((3,))],
+        [((c, n, lat), BF16)] * 2 + [halo] * 2 + [((1, lat), F32)],
+        [((4, c, lat), BF16), ((lat,), F32), pltpu.SemaphoreType.DMA((3,))],
         *(pltpu.with_memory_space_constraint(a, pltpu.HBM) for a in inputs),
         specs=[pl.BlockSpec(memory_space=pltpu.HBM)] * len(inputs),
     )
@@ -395,18 +374,19 @@
     pair = ((2, c, lat), F32)
     two = ((2, c, lat), BF16)
     two_wide = ((2,) + column, BF16)
-    g1, g2, d, s, fields, upstream, upstream_scaled, u, grad, y, z = call(
+    et, w1, w1a, w2a, g1, g2, d, s, fields, upstream, upstream_scaled, u, grad, y, z = call(
         interior_kernel,
-        [(square, F32)] * 2
-        + [((n, c, lat), BF16)] * 2
+        [turned_form]
+        + [(square, BF16)] * 3
+        + [(square, F32)] * 2
+        + [turned_form] * 2
         + [((4,) + column, BF16)]
         + [two] * 2
         + [pair] * 4,
-        [((n,) + column, BF16)]
-        + [((n, c, lat), BF16)] * 2
+        [turned_form, ((n,) + column, BF16), turned_form]
         + [wide_columns] * 2
         + [((n,) + column, BF16)],
-        xf, ef, w1, w2a, row,
+        x_here, e_here, kernel_first, kernel_second, row,
     )
     packed = (3 * wide // 2, 2 * c)
     common = (from_outer, from_mate, row, w1, w2a, g1, g2, fields, upstream, upstream_scaled)
@@ -424,15 +404,14 @@
     def part(done, gate, start, count):
         return call(
             functools.partial(field_kernel, start=start),
-            [((count, c, lat), F32)],
+            [((count, c, lat), BF16)],
             [((count + 2, c, lat), F32), ((count + 2, 2 * c, lat), F32)],
-            d, s, delta, delta_scaled, done[0][1], done[0][2], gate(w1a),
+            et, d, s, delta, delta_scaled, done[0][1], done[0][2], gate(w1a),
         )
 
     def assemble(done, gate):
         return call(
-            assemble_kernel, [((c, n, lat), BF16)], [strided_form],
-            ef, done[1][0], gate(done[2][0]),
+            assemble_kernel, [((c, n, lat), BF16)], [], done[1][0], gate(done[2][0])
         )
 
     half = n // 2

time: 34.2 us -> 34 us (level)
  Pallas kernels: 12.7 us -> 11.6 us
  waiting for transfers between devices: 9.9 us -> 10.8 us
    pallas_call x8, Pallas kernels: 12.7 us -> 11.6 us  [call(): pl.pallas_call(kernel, out_shape=[jax.ShapeDtypeStruct(s, d) for s, d in...]
    ppermute x8, waiting for transfers between devices: 9.9 us -> 10.8 us  [exchange(): return lax.ppermute(value, ('dp', 'lon'), pairs)]
  transfers between devices with their start and end apart: 8 -> 8, of which waited for: 6 -> 7; matrix products, arithmetic and copies ran while one was open for 0% -> 0% of each run, Pallas kernels for 26% -> 24%
where the time goes in v6:
time: 34 us; the launch traced here: 33.8 us
  Pallas kernels  11.6 us (34%)
  waiting for transfers between devices  10.8 us (32%)
  starting transfers between devices  10.6 us (31%)
  between operations  0.73 us (2%)
    pallas_call x8, Pallas kernels, call(): pl.pallas_call(kernel, out_shape=[jax.ShapeDtypeStruct(s, d) for s, d in...  11.6 us
    ppermute x8, waiting for transfers between devices, exchange(): return lax.ppermute(value, ('dp', 'lon'), pairs)  10.8 us
    ppermute x8, starting transfers between devices, exchange(): return lax.ppermute(value, ('dp', 'lon'), pairs)  10.6 us
  transfers between devices with their start and end apart: 8, of which 7 were waited for; matrix products, arithmetic and copies ran while one was open for 0% of the time, Pallas kernels for 24%

profile of v6, /device:TPU:0, one launch (start us, length us, event | category | flops | bytes accessed | tf_op | source)
XLA Modules:
  0.0 33.8 jit_solution(2929959674172233263)
XLA Ops:
  0.6 0.0 copy-start
  0.6 0.0 copy-start.1
  0.7 1.7 %shard_map.76 = (bf16[64,16,384]{2,1,0:T(8,128)(2,1)S(1)}, bf16[64,16,384]{2,1,0:T(8,128)(2,1)S(1)}, bf16[2,2,64,384]{3,2,1,0:T(8,128)(2,1)S(1)}, bf16[2,2,64,384]{3,2,1,0:T(8,128)(2,1)S(1)}, f32[1,384]{1,0:T(1,128)S(1)}) custom-call(bf16[64,16,384]{2,1,0:T(8,128)(2,1)} %bitcast.3, bf16[64,16,384]{2,1,0:T(8,128)(2,1)} %bitcast.4, f32[384]{0:T(512)} %m_hbm.1), custom_call_target="tpu_custom_call" | custom-call | tf_op jit(solution)/shard_map/pallas_call | solution.py:336
  2.4 4.6 %collective-permute-start = (bf16[2,2,64,384]{3,2,1,0:T(8,128)(2,1)S(1)}, bf16[2,2,64,384]{3,2,1,0:T(8,128)(2,1)S(1)}, u32[]{:S(2)}, u32[]{:S(2)}) collective-permute-start(bf16[2,2,64,384]{3,2,1,0:T(8,128)(2,1)S(1)} %get-tuple-element.46), channel_id=1, source_target_pairs={{0,7},{1,2},{2,1},{3,4},{4,3},{5,6},{6,5},{7,0},{8,15},{9,10},{10,... | collective-permute-start | bytes 589832 | tf_op jit(solution)/shard_map/ppermute | solution.py:347
  6.9 0.0 collective-permute-start.1
  7.0 0.0 copy-done
  7.0 0.0 copy-done.1
  7.0 4.4 %shard_map.77 = (bf16[16,64,384]{2,1,0:T(8,128)(2,1)S(1)}, bf16[192,192]{1,0:T(8,128)(2,1)S(1)}, bf16[192,192]{1,0:T(8,128)(2,1)S(1)}, bf16[192,192]{1,0:T(8,128...) custom-call(bf16[64,16,384]{2,1,0:T(8,128)(2,1)S(1)} %get-tuple-elem, ...), custom_call_target="tpu_custom_call" | custom-call | tf_op jit(solution)/shard_map/pallas_call | solution.py:336
  11.4 0.2 collective-permute-done.from_outer
  11.6 0.0 collective-permute-done.1.from_mate
  11.6 0.9 %shard_map.78 = (bf16[288,128]{1,0:T(8,128)(2,1)S(1)}, bf16[2,192,384]{2,1,0:T(8,128)(2,1)S(1)}, bf16[2,64,384]{2,1,0:T(8,128)(2,1)S(1)}, bf16[2,64,384]{2,1,0:T...) custom-call(bf16[2,2,64,384]{3,2,1,0:T(8,128)(2,1)S(1)} %collective-permute-done.from_outer, ...), custom_call_target="tpu_custom_call" | custom-call | tf_op jit(solution)/shard_map/pallas_call | solution.py:336
  12.5 0.4 %collective-permute-start.2 = (bf16[288,128]{1,0:T(8,128)(2,1)S(1)}, bf16[288,128]{1,0:T(8,128)(2,1)S(1)}, u32[]{:S(2)}, u32[]{:S(2)}) collective-permute-start(bf16[288,128]{1,0:T(8,128)(2,1)S(1)} %get-tuple-element.60), channel_id=1, source_target_pairs={{0,1},{1,0},{2,3},{3,2},{4,5},{5,4},{6,7},{7,6},{8,9},{9,8},{10,11... | collective-permute-start | bytes 221192 | tf_op jit(solution)/shard_map/ppermute | solution.py:347
  12.9 0.7 %shard_map.79 = (f32[288,128]{1,0:T(8,128)S(1)}, bf16[2,64,384]{2,1,0:T(8,128)(2,1)S(1)}, bf16[2,64,384]{2,1,0:T(8,128)(2,1)S(1)}) custom-call(bf16[2,2,64,384]{3,2,1,0:T(8,128)(2,1)S(1)} %collective-permute-done.from_outer, bf16[2,2,64,384]{3,2,1,0:T(8,128)(2,1)S(1)} %collective-permute-done.1.from_mate, f32[1,384]{1,0:T(1,128)S(1)} %get-tuple-element.48.m_ref, ...), custom_call_target="tpu_custom_call" | custom-call | tf_op jit(solution)/shard_map/pallas_call | solution.py:336
  13.6 0.2 collective-permute-done.2
  13.9 2.4 %collective-permute-start.3 = (bf16[288,128]{1,0:T(8,128)(2,1)S(1)}, bf16[288,128]{1,0:T(8,128)(2,1)S(1)}, u32[]{:S(2)}, u32[]{:S(2)}) collective-permute-start(bf16[288,128]{1,0:T(8,128)(2,1)S(1)} %add_convert_fusion.3), channel_id=1, source_target_pairs={{0,9},{1,4},{2,7},{3,10},{4,1},{5,12},{6,15},{7,2},{8,13},{9,0},{1... | collective-permute-start | bytes 221192 | tf_op jit(solution)/shard_map/ppermute | solution.py:347
  16.2 0.8 %shard_map.80.refs_0_ = bf16[8,64,384]{2,1,0:T(8,128)(2,1)S(1)} custom-call(bf16[16,64,384]{2,1,0:T(8,128)(2,1)S(1)} %get-tuple-element.72.e_ref, bf16[16,64,384]{2,1,0:T(8,128)(2,1)S(1)} %get-tuple-element.73.d_in, bf16[16,64,384]{2,1,0:T(8,128)(2,1)S(1)} %get-tuple-element.74.s_in, bf16[2,64,384]{2,1,0:T(8,128)(2,1)S(1)} %get-tuple-element.65.delta, ...), custom_call_target="tpu_custom_call" | custom-call | tf_op jit(solution)/shard_map/pallas_call | solution.py:336
  17.1 1.2 %collective-permute-done.3 = bf16[288,128]{1,0:T(8,128)(2,1)S(1)} collective-permute-done((bf16[288,128]{1,0:T(8,128)(2,1)S(1)}, bf16[288,128]{1,0:T(8,128)(2,1)S(1)}, u32[]{:S(2)}, u32[]{:S(2)}) %collective-permute-start.3) | collective-permute-done | bytes 73760 | tf_op jit(solution)/shard_map/ppermute | solution.py:347
  18.3 1.7 %collective-permute-start.4 = (bf16[288,128]{1,0:T(8,128)(2,1)S(1)}, bf16[288,128]{1,0:T(8,128)(2,1)S(1)}, u32[]{:S(2)}, u32[]{:S(2)}) collective-permute-start(bf16[288,128]{1,0:T(8,128)(2,1)S(1)} %add_convert_fusion.2), channel_id=1, source_target_pairs={{0,5},{1,8},{2,11},{3,6},{4,13},{5,0},{6,3},{7,14},{8,1},{9,12},{1... | collective-permute-start | bytes 221192 | tf_op jit(solution)/shard_map/ppermute | solution.py:347
  20.0 0.8 %shard_map.81.refs_1_ = bf16[8,64,384]{2,1,0:T(8,128)(2,1)S(1)} custom-call(bf16[16,64,384]{2,1,0:T(8,128)(2,1)S(1)} %get-tuple-element.72.e_ref, bf16[16,64,384]{2,1,0:T(8,128)(2,1)S(1)} %get-tuple-element.73.d_in, bf16[16,64,384]{2,1,0:T(8,128)(2,1)S(1)} %get-tuple-element.74.s_in, bf16[2,64,384]{2,1,0:T(8,128)(2,1)S(1)} %get-tuple-element.65.delta, ...), custom_call_target="tpu_custom_call" | custom-call | tf_op jit(solution)/shard_map/pallas_call | solution.py:336
  20.8 3.0 %collective-permute-done.4 = bf16[288,128]{1,0:T(8,128)(2,1)S(1)} collective-permute-done((bf16[288,128]{1,0:T(8,128)(2,1)S(1)}, bf16[288,128]{1,0:T(8,128)(2,1)S(1)}, u32[]{:S(2)}, u32[]{:S(2)}) %collective-permute-start.4) | collective-permute-done | bytes 73760 | tf_op jit(solution)/shard_map/ppermute | solution.py:347
  23.9 1.3 %collective-permute-start.5 = (bf16[288,128]{1,0:T(8,128)(2,1)S(1)}, bf16[288,128]{1,0:T(8,128)(2,1)S(1)}, u32[]{:S(2)}, u32[]{:S(2)}) collective-permute-start(bf16[288,128]{1,0:T(8,128)(2,1)S(1)} %add_convert_fusion.1), channel_id=1, source_target_pairs={{0,17},{1,2},{2,1},{3,18},{4,7},{5,20},{6,23},{7,4},{8,11},{9,24},... | collective-permute-start | bytes 221192 | tf_op jit(solution)/shard_map/ppermute | solution.py:347
  25.2 1.3 %shard_map.82 = bf16[64,16,384]{2,1,0:T(8,128)(2,1)} custom-call(bf16[8,64,384]{2,1,0:T(8,128)(2,1)S(1)} %shard_map.80.refs_0_, bf16[8,64,384]{2,1,0:T(8,128)(2,1)S(1)} %shard_map.81.refs_1_), custom_call_target="tpu_custom_call" | custom-call | tf_op jit(solution)/shard_map/pallas_call | solution.py:336
  26.5 1.2 %collective-permute-done.5 = bf16[288,128]{1,0:T(8,128)(2,1)S(1)} collective-permute-done((bf16[288,128]{1,0:T(8,128)(2,1)S(1)}, bf16[288,128]{1,0:T(8,128)(2,1)S(1)}, u32[]{:S(2)}, u32[]{:S(2)}) %collective-permute-start.5) | collective-permute-done | bytes 73760 | tf_op jit(solution)/shard_map/ppermute | solution.py:347
  27.7 0.1 collective-permute-start.6
  27.8 3.8 %collective-permute-done.6 = bf16[288,128]{1,0:T(8,128)(2,1)S(1)} collective-permute-done((bf16[288,128]{1,0:T(8,128)(2,1)S(1)}, bf16[288,128]{1,0:T(8,128)(2,1)S(1)}, u32[]{:S(2)}, u32[]{:S(2)}) %collective-permute-start.6) | collective-permute-done | bytes 73760 | tf_op jit(solution)/shard_map/ppermute | solution.py:347
  31.6 0.2 collective-permute-start.7
  31.8 1.2 %collective-permute-done.7.theirs_ref = bf16[288,128]{1,0:T(8,128)(2,1)S(1)} collective-permute-done((bf16[288,128]{1,0:T(8,128)(2,1)S(1)}, bf16[288,128]{1,0:T(8,128)(2,1)S(1)}, u32[]{:S(2)}, u32[]{:S(2)}) %collective-permute-start.7) | collective-permute-done | bytes 73760 | tf_op jit(solution)/shard_map/ppermute | solution.py:347
  32.9 0.9 %shard_map.83 = (bf16[3,3,64,64]{3,2,1,0:T(8,128)(2,1)}, bf16[3,3,64,64]{3,2,1,0:T(8,128)(2,1)}) custom-call(bf16[288,128]{1,0:T(8,128)(2,1)S(1)} %multiply_convert_fusion.mine_ref, bf16[288,128]{1,0:T(8,128)(2,1)S(1)} %collective-permute-done.7.theirs_ref), custom_call_target="tpu_custom_call" | custom-call | tf_op jit(solution)/shard_map/pallas_call | solution.py:336
  (5 shorter events, 0.1 us)
Async XLA Ops:
  0.6 6.3 %copy-start = (bf16[3,3,64,64]{3,2,1,0:T(8,128)(2,1)S(1)}, bf16[3,3,64,64]{3,2,1,0:T(8,128)(2,1)}, u32[]{:S(2)}) copy-start(bf16[3,3,64,64]{3,2,1,0:T(8,128)(2,1)} %k1_ref.1) | copy-start | bytes 221188
  0.6 6.3 %copy-start.1 = (bf16[3,3,64,64]{3,2,1,0:T(8,128)(2,1)S(1)}, bf16[3,3,64,64]{3,2,1,0:T(8,128)(2,1)}, u32[]{:S(2)}) copy-start(bf16[3,3,64,64]{3,2,1,0:T(8,128)(2,1)} %k2_ref.1) | copy-start | bytes 221188
  2.4 9.2 %collective-permute-start = (bf16[2,2,64,384]{3,2,1,0:T(8,128)(2,1)S(1)}, bf16[2,2,64,384]{3,2,1,0:T(8,128)(2,1)S(1)}, u32[]{:S(2)}, u32[]{:S(2)}) collective-permute-start(bf16[2,2,64,384]{3,2,1,0:T(8,128)(2,1)S(1)} %get-tuple-element.46), channel_id=1, source_target_pairs={{0,7},{1,2},{2,1},{3,4},{4,3},{5,6},{6,5},{7,0},{8,15},{9,10},{10,... | collective-permute-start | bytes 589832 | tf_op jit(solution)/shard_map/ppermute | solution.py:347
  6.9 4.6 %collective-permute-start.1 = (bf16[2,2,64,384]{3,2,1,0:T(8,128)(2,1)S(1)}, bf16[2,2,64,384]{3,2,1,0:T(8,128)(2,1)S(1)}, u32[]{:S(2)}, u32[]{:S(2)}) collective-permute-start(bf16[2,2,64,384]{3,2,1,0:T(8,128)(2,1)S(1)} %get-tuple-element.47), channel_id=1, source_target_pairs={{0,1},{1,0},{2,3},{3,2},{4,5},{5,4},{6,7},{7,6},{8,9},{9,8},{10,11... | collective-permute-start | bytes 589832 | tf_op jit(solution)/shard_map/ppermute | solution.py:347
  12.5 1.3 %collective-permute-start.2 = (bf16[288,128]{1,0:T(8,128)(2,1)S(1)}, bf16[288,128]{1,0:T(8,128)(2,1)S(1)}, u32[]{:S(2)}, u32[]{:S(2)}) collective-permute-start(bf16[288,128]{1,0:T(8,128)(2,1)S(1)} %get-tuple-element.60), channel_id=1, source_target_pairs={{0,1},{1,0},{2,3},{3,2},{4,5},{5,4},{6,7},{7,6},{8,9},{9,8},{10,11... | collective-permute-start | bytes 221192 | tf_op jit(solution)/shard_map/ppermute | solution.py:347
  13.9 4.4 %collective-permute-start.3 = (bf16[288,128]{1,0:T(8,128)(2,1)S(1)}, bf16[288,128]{1,0:T(8,128)(2,1)S(1)}, u32[]{:S(2)}, u32[]{:S(2)}) collective-permute-start(bf16[288,128]{1,0:T(8,128)(2,1)S(1)} %add_convert_fusion.3), channel_id=1, source_target_pairs={{0,9},{1,4},{2,7},{3,10},{4,1},{5,12},{6,15},{7,2},{8,13},{9,0},{1... | collective-permute-start | bytes 221192 | tf_op jit(solution)/shard_map/ppermute | solution.py:347
  18.3 5.5 %collective-permute-start.4 = (bf16[288,128]{1,0:T(8,128)(2,1)S(1)}, bf16[288,128]{1,0:T(8,128)(2,1)S(1)}, u32[]{:S(2)}, u32[]{:S(2)}) collective-permute-start(bf16[288,128]{1,0:T(8,128)(2,1)S(1)} %add_convert_fusion.2), channel_id=1, source_target_pairs={{0,5},{1,8},{2,11},{3,6},{4,13},{5,0},{6,3},{7,14},{8,1},{9,12},{1... | collective-permute-start | bytes 221192 | tf_op jit(solution)/shard_map/ppermute | solution.py:347
  23.9 3.8 %collective-permute-start.5 = (bf16[288,128]{1,0:T(8,128)(2,1)S(1)}, bf16[288,128]{1,0:T(8,128)(2,1)S(1)}, u32[]{:S(2)}, u32[]{:S(2)}) collective-permute-start(bf16[288,128]{1,0:T(8,128)(2,1)S(1)} %add_convert_fusion.1), channel_id=1, source_target_pairs={{0,17},{1,2},{2,1},{3,18},{4,7},{5,20},{6,23},{7,4},{8,11},{9,24},... | collective-permute-start | bytes 221192 | tf_op jit(solution)/shard_map/ppermute | solution.py:347
  27.7 3.8 %collective-permute-start.6 = (bf16[288,128]{1,0:T(8,128)(2,1)S(1)}, bf16[288,128]{1,0:T(8,128)(2,1)S(1)}, u32[]{:S(2)}, u32[]{:S(2)}) collective-permute-start(bf16[288,128]{1,0:T(8,128)(2,1)S(1)} %add_convert_fusion), channel_id=1, source_target_pairs={{0,3},{1,16},{2,19},{3,0},{4,21},{5,6},{6,5},{7,22},{8,25},{9,10},... | collective-permute-start | bytes 221192 | tf_op jit(solution)/shard_map/ppermute | solution.py:347
  31.6 1.3 %collective-permute-start.7 = (bf16[288,128]{1,0:T(8,128)(2,1)S(1)}, bf16[288,128]{1,0:T(8,128)(2,1)S(1)}, u32[]{:S(2)}, u32[]{:S(2)}) collective-permute-start(bf16[288,128]{1,0:T(8,128)(2,1)S(1)} %multiply_convert_fusion.mine_ref), channel_id=1, source_target_pairs={{0,1},{1,0},{2,3},{3,2},{4,5},{5,4},{6,7},{7,6},{8,9},{9,8},{10,11... | collective-permute-start | bytes 221192 | tf_op jit(solution)/shard_map/ppermute | solution.py:347

commit v7 on v6

--- a/solution.py
+++ b/solution.py
@@ -441,15 +441,7 @@
     total = done[0][0] + got.astype(F32)
     along_lon = [1 << k for k in range(1, lon.bit_length() - 1)]
     along_dp = [lon << k for k in range(dp.bit_length() - 1)]
-    bits = []
-    while along_lon or along_dp:
-        if along_dp:
-            bits.append(along_dp.pop(0))
-        if along_lon:
-            bits.append(along_lon.pop())
-    other = list(bits)
-    for k in range(0, len(bits) - 1, 2):
-        other[k], other[k + 1] = bits[k + 1], bits[k]
+    bits, other = along_lon + along_dp, along_dp + along_lon
     for even_bit, odd_bit in zip(bits, other):
         sent = total.astype(BF16)
         got = beside(

time: 34 us -> 33.7 us (level)
  waiting for transfers between devices: 10.8 us -> 8.49 us
  starting transfers between devices: 10.6 us -> 12.6 us
    ppermute x8, waiting for transfers between devices: 10.8 us -> 8.49 us  [exchange(): return lax.ppermute(value, ('dp', 'lon'), pairs)]
    ppermute x8, starting transfers between devices: 10.6 us -> 12.6 us  [exchange(): return lax.ppermute(value, ('dp', 'lon'), pairs)]
where the time goes in v7:
time: 33.7 us; the launch traced here: 33.6 us
  starting transfers between devices  12.6 us (37%)
  Pallas kernels  11.6 us (34%)
  waiting for transfers between devices  8.49 us (25%)
  between operations  0.72 us (2%)
    ppermute x8, starting transfers between devices, exchange(): return lax.ppermute(value, ('dp', 'lon'), pairs)  12.6 us
    pallas_call x8, Pallas kernels, call(): pl.pallas_call(kernel, out_shape=[jax.ShapeDtypeStruct(s, d) for s, d in...  11.6 us
    ppermute x8, waiting for transfers between devices, exchange(): return lax.ppermute(value, ('dp', 'lon'), pairs)  8.49 us
  transfers between devices with their start and end apart: 8, of which 7 were waited for; matrix products, arithmetic and copies ran while one was open for 0% of the time, Pallas kernels for 24%

profile of v7, /device:TPU:0, one launch (start us, length us, event | category | flops | bytes accessed | tf_op | source)
XLA Modules:
  0.0 33.6 jit_solution(15107420856828285826)
XLA Ops:
  0.6 0.0 copy-start
  0.6 0.0 copy-start.1
  0.7 1.7 %shard_map.76 = (bf16[64,16,384]{2,1,0:T(8,128)(2,1)S(1)}, bf16[64,16,384]{2,1,0:T(8,128)(2,1)S(1)}, bf16[2,2,64,384]{3,2,1,0:T(8,128)(2,1)S(1)}, bf16[2,2,64,384]{3,2,1,0:T(8,128)(2,1)S(1)}, f32[1,384]{1,0:T(1,128)S(1)}) custom-call(bf16[64,16,384]{2,1,0:T(8,128)(2,1)} %bitcast.3, bf16[64,16,384]{2,1,0:T(8,128)(2,1)} %bitcast.4, f32[384]{0:T(512)} %m_hbm.1), custom_call_target="tpu_custom_call" | custom-call | tf_op jit(solution)/shard_map/pallas_call | solution.py:336
  2.4 4.6 %collective-permute-start = (bf16[2,2,64,384]{3,2,1,0:T(8,128)(2,1)S(1)}, bf16[2,2,64,384]{3,2,1,0:T(8,128)(2,1)S(1)}, u32[]{:S(2)}, u32[]{:S(2)}) collective-permute-start(bf16[2,2,64,384]{3,2,1,0:T(8,128)(2,1)S(1)} %get-tuple-element.46), channel_id=1, source_target_pairs={{0,7},{1,2},{2,1},{3,4},{4,3},{5,6},{6,5},{7,0},{8,15},{9,10},{10,... | collective-permute-start | bytes 589832 | tf_op jit(solution)/shard_map/ppermute | solution.py:347
  6.9 0.0 collective-permute-start.1
  7.0 0.0 copy-done
  7.0 0.0 copy-done.1
  7.0 4.4 %shard_map.77 = (bf16[16,64,384]{2,1,0:T(8,128)(2,1)S(1)}, bf16[192,192]{1,0:T(8,128)(2,1)S(1)}, bf16[192,192]{1,0:T(8,128)(2,1)S(1)}, bf16[192,192]{1,0:T(8,128...) custom-call(bf16[64,16,384]{2,1,0:T(8,128)(2,1)S(1)} %get-tuple-elem, ...), custom_call_target="tpu_custom_call" | custom-call | tf_op jit(solution)/shard_map/pallas_call | solution.py:336
  11.4 0.2 collective-permute-done.from_outer
  11.6 0.0 collective-permute-done.1.from_mate
  11.6 0.9 %shard_map.78 = (bf16[288,128]{1,0:T(8,128)(2,1)S(1)}, bf16[2,192,384]{2,1,0:T(8,128)(2,1)S(1)}, bf16[2,64,384]{2,1,0:T(8,128)(2,1)S(1)}, bf16[2,64,384]{2,1,0:T...) custom-call(bf16[2,2,64,384]{3,2,1,0:T(8,128)(2,1)S(1)} %collective-permute-done.from_outer, ...), custom_call_target="tpu_custom_call" | custom-call | tf_op jit(solution)/shard_map/pallas_call | solution.py:336
  12.5 0.4 %collective-permute-start.2 = (bf16[288,128]{1,0:T(8,128)(2,1)S(1)}, bf16[288,128]{1,0:T(8,128)(2,1)S(1)}, u32[]{:S(2)}, u32[]{:S(2)}) collective-permute-start(bf16[288,128]{1,0:T(8,128)(2,1)S(1)} %get-tuple-element.60), channel_id=1, source_target_pairs={{0,1},{1,0},{2,3},{3,2},{4,5},{5,4},{6,7},{7,6},{8,9},{9,8},{10,11... | collective-permute-start | bytes 221192 | tf_op jit(solution)/shard_map/ppermute | solution.py:347
  12.9 0.7 %shard_map.79 = (f32[288,128]{1,0:T(8,128)S(1)}, bf16[2,64,384]{2,1,0:T(8,128)(2,1)S(1)}, bf16[2,64,384]{2,1,0:T(8,128)(2,1)S(1)}) custom-call(bf16[2,2,64,384]{3,2,1,0:T(8,128)(2,1)S(1)} %collective-permute-done.from_outer, bf16[2,2,64,384]{3,2,1,0:T(8,128)(2,1)S(1)} %collective-permute-done.1.from_mate, f32[1,384]{1,0:T(1,128)S(1)} %get-tuple-element.48.m_ref, ...), custom_call_target="tpu_custom_call" | custom-call | tf_op jit(solution)/shard_map/pallas_call | solution.py:336
  13.6 0.2 collective-permute-done.2
  13.9 0.7 %collective-permute-start.3 = (bf16[288,128]{1,0:T(8,128)(2,1)S(1)}, bf16[288,128]{1,0:T(8,128)(2,1)S(1)}, u32[]{:S(2)}, u32[]{:S(2)}) collective-permute-start(bf16[288,128]{1,0:T(8,128)(2,1)S(1)} %add_convert_fusion.3), channel_id=1, source_target_pairs={{0,3},{1,8},{2,11},{3,0},{4,13},{5,6},{6,5},{7,14},{8,1},{9,10},{1... | collective-permute-start | bytes 221192 | tf_op jit(solution)/shard_map/ppermute | solution.py:347
  14.6 0.8 %shard_map.80.refs_0_ = bf16[8,64,384]{2,1,0:T(8,128)(2,1)S(1)} custom-call(bf16[16,64,384]{2,1,0:T(8,128)(2,1)S(1)} %get-tuple-element.72.e_ref, bf16[16,64,384]{2,1,0:T(8,128)(2,1)S(1)} %get-tuple-element.73.d_in, bf16[16,64,384]{2,1,0:T(8,128)(2,1)S(1)} %get-tuple-element.74.s_in, bf16[2,64,384]{2,1,0:T(8,128)(2,1)S(1)} %get-tuple-element.65.delta, ...), custom_call_target="tpu_custom_call" | custom-call | tf_op jit(solution)/shard_map/pallas_call | solution.py:336
  15.4 2.3 %collective-permute-done.3 = bf16[288,128]{1,0:T(8,128)(2,1)S(1)} collective-permute-done((bf16[288,128]{1,0:T(8,128)(2,1)S(1)}, bf16[288,128]{1,0:T(8,128)(2,1)S(1)}, u32[]{:S(2)}, u32[]{:S(2)}) %collective-permute-start.3) | collective-permute-done | bytes 73760 | tf_op jit(solution)/shard_map/ppermute | solution.py:347
  17.7 1.9 %collective-permute-start.4 = (bf16[288,128]{1,0:T(8,128)(2,1)S(1)}, bf16[288,128]{1,0:T(8,128)(2,1)S(1)}, u32[]{:S(2)}, u32[]{:S(2)}) collective-permute-start(bf16[288,128]{1,0:T(8,128)(2,1)S(1)} %add_convert_fusion.2), channel_id=1, source_target_pairs={{0,5},{1,16},{2,19},{3,6},{4,21},{5,0},{6,3},{7,22},{8,25},{9,12},... | collective-permute-start | bytes 221192 | tf_op jit(solution)/shard_map/ppermute | solution.py:347
  19.7 0.8 %shard_map.81.refs_1_ = bf16[8,64,384]{2,1,0:T(8,128)(2,1)S(1)} custom-call(bf16[16,64,384]{2,1,0:T(8,128)(2,1)S(1)} %get-tuple-element.72.e_ref, bf16[16,64,384]{2,1,0:T(8,128)(2,1)S(1)} %get-tuple-element.73.d_in, bf16[16,64,384]{2,1,0:T(8,128)(2,1)S(1)} %get-tuple-element.74.s_in, bf16[2,64,384]{2,1,0:T(8,128)(2,1)S(1)} %get-tuple-element.65.delta, ...), custom_call_target="tpu_custom_call" | custom-call | tf_op jit(solution)/shard_map/pallas_call | solution.py:336
  20.5 2.0 %collective-permute-done.4 = bf16[288,128]{1,0:T(8,128)(2,1)S(1)} collective-permute-done((bf16[288,128]{1,0:T(8,128)(2,1)S(1)}, bf16[288,128]{1,0:T(8,128)(2,1)S(1)}, u32[]{:S(2)}, u32[]{:S(2)}) %collective-permute-start.4) | collective-permute-done | bytes 73760 | tf_op jit(solution)/shard_map/ppermute | solution.py:347
  22.5 2.4 %collective-permute-start.5 = (bf16[288,128]{1,0:T(8,128)(2,1)S(1)}, bf16[288,128]{1,0:T(8,128)(2,1)S(1)}, u32[]{:S(2)}, u32[]{:S(2)}) collective-permute-start(bf16[288,128]{1,0:T(8,128)(2,1)S(1)} %add_convert_fusion.1), channel_id=1, source_target_pairs={{0,9},{1,2},{2,1},{3,10},{4,7},{5,12},{6,15},{7,4},{8,11},{9,0},{1... | collective-permute-start | bytes 221192 | tf_op jit(solution)/shard_map/ppermute | solution.py:347
  24.9 1.3 %shard_map.82 = bf16[64,16,384]{2,1,0:T(8,128)(2,1)} custom-call(bf16[8,64,384]{2,1,0:T(8,128)(2,1)S(1)} %shard_map.80.refs_0_, bf16[8,64,384]{2,1,0:T(8,128)(2,1)S(1)} %shard_map.81.refs_1_), custom_call_target="tpu_custom_call" | custom-call | tf_op jit(solution)/shard_map/pallas_call | solution.py:336
  26.2 0.7 %collective-permute-done.5 = bf16[288,128]{1,0:T(8,128)(2,1)S(1)} collective-permute-done((bf16[288,128]{1,0:T(8,128)(2,1)S(1)}, bf16[288,128]{1,0:T(8,128)(2,1)S(1)}, u32[]{:S(2)}, u32[]{:S(2)}) %collective-permute-start.5) | collective-permute-done | bytes 73760 | tf_op jit(solution)/shard_map/ppermute | solution.py:347
  26.9 2.3 %collective-permute-start.6 = (bf16[288,128]{1,0:T(8,128)(2,1)S(1)}, bf16[288,128]{1,0:T(8,128)(2,1)S(1)}, u32[]{:S(2)}, u32[]{:S(2)}) collective-permute-start(bf16[288,128]{1,0:T(8,128)(2,1)S(1)} %add_convert_fusion), channel_id=1, source_target_pairs={{0,17},{1,4},{2,7},{3,18},{4,1},{5,20},{6,23},{7,2},{8,13},{9,24},... | collective-permute-start | bytes 221192 | tf_op jit(solution)/shard_map/ppermute | solution.py:347
  29.3 2.0 %collective-permute-done.6 = bf16[288,128]{1,0:T(8,128)(2,1)S(1)} collective-permute-done((bf16[288,128]{1,0:T(8,128)(2,1)S(1)}, bf16[288,128]{1,0:T(8,128)(2,1)S(1)}, u32[]{:S(2)}, u32[]{:S(2)}) %collective-permute-start.6) | collective-permute-done | bytes 73760 | tf_op jit(solution)/shard_map/ppermute | solution.py:347
  31.4 0.3 collective-permute-start.7
  31.6 1.1 %collective-permute-done.7.theirs_ref = bf16[288,128]{1,0:T(8,128)(2,1)S(1)} collective-permute-done((bf16[288,128]{1,0:T(8,128)(2,1)S(1)}, bf16[288,128]{1,0:T(8,128)(2,1)S(1)}, u32[]{:S(2)}, u32[]{:S(2)}) %collective-permute-start.7) | collective-permute-done | bytes 73760 | tf_op jit(solution)/shard_map/ppermute | solution.py:347
  32.7 0.9 %shard_map.83 = (bf16[3,3,64,64]{3,2,1,0:T(8,128)(2,1)}, bf16[3,3,64,64]{3,2,1,0:T(8,128)(2,1)}) custom-call(bf16[288,128]{1,0:T(8,128)(2,1)S(1)} %multiply_convert_fusion.mine_ref, bf16[288,128]{1,0:T(8,128)(2,1)S(1)} %collective-permute-done.7.theirs_ref), custom_call_target="tpu_custom_call" | custom-call | tf_op jit(solution)/shard_map/pallas_call | solution.py:336
  (5 shorter events, 0.1 us)
Async XLA Ops:
  0.6 6.3 %copy-start = (bf16[3,3,64,64]{3,2,1,0:T(8,128)(2,1)S(1)}, bf16[3,3,64,64]{3,2,1,0:T(8,128)(2,1)}, u32[]{:S(2)}) copy-start(bf16[3,3,64,64]{3,2,1,0:T(8,128)(2,1)} %k1_ref.1) | copy-start | bytes 221188
  0.6 6.3 %copy-start.1 = (bf16[3,3,64,64]{3,2,1,0:T(8,128)(2,1)S(1)}, bf16[3,3,64,64]{3,2,1,0:T(8,128)(2,1)}, u32[]{:S(2)}) copy-start(bf16[3,3,64,64]{3,2,1,0:T(8,128)(2,1)} %k2_ref.1) | copy-start | bytes 221188
  2.4 9.2 %collective-permute-start = (bf16[2,2,64,384]{3,2,1,0:T(8,128)(2,1)S(1)}, bf16[2,2,64,384]{3,2,1,0:T(8,128)(2,1)S(1)}, u32[]{:S(2)}, u32[]{:S(2)}) collective-permute-start(bf16[2,2,64,384]{3,2,1,0:T(8,128)(2,1)S(1)} %get-tuple-element.46), channel_id=1, source_target_pairs={{0,7},{1,2},{2,1},{3,4},{4,3},{5,6},{6,5},{7,0},{8,15},{9,10},{10,... | collective-permute-start | bytes 589832 | tf_op jit(solution)/shard_map/ppermute | solution.py:347
  6.9 4.6 %collective-permute-start.1 = (bf16[2,2,64,384]{3,2,1,0:T(8,128)(2,1)S(1)}, bf16[2,2,64,384]{3,2,1,0:T(8,128)(2,1)S(1)}, u32[]{:S(2)}, u32[]{:S(2)}) collective-permute-start(bf16[2,2,64,384]{3,2,1,0:T(8,128)(2,1)S(1)} %get-tuple-element.47), channel_id=1, source_target_pairs={{0,1},{1,0},{2,3},{3,2},{4,5},{5,4},{6,7},{7,6},{8,9},{9,8},{10,11... | collective-permute-start | bytes 589832 | tf_op jit(solution)/shard_map/ppermute | solution.py:347
  12.5 1.3 %collective-permute-start.2 = (bf16[288,128]{1,0:T(8,128)(2,1)S(1)}, bf16[288,128]{1,0:T(8,128)(2,1)S(1)}, u32[]{:S(2)}, u32[]{:S(2)}) collective-permute-start(bf16[288,128]{1,0:T(8,128)(2,1)S(1)} %get-tuple-element.60), channel_id=1, source_target_pairs={{0,1},{1,0},{2,3},{3,2},{4,5},{5,4},{6,7},{7,6},{8,9},{9,8},{10,11... | collective-permute-start | bytes 221192 | tf_op jit(solution)/shard_map/ppermute | solution.py:347
  13.9 3.8 %collective-permute-start.3 = (bf16[288,128]{1,0:T(8,128)(2,1)S(1)}, bf16[288,128]{1,0:T(8,128)(2,1)S(1)}, u32[]{:S(2)}, u32[]{:S(2)}) collective-permute-start(bf16[288,128]{1,0:T(8,128)(2,1)S(1)} %add_convert_fusion.3), channel_id=1, source_target_pairs={{0,3},{1,8},{2,11},{3,0},{4,13},{5,6},{6,5},{7,14},{8,1},{9,10},{1... | collective-permute-start | bytes 221192 | tf_op jit(solution)/shard_map/ppermute | solution.py:347
  17.7 4.7 %collective-permute-start.4 = (bf16[288,128]{1,0:T(8,128)(2,1)S(1)}, bf16[288,128]{1,0:T(8,128)(2,1)S(1)}, u32[]{:S(2)}, u32[]{:S(2)}) collective-permute-start(bf16[288,128]{1,0:T(8,128)(2,1)S(1)} %add_convert_fusion.2), channel_id=1, source_target_pairs={{0,5},{1,16},{2,19},{3,6},{4,21},{5,0},{6,3},{7,22},{8,25},{9,12},... | collective-permute-start | bytes 221192 | tf_op jit(solution)/shard_map/ppermute | solution.py:347
  22.5 4.4 %collective-permute-start.5 = (bf16[288,128]{1,0:T(8,128)(2,1)S(1)}, bf16[288,128]{1,0:T(8,128)(2,1)S(1)}, u32[]{:S(2)}, u32[]{:S(2)}) collective-permute-start(bf16[288,128]{1,0:T(8,128)(2,1)S(1)} %add_convert_fusion.1), channel_id=1, source_target_pairs={{0,9},{1,2},{2,1},{3,10},{4,7},{5,12},{6,15},{7,4},{8,11},{9,0},{1... | collective-permute-start | bytes 221192 | tf_op jit(solution)/shard_map/ppermute | solution.py:347
  26.9 4.4 %collective-permute-start.6 = (bf16[288,128]{1,0:T(8,128)(2,1)S(1)}, bf16[288,128]{1,0:T(8,128)(2,1)S(1)}, u32[]{:S(2)}, u32[]{:S(2)}) collective-permute-start(bf16[288,128]{1,0:T(8,128)(2,1)S(1)} %add_convert_fusion), channel_id=1, source_target_pairs={{0,17},{1,4},{2,7},{3,18},{4,1},{5,20},{6,23},{7,2},{8,13},{9,24},... | collective-permute-start | bytes 221192 | tf_op jit(solution)/shard_map/ppermute | solution.py:347
  31.4 1.3 %collective-permute-start.7 = (bf16[288,128]{1,0:T(8,128)(2,1)S(1)}, bf16[288,128]{1,0:T(8,128)(2,1)S(1)}, u32[]{:S(2)}, u32[]{:S(2)}) collective-permute-start(bf16[288,128]{1,0:T(8,128)(2,1)S(1)} %multiply_convert_fusion.mine_ref), channel_id=1, source_target_pairs={{0,1},{1,0},{2,3},{3,2},{4,5},{5,4},{6,7},{7,6},{8,9},{9,8},{10,11... | collective-permute-start | bytes 221192 | tf_op jit(solution)/shard_map/ppermute | solution.py:347

commit v8 on v7

--- a/solution.py
+++ b/solution.py
@@ -105,13 +105,14 @@
     ref[2 * half :, :] = jnp.concatenate([tail[0:half], tail[half:]], axis=1).astype(ref.dtype)
 
 
-def turning(n, back=False, edges=False):
-    shape = (64 if edges else 16 * n, 16 * n)
+def turning(n, back=False, odd=None):
+    shape = (16 * n if odd is None else 64, 16 * n)
     row = lax.broadcasted_iota(jnp.int32, shape, 1 if back else 0)
     source = lax.broadcasted_iota(jnp.int32, shape, 0 if back else 1)
     place = lax.shift_right_logical(row, jnp.full_like(row, 4))
-    if edges:
-        place = jnp.where(place < 2, place, place + n - 4)
+    if odd is not None:
+        mate = jnp.where(odd, 0, n - 2)
+        place = jnp.where(place < 2, place + mate, place - 2 + (n - 2 - mate))
     return jnp.where(source == (row & 15) * n + place, 1.0, 0.0).astype(BF16)
 
 
@@ -120,11 +121,11 @@
     for b in range(0, c, 16):
         turned = dot(turn, source[b : b + 16].reshape(16 * n, lat)).astype(BF16)
         for i in range(turn.shape[0] // 16):
-            target[i, b : b + 16, :] = turned[16 * i : 16 * (i + 1)]
+            target(i)[b : b + 16, :] = turned[16 * i : 16 * (i + 1)]
 
 
 def pack_kernel(
-    x_hbm, e_hbm, m_hbm, x_ref, e_ref, mate_ref, outer_ref, row_ref, edges, ms, sems
+    x_hbm, e_hbm, m_hbm, x_ref, e_ref, mate_ref, outer_ref, row_ref, ms, sems
 ):
     n, lat = x_hbm.shape[1:]
     copies = [
@@ -133,14 +134,12 @@
     ]
     for copy in copies:
         copy.start()
-    turn = turning(n, edges=True)
-    odd = lax.axis_index("lon") % 2 == 1
+    turn = turning(n, odd=lax.axis_index("lon") % 2 == 1)
     for a, source in enumerate((x_ref, e_ref)):
         copies[a].wait()
-        turn_columns(turn, source, edges)
-        for k in range(2):
-            mate_ref[a, k] = jnp.where(odd, edges[k], edges[2 + k])
-            outer_ref[a, k] = jnp.where(odd, edges[2 + k], edges[k])
+        turn_columns(
+            turn, source, lambda i, a=a: mate_ref.at[a, i] if i < 2 else outer_ref.at[a, i - 2]
+        )
     copies[2].wait()
     row_ref[...] = ms[...].reshape(1, lat)
 
@@ -154,8 +153,8 @@
     low, mid, high = slice(0, c), slice(c, 2 * c), slice(2 * c, 3 * c)
     metric = m_ref[...]
     turn = turning(n)
-    turn_columns(turn, x_ref, x)
-    turn_columns(turn, e_ref, e)
+    turn_columns(turn, x_ref, lambda i: x.at[i])
+    turn_columns(turn, e_ref, lambda i: e.at[i])
     prepare(k1_ref, w1_ref, w1a_ref)
     prepare(k2_ref, None, w2a_ref)
     blank = jnp.zeros((c, lat), BF16)
@@ -364,7 +363,7 @@
     x_here, e_here, to_mate, to_outer, row = call(
         pack_kernel,
         [((c, n, lat), BF16)] * 2 + [halo] * 2 + [((1, lat), F32)],
-        [((4, c, lat), BF16), ((lat,), F32), pltpu.SemaphoreType.DMA((3,))],
+        [((lat,), F32), pltpu.SemaphoreType.DMA((3,))],
         *(pltpu.with_memory_space_constraint(a, pltpu.HBM) for a in inputs),
         specs=[pl.BlockSpec(memory_space=pltpu.HBM)] * len(inputs),
     )

time: 33.7 us -> 33.7 us (level)
  no operation moved by 1% of the time
where the time goes in v8:
time: 33.7 us; the launch traced here: 33.5 us
  starting transfers between devices  12.6 us (37%)
  Pallas kernels  11.6 us (34%)
  waiting for transfers between devices  8.51 us (25%)
  between operations  0.72 us (2%)
    ppermute x8, starting transfers between devices, exchange(): return lax.ppermute(value, ('dp', 'lon'), pairs)  12.6 us
    pallas_call x8, Pallas kernels, call(): pl.pallas_call(kernel, out_shape=[jax.ShapeDtypeStruct(s, d) for s, d in...  11.6 us
    ppermute x8, waiting for transfers between devices, exchange(): return lax.ppermute(value, ('dp', 'lon'), pairs)  8.51 us
  transfers between devices with their start and end apart: 8, of which 7 were waited for; matrix products, arithmetic and copies ran while one was open for 0% of the time, Pallas kernels for 24%

profile of v8, /device:TPU:0, one launch (start us, length us, event | category | flops | bytes accessed | tf_op | source)
XLA Modules:
  0.0 33.5 jit_solution(7207955737066824968)
XLA Ops:
  0.6 0.0 copy-start
  0.6 0.0 copy-start.1
  0.7 1.7 %shard_map.76 = (bf16[64,16,384]{2,1,0:T(8,128)(2,1)S(1)}, bf16[64,16,384]{2,1,0:T(8,128)(2,1)S(1)}, bf16[2,2,64,384]{3,2,1,0:T(8,128)(2,1)S(1)}, bf16[2,2,64,384]{3,2,1,0:T(8,128)(2,1)S(1)}, f32[1,384]{1,0:T(1,128)S(1)}) custom-call(bf16[64,16,384]{2,1,0:T(8,128)(2,1)} %bitcast.3, bf16[64,16,384]{2,1,0:T(8,128)(2,1)} %bitcast.4, f32[384]{0:T(512)} %m_hbm.1), custom_call_target="tpu_custom_call" | custom-call | tf_op jit(solution)/shard_map/pallas_call | solution.py:335
  2.4 4.6 %collective-permute-start = (bf16[2,2,64,384]{3,2,1,0:T(8,128)(2,1)S(1)}, bf16[2,2,64,384]{3,2,1,0:T(8,128)(2,1)S(1)}, u32[]{:S(2)}, u32[]{:S(2)}) collective-permute-start(bf16[2,2,64,384]{3,2,1,0:T(8,128)(2,1)S(1)} %get-tuple-element.46), channel_id=1, source_target_pairs={{0,7},{1,2},{2,1},{3,4},{4,3},{5,6},{6,5},{7,0},{8,15},{9,10},{10,... | collective-permute-start | bytes 589832 | tf_op jit(solution)/shard_map/ppermute | solution.py:346
  6.9 0.0 collective-permute-start.1
  6.9 0.0 copy-done
  6.9 0.0 copy-done.1
  6.9 4.4 %shard_map.77 = (bf16[16,64,384]{2,1,0:T(8,128)(2,1)S(1)}, bf16[192,192]{1,0:T(8,128)(2,1)S(1)}, bf16[192,192]{1,0:T(8,128)(2,1)S(1)}, bf16[192,192]{1,0:T(8,128...) custom-call(bf16[64,16,384]{2,1,0:T(8,128)(2,1)S(1)} %get-tuple-elem, ...), custom_call_target="tpu_custom_call" | custom-call | tf_op jit(solution)/shard_map/pallas_call | solution.py:335
  11.3 0.2 collective-permute-done.from_outer
  11.5 0.0 collective-permute-done.1.from_mate
  11.5 0.9 %shard_map.78 = (bf16[288,128]{1,0:T(8,128)(2,1)S(1)}, bf16[2,192,384]{2,1,0:T(8,128)(2,1)S(1)}, bf16[2,64,384]{2,1,0:T(8,128)(2,1)S(1)}, bf16[2,64,384]{2,1,0:T...) custom-call(bf16[2,2,64,384]{3,2,1,0:T(8,128)(2,1)S(1)} %collective-permute-done.from_outer, ...), custom_call_target="tpu_custom_call" | custom-call | tf_op jit(solution)/shard_map/pallas_call | solution.py:335
  12.5 0.4 %collective-permute-start.2 = (bf16[288,128]{1,0:T(8,128)(2,1)S(1)}, bf16[288,128]{1,0:T(8,128)(2,1)S(1)}, u32[]{:S(2)}, u32[]{:S(2)}) collective-permute-start(bf16[288,128]{1,0:T(8,128)(2,1)S(1)} %get-tuple-element.60), channel_id=1, source_target_pairs={{0,1},{1,0},{2,3},{3,2},{4,5},{5,4},{6,7},{7,6},{8,9},{9,8},{10,11... | collective-permute-start | bytes 221192 | tf_op jit(solution)/shard_map/ppermute | solution.py:346
  12.8 0.7 %shard_map.79 = (f32[288,128]{1,0:T(8,128)S(1)}, bf16[2,64,384]{2,1,0:T(8,128)(2,1)S(1)}, bf16[2,64,384]{2,1,0:T(8,128)(2,1)S(1)}) custom-call(bf16[2,2,64,384]{3,2,1,0:T(8,128)(2,1)S(1)} %collective-permute-done.from_outer, bf16[2,2,64,384]{3,2,1,0:T(8,128)(2,1)S(1)} %collective-permute-done.1.from_mate, f32[1,384]{1,0:T(1,128)S(1)} %get-tuple-element.48.m_ref, ...), custom_call_target="tpu_custom_call" | custom-call | tf_op jit(solution)/shard_map/pallas_call | solution.py:335
  13.6 0.2 collective-permute-done.2
  13.8 0.7 %collective-permute-start.3 = (bf16[288,128]{1,0:T(8,128)(2,1)S(1)}, bf16[288,128]{1,0:T(8,128)(2,1)S(1)}, u32[]{:S(2)}, u32[]{:S(2)}) collective-permute-start(bf16[288,128]{1,0:T(8,128)(2,1)S(1)} %add_convert_fusion.3), channel_id=1, source_target_pairs={{0,3},{1,8},{2,11},{3,0},{4,13},{5,6},{6,5},{7,14},{8,1},{9,10},{1... | collective-permute-start | bytes 221192 | tf_op jit(solution)/shard_map/ppermute | solution.py:346
  14.6 0.8 %shard_map.80.refs_0_ = bf16[8,64,384]{2,1,0:T(8,128)(2,1)S(1)} custom-call(bf16[16,64,384]{2,1,0:T(8,128)(2,1)S(1)} %get-tuple-element.72.e_ref, bf16[16,64,384]{2,1,0:T(8,128)(2,1)S(1)} %get-tuple-element.73.d_in, bf16[16,64,384]{2,1,0:T(8,128)(2,1)S(1)} %get-tuple-element.74.s_in, bf16[2,64,384]{2,1,0:T(8,128)(2,1)S(1)} %get-tuple-element.65.delta, ...), custom_call_target="tpu_custom_call" | custom-call | tf_op jit(solution)/shard_map/pallas_call | solution.py:335
  15.4 2.3 %collective-permute-done.3 = bf16[288,128]{1,0:T(8,128)(2,1)S(1)} collective-permute-done((bf16[288,128]{1,0:T(8,128)(2,1)S(1)}, bf16[288,128]{1,0:T(8,128)(2,1)S(1)}, u32[]{:S(2)}, u32[]{:S(2)}) %collective-permute-start.3) | collective-permute-done | bytes 73760 | tf_op jit(solution)/shard_map/ppermute | solution.py:346
  17.7 1.9 %collective-permute-start.4 = (bf16[288,128]{1,0:T(8,128)(2,1)S(1)}, bf16[288,128]{1,0:T(8,128)(2,1)S(1)}, u32[]{:S(2)}, u32[]{:S(2)}) collective-permute-start(bf16[288,128]{1,0:T(8,128)(2,1)S(1)} %add_convert_fusion.2), channel_id=1, source_target_pairs={{0,5},{1,16},{2,19},{3,6},{4,21},{5,0},{6,3},{7,22},{8,25},{9,12},... | collective-permute-start | bytes 221192 | tf_op jit(solution)/shard_map/ppermute | solution.py:346
  19.6 0.8 %shard_map.81.refs_1_ = bf16[8,64,384]{2,1,0:T(8,128)(2,1)S(1)} custom-call(bf16[16,64,384]{2,1,0:T(8,128)(2,1)S(1)} %get-tuple-element.72.e_ref, bf16[16,64,384]{2,1,0:T(8,128)(2,1)S(1)} %get-tuple-element.73.d_in, bf16[16,64,384]{2,1,0:T(8,128)(2,1)S(1)} %get-tuple-element.74.s_in, bf16[2,64,384]{2,1,0:T(8,128)(2,1)S(1)} %get-tuple-element.65.delta, ...), custom_call_target="tpu_custom_call" | custom-call | tf_op jit(solution)/shard_map/pallas_call | solution.py:335
  20.5 2.0 %collective-permute-done.4 = bf16[288,128]{1,0:T(8,128)(2,1)S(1)} collective-permute-done((bf16[288,128]{1,0:T(8,128)(2,1)S(1)}, bf16[288,128]{1,0:T(8,128)(2,1)S(1)}, u32[]{:S(2)}, u32[]{:S(2)}) %collective-permute-start.4) | collective-permute-done | bytes 73760 | tf_op jit(solution)/shard_map/ppermute | solution.py:346
  22.5 2.4 %collective-permute-start.5 = (bf16[288,128]{1,0:T(8,128)(2,1)S(1)}, bf16[288,128]{1,0:T(8,128)(2,1)S(1)}, u32[]{:S(2)}, u32[]{:S(2)}) collective-permute-start(bf16[288,128]{1,0:T(8,128)(2,1)S(1)} %add_convert_fusion.1), channel_id=1, source_target_pairs={{0,9},{1,2},{2,1},{3,10},{4,7},{5,12},{6,15},{7,4},{8,11},{9,0},{1... | collective-permute-start | bytes 221192 | tf_op jit(solution)/shard_map/ppermute | solution.py:346
  24.8 1.3 %shard_map.82 = bf16[64,16,384]{2,1,0:T(8,128)(2,1)} custom-call(bf16[8,64,384]{2,1,0:T(8,128)(2,1)S(1)} %shard_map.80.refs_0_, bf16[8,64,384]{2,1,0:T(8,128)(2,1)S(1)} %shard_map.81.refs_1_), custom_call_target="tpu_custom_call" | custom-call | tf_op jit(solution)/shard_map/pallas_call | solution.py:335
  26.2 0.7 %collective-permute-done.5 = bf16[288,128]{1,0:T(8,128)(2,1)S(1)} collective-permute-done((bf16[288,128]{1,0:T(8,128)(2,1)S(1)}, bf16[288,128]{1,0:T(8,128)(2,1)S(1)}, u32[]{:S(2)}, u32[]{:S(2)}) %collective-permute-start.5) | collective-permute-done | bytes 73760 | tf_op jit(solution)/shard_map/ppermute | solution.py:346
  26.9 2.3 %collective-permute-start.6 = (bf16[288,128]{1,0:T(8,128)(2,1)S(1)}, bf16[288,128]{1,0:T(8,128)(2,1)S(1)}, u32[]{:S(2)}, u32[]{:S(2)}) collective-permute-start(bf16[288,128]{1,0:T(8,128)(2,1)S(1)} %add_convert_fusion), channel_id=1, source_target_pairs={{0,17},{1,4},{2,7},{3,18},{4,1},{5,20},{6,23},{7,2},{8,13},{9,24},... | collective-permute-start | bytes 221192 | tf_op jit(solution)/shard_map/ppermute | solution.py:346
  29.2 2.0 %collective-permute-done.6 = bf16[288,128]{1,0:T(8,128)(2,1)S(1)} collective-permute-done((bf16[288,128]{1,0:T(8,128)(2,1)S(1)}, bf16[288,128]{1,0:T(8,128)(2,1)S(1)}, u32[]{:S(2)}, u32[]{:S(2)}) %collective-permute-start.6) | collective-permute-done | bytes 73760 | tf_op jit(solution)/shard_map/ppermute | solution.py:346
  31.3 0.3 collective-permute-start.7
  31.6 1.1 %collective-permute-done.7.theirs_ref = bf16[288,128]{1,0:T(8,128)(2,1)S(1)} collective-permute-done((bf16[288,128]{1,0:T(8,128)(2,1)S(1)}, bf16[288,128]{1,0:T(8,128)(2,1)S(1)}, u32[]{:S(2)}, u32[]{:S(2)}) %collective-permute-start.7) | collective-permute-done | bytes 73760 | tf_op jit(solution)/shard_map/ppermute | solution.py:346
  32.6 0.9 %shard_map.83 = (bf16[3,3,64,64]{3,2,1,0:T(8,128)(2,1)}, bf16[3,3,64,64]{3,2,1,0:T(8,128)(2,1)}) custom-call(bf16[288,128]{1,0:T(8,128)(2,1)S(1)} %multiply_convert_fusion.mine_ref, bf16[288,128]{1,0:T(8,128)(2,1)S(1)} %collective-permute-done.7.theirs_ref), custom_call_target="tpu_custom_call" | custom-call | tf_op jit(solution)/shard_map/pallas_call | solution.py:335
  (5 shorter events, 0.1 us)
Async XLA Ops:
  0.6 6.3 %copy-start = (bf16[3,3,64,64]{3,2,1,0:T(8,128)(2,1)S(1)}, bf16[3,3,64,64]{3,2,1,0:T(8,128)(2,1)}, u32[]{:S(2)}) copy-start(bf16[3,3,64,64]{3,2,1,0:T(8,128)(2,1)} %k1_ref.1) | copy-start | bytes 221188
  0.6 6.3 %copy-start.1 = (bf16[3,3,64,64]{3,2,1,0:T(8,128)(2,1)S(1)}, bf16[3,3,64,64]{3,2,1,0:T(8,128)(2,1)}, u32[]{:S(2)}) copy-start(bf16[3,3,64,64]{3,2,1,0:T(8,128)(2,1)} %k2_ref.1) | copy-start | bytes 221188
  2.4 9.2 %collective-permute-start = (bf16[2,2,64,384]{3,2,1,0:T(8,128)(2,1)S(1)}, bf16[2,2,64,384]{3,2,1,0:T(8,128)(2,1)S(1)}, u32[]{:S(2)}, u32[]{:S(2)}) collective-permute-start(bf16[2,2,64,384]{3,2,1,0:T(8,128)(2,1)S(1)} %get-tuple-element.46), channel_id=1, source_target_pairs={{0,7},{1,2},{2,1},{3,4},{4,3},{5,6},{6,5},{7,0},{8,15},{9,10},{10,... | collective-permute-start | bytes 589832 | tf_op jit(solution)/shard_map/ppermute | solution.py:346
  6.9 4.6 %collective-permute-start.1 = (bf16[2,2,64,384]{3,2,1,0:T(8,128)(2,1)S(1)}, bf16[2,2,64,384]{3,2,1,0:T(8,128)(2,1)S(1)}, u32[]{:S(2)}, u32[]{:S(2)}) collective-permute-start(bf16[2,2,64,384]{3,2,1,0:T(8,128)(2,1)S(1)} %get-tuple-element.47), channel_id=1, source_target_pairs={{0,1},{1,0},{2,3},{3,2},{4,5},{5,4},{6,7},{7,6},{8,9},{9,8},{10,11... | collective-permute-start | bytes 589832 | tf_op jit(solution)/shard_map/ppermute | solution.py:346
  12.5 1.3 %collective-permute-start.2 = (bf16[288,128]{1,0:T(8,128)(2,1)S(1)}, bf16[288,128]{1,0:T(8,128)(2,1)S(1)}, u32[]{:S(2)}, u32[]{:S(2)}) collective-permute-start(bf16[288,128]{1,0:T(8,128)(2,1)S(1)} %get-tuple-element.60), channel_id=1, source_target_pairs={{0,1},{1,0},{2,3},{3,2},{4,5},{5,4},{6,7},{7,6},{8,9},{9,8},{10,11... | collective-permute-start | bytes 221192 | tf_op jit(solution)/shard_map/ppermute | solution.py:346
  13.8 3.8 %collective-permute-start.3 = (bf16[288,128]{1,0:T(8,128)(2,1)S(1)}, bf16[288,128]{1,0:T(8,128)(2,1)S(1)}, u32[]{:S(2)}, u32[]{:S(2)}) collective-permute-start(bf16[288,128]{1,0:T(8,128)(2,1)S(1)} %add_convert_fusion.3), channel_id=1, source_target_pairs={{0,3},{1,8},{2,11},{3,0},{4,13},{5,6},{6,5},{7,14},{8,1},{9,10},{1... | collective-permute-start | bytes 221192 | tf_op jit(solution)/shard_map/ppermute | solution.py:346
  17.7 4.7 %collective-permute-start.4 = (bf16[288,128]{1,0:T(8,128)(2,1)S(1)}, bf16[288,128]{1,0:T(8,128)(2,1)S(1)}, u32[]{:S(2)}, u32[]{:S(2)}) collective-permute-start(bf16[288,128]{1,0:T(8,128)(2,1)S(1)} %add_convert_fusion.2), channel_id=1, source_target_pairs={{0,5},{1,16},{2,19},{3,6},{4,21},{5,0},{6,3},{7,22},{8,25},{9,12},... | collective-permute-start | bytes 221192 | tf_op jit(solution)/shard_map/ppermute | solution.py:346
  22.5 4.4 %collective-permute-start.5 = (bf16[288,128]{1,0:T(8,128)(2,1)S(1)}, bf16[288,128]{1,0:T(8,128)(2,1)S(1)}, u32[]{:S(2)}, u32[]{:S(2)}) collective-permute-start(bf16[288,128]{1,0:T(8,128)(2,1)S(1)} %add_convert_fusion.1), channel_id=1, source_target_pairs={{0,9},{1,2},{2,1},{3,10},{4,7},{5,12},{6,15},{7,4},{8,11},{9,0},{1... | collective-permute-start | bytes 221192 | tf_op jit(solution)/shard_map/ppermute | solution.py:346
  26.9 4.4 %collective-permute-start.6 = (bf16[288,128]{1,0:T(8,128)(2,1)S(1)}, bf16[288,128]{1,0:T(8,128)(2,1)S(1)}, u32[]{:S(2)}, u32[]{:S(2)}) collective-permute-start(bf16[288,128]{1,0:T(8,128)(2,1)S(1)} %add_convert_fusion), channel_id=1, source_target_pairs={{0,17},{1,4},{2,7},{3,18},{4,1},{5,20},{6,23},{7,2},{8,13},{9,24},... | collective-permute-start | bytes 221192 | tf_op jit(solution)/shard_map/ppermute | solution.py:346
  31.3 1.3 %collective-permute-start.7 = (bf16[288,128]{1,0:T(8,128)(2,1)S(1)}, bf16[288,128]{1,0:T(8,128)(2,1)S(1)}, u32[]{:S(2)}, u32[]{:S(2)}) collective-permute-start(bf16[288,128]{1,0:T(8,128)(2,1)S(1)} %multiply_convert_fusion.mine_ref), channel_id=1, source_target_pairs={{0,1},{1,0},{2,3},{3,2},{4,5},{5,4},{6,7},{7,6},{8,9},{9,8},{10,11... | collective-permute-start | bytes 221192 | tf_op jit(solution)/shard_map/ppermute | solution.py:346

commit v9 on v7

--- a/solution.py
+++ b/solution.py
@@ -48,16 +48,17 @@
     return jnp.concatenate([above, v, below] if adjoint else [below, v, above], axis=0)
 
 
-def prepare(k_ref, forward_ref, adjoint_ref):
+def prepare(k_ref, forward_ref=None, adjoint_ref=None):
     c = k_ref.shape[-1]
     for p in range(3):
         if forward_ref is not None:
             forward_ref[p * c : (p + 1) * c, :] = jnp.concatenate(
                 [k_ref[p, q].astype(F32) for q in range(3)], axis=1
             ).astype(BF16)
-        adjoint_ref[p * c : (p + 1) * c, :] = jnp.concatenate(
-            [k_ref[p, q].astype(F32).T for q in range(3)], axis=1
-        ).astype(BF16)
+        if adjoint_ref is not None:
+            adjoint_ref[p * c : (p + 1) * c, :] = jnp.concatenate(
+                [k_ref[p, q].astype(F32).T for q in range(3)], axis=1
+            ).astype(BF16)
 
 
 def products(i, w1, w2a, x3, e3, s3, y, z):
@@ -147,7 +148,7 @@
 
 def interior_kernel(
     x_ref, e_ref, k1_ref, k2_ref, m_ref,
-    e, w1_ref, w1a_ref, w2a_ref, g1_ref, g2_ref, d_ref, s_ref, fields, upstream, upstream_scaled, u_ref, grad_ref, y_ref, z_ref,
+    e, w1_ref, w2a_ref, g1_ref, g2_ref, d_ref, s_ref, fields, upstream, upstream_scaled, u_ref, grad_ref, y_ref, z_ref,
     x, x3, es, y, z, h3,
 ):
     n, c, lat = d_ref.shape
@@ -156,8 +157,8 @@
     turn = turning(n)
     turn_columns(turn, x_ref, x)
     turn_columns(turn, e_ref, e)
-    prepare(k1_ref, w1_ref, w1a_ref)
-    prepare(k2_ref, None, w2a_ref)
+    prepare(k1_ref, forward_ref=w1_ref)
+    prepare(k2_ref, adjoint_ref=w2a_ref)
     blank = jnp.zeros((c, lat), BF16)
     for i in (0, n - 1):
         d_ref[i] = blank
@@ -246,8 +247,8 @@
 
 def kept_kernel(
     from_outer, from_mate, m_ref, w1, w2a, g1, g2, fields, upstream, upstream_scaled, y_ref, z_ref,
-    near_fields, near_scaled, delta, delta_scaled, hidden,
-    kept_ref, near_delta, near_delta_scaled,
+    near_fields, near_scaled, delta, delta_scaled, hidden, k1_ref,
+    kept_ref, near_delta, near_delta_scaled, w1a_ref,
 ):
     metric = m_ref[...]
     c = from_mate.shape[2]
@@ -258,6 +259,7 @@
         t, fields, upstream, upstream_scaled, near_fields, near_scaled, delta, delta_scaled, hidden
     )
     put_packed(kept_ref, total + jnp.where(t == 0, g1[...], g2[...]))
+    prepare(k1_ref, adjoint_ref=w1a_ref)
     for side, one, two in ((0, low, high), (1, high, low)):
         x, e = (beyond(odd, from_mate, from_outer, side, a, 2) for a in range(2))
         near_e = beyond(odd, from_mate, from_outer, side, 1, 1)
@@ -374,10 +376,10 @@
     pair = ((2, c, lat), F32)
     two = ((2, c, lat), BF16)
     two_wide = ((2,) + column, BF16)
-    et, w1, w1a, w2a, g1, g2, d, s, fields, upstream, upstream_scaled, u, grad, y, z = call(
+    et, w1, w2a, g1, g2, d, s, fields, upstream, upstream_scaled, u, grad, y, z = call(
         interior_kernel,
         [turned_form]
-        + [(square, BF16)] * 3
+        + [(square, BF16)] * 2
         + [(square, F32)] * 2
         + [turned_form] * 2
         + [((4,) + column, BF16)]
@@ -397,8 +399,8 @@
 
     def keep(done, gate):
         return call(
-            kept_kernel, [(packed, F32), two, two], [],
-            *common, y, z, near_fields, near_scaled, delta, delta_scaled, gate(hidden),
+            kept_kernel, [(packed, F32), two, two, (square, BF16)], [],
+            *common, y, z, near_fields, near_scaled, delta, delta_scaled, gate(hidden), kernel_first,
         )
 
     def part(done, gate, start, count):
@@ -406,7 +408,7 @@
             functools.partial(field_kernel, start=start),
             [((count, c, lat), BF16)],
             [((count + 2, c, lat), F32), ((count + 2, 2 * c, lat), F32)],
-            et, d, s, delta, delta_scaled, done[0][1], done[0][2], gate(w1a),
+            et, d, s, delta, delta_scaled, done[0][1], done[0][2], gate(done[0][3]),
         )
 
     def assemble(done, gate):

time: 33.7 us -> 33.7 us (level)
  no operation moved by 1% of the time
where the time goes in v9:
time: 33.7 us; the launch traced here: 33.6 us
  starting transfers between devices  12.6 us (37%)
  Pallas kernels  11.7 us (35%)
  waiting for transfers between devices  8.47 us (25%)
  between operations  0.72 us (2%)
    ppermute x8, starting transfers between devices, exchange(): return lax.ppermute(value, ('dp', 'lon'), pairs)  12.6 us
    pallas_call x8, Pallas kernels, call(): pl.pallas_call(kernel, out_shape=[jax.ShapeDtypeStruct(s, d) for s, d in...  11.7 us
    ppermute x8, waiting for transfers between devices, exchange(): return lax.ppermute(value, ('dp', 'lon'), pairs)  8.47 us
  transfers between devices with their start and end apart: 8, of which 7 were waited for; matrix products, arithmetic and copies ran while one was open for 0% of the time, Pallas kernels for 24%

profile of v9, /device:TPU:0, one launch (start us, length us, event | category | flops | bytes accessed | tf_op | source)
XLA Modules:
  0.0 33.6 jit_solution(5165233374287146592)
XLA Ops:
  0.6 0.0 copy-start
  0.6 0.0 copy-start.1
  0.7 1.7 %shard_map.76 = (bf16[64,16,384]{2,1,0:T(8,128)(2,1)S(1)}, bf16[64,16,384]{2,1,0:T(8,128)(2,1)S(1)}, bf16[2,2,64,384]{3,2,1,0:T(8,128)(2,1)S(1)}, bf16[2,2,64,384]{3,2,1,0:T(8,128)(2,1)S(1)}, f32[1,384]{1,0:T(1,128)S(1)}) custom-call(bf16[64,16,384]{2,1,0:T(8,128)(2,1)} %bitcast.3, bf16[64,16,384]{2,1,0:T(8,128)(2,1)} %bitcast.4, f32[384]{0:T(512)} %m_hbm.1), custom_call_target="tpu_custom_call" | custom-call | tf_op jit(solution)/shard_map/pallas_call | solution.py:338
  2.4 4.6 %collective-permute-start = (bf16[2,2,64,384]{3,2,1,0:T(8,128)(2,1)S(1)}, bf16[2,2,64,384]{3,2,1,0:T(8,128)(2,1)S(1)}, u32[]{:S(2)}, u32[]{:S(2)}) collective-permute-start(bf16[2,2,64,384]{3,2,1,0:T(8,128)(2,1)S(1)} %get-tuple-element.46), channel_id=1, source_target_pairs={{0,7},{1,2},{2,1},{3,4},{4,3},{5,6},{6,5},{7,0},{8,15},{9,10},{10,... | collective-permute-start | bytes 589832 | tf_op jit(solution)/shard_map/ppermute | solution.py:349
  6.9 0.0 collective-permute-start.1
  7.0 0.0 copy-done
  7.0 0.0 copy-done.1
  7.0 4.4 %shard_map.77 = (bf16[16,64,384]{2,1,0:T(8,128)(2,1)S(1)}, bf16[192,192]{1,0:T(8,128)(2,1)S(1)}, bf16[192,192]{1,0:T(8,128)(2,1)S(1)}, f32[192,192]{1,0:T(8,128)...) custom-call(bf16[64,16,384]{2,1,0:T(8,128)(2,1)S(1)} %get-tuple-elem, ...), custom_call_target="tpu_custom_call" | custom-call | tf_op jit(solution)/shard_map/pallas_call | solution.py:338
  11.4 0.2 collective-permute-done.from_outer
  11.6 0.0 collective-permute-done.1.from_mate
  11.6 0.9 %shard_map.78 = (bf16[288,128]{1,0:T(8,128)(2,1)S(1)}, bf16[2,192,384]{2,1,0:T(8,128)(2,1)S(1)}, bf16[2,64,384]{2,1,0:T(8,128)(2,1)S(1)}, bf16[2,64,384]{2,1,0:T...) custom-call(bf16[2,2,64,384]{3,2,1,0:T(8,128)(2,1)S(1)} %collective-permute-done.from_outer, ...), custom_call_target="tpu_custom_call" | custom-call | tf_op jit(solution)/shard_map/pallas_call | solution.py:338
  12.5 0.4 %collective-permute-start.2 = (bf16[288,128]{1,0:T(8,128)(2,1)S(1)}, bf16[288,128]{1,0:T(8,128)(2,1)S(1)}, u32[]{:S(2)}, u32[]{:S(2)}) collective-permute-start(bf16[288,128]{1,0:T(8,128)(2,1)S(1)} %get-tuple-element.60), channel_id=1, source_target_pairs={{0,1},{1,0},{2,3},{3,2},{4,5},{5,4},{6,7},{7,6},{8,9},{9,8},{10,11... | collective-permute-start | bytes 221192 | tf_op jit(solution)/shard_map/ppermute | solution.py:349
  12.9 0.8 %shard_map.79 = (f32[288,128]{1,0:T(8,128)S(1)}, bf16[2,64,384]{2,1,0:T(8,128)(2,1)S(1)}, bf16[2,64,384]{2,1,0:T(8,128)(2,1)S(1)}, bf16[192,192]{1,0:T(8,128)(2,1)S(1)}) custom-call(bf16[2,2,64,384]{3,2,1,0:T(8,128)(2,1)S(1)} %collective-permute-done.from_outer, bf16[2,2,64,384]{3,2,1,0:T(8,128)(2,1)S(1)} %collective-permute-done.1.from_mate, ...), custom_call_target="tpu_custom_call" | custom-call | tf_op jit(solution)/shard_map/pallas_call | solution.py:338
  13.7 0.2 collective-permute-done.2
  13.9 0.7 %collective-permute-start.3 = (bf16[288,128]{1,0:T(8,128)(2,1)S(1)}, bf16[288,128]{1,0:T(8,128)(2,1)S(1)}, u32[]{:S(2)}, u32[]{:S(2)}) collective-permute-start(bf16[288,128]{1,0:T(8,128)(2,1)S(1)} %add_convert_fusion.3), channel_id=1, source_target_pairs={{0,3},{1,8},{2,11},{3,0},{4,13},{5,6},{6,5},{7,14},{8,1},{9,10},{1... | collective-permute-start | bytes 221192 | tf_op jit(solution)/shard_map/ppermute | solution.py:349
  14.6 0.8 %shard_map.80.refs_0_ = bf16[8,64,384]{2,1,0:T(8,128)(2,1)S(1)} custom-call(bf16[16,64,384]{2,1,0:T(8,128)(2,1)S(1)} %get-tuple-element.72.e_ref, bf16[16,64,384]{2,1,0:T(8,128)(2,1)S(1)} %get-tuple-element.73.d_in, bf16[16,64,384]{2,1,0:T(8,128)(2,1)S(1)} %get-tuple-element.74.s_in, bf16[2,64,384]{2,1,0:T(8,128)(2,1)S(1)} %get-tuple-element.65.delta, ...), custom_call_target="tpu_custom_call" | custom-call | tf_op jit(solution)/shard_map/pallas_call | solution.py:338
  15.4 2.3 %collective-permute-done.3 = bf16[288,128]{1,0:T(8,128)(2,1)S(1)} collective-permute-done((bf16[288,128]{1,0:T(8,128)(2,1)S(1)}, bf16[288,128]{1,0:T(8,128)(2,1)S(1)}, u32[]{:S(2)}, u32[]{:S(2)}) %collective-permute-start.3) | collective-permute-done | bytes 73760 | tf_op jit(solution)/shard_map/ppermute | solution.py:349
  17.7 1.9 %collective-permute-start.4 = (bf16[288,128]{1,0:T(8,128)(2,1)S(1)}, bf16[288,128]{1,0:T(8,128)(2,1)S(1)}, u32[]{:S(2)}, u32[]{:S(2)}) collective-permute-start(bf16[288,128]{1,0:T(8,128)(2,1)S(1)} %add_convert_fusion.2), channel_id=1, source_target_pairs={{0,5},{1,16},{2,19},{3,6},{4,21},{5,0},{6,3},{7,22},{8,25},{9,12},... | collective-permute-start | bytes 221192 | tf_op jit(solution)/shard_map/ppermute | solution.py:349
  19.7 0.8 %shard_map.81.refs_1_ = bf16[8,64,384]{2,1,0:T(8,128)(2,1)S(1)} custom-call(bf16[16,64,384]{2,1,0:T(8,128)(2,1)S(1)} %get-tuple-element.72.e_ref, bf16[16,64,384]{2,1,0:T(8,128)(2,1)S(1)} %get-tuple-element.73.d_in, bf16[16,64,384]{2,1,0:T(8,128)(2,1)S(1)} %get-tuple-element.74.s_in, bf16[2,64,384]{2,1,0:T(8,128)(2,1)S(1)} %get-tuple-element.65.delta, ...), custom_call_target="tpu_custom_call" | custom-call | tf_op jit(solution)/shard_map/pallas_call | solution.py:338
  20.5 2.0 %collective-permute-done.4 = bf16[288,128]{1,0:T(8,128)(2,1)S(1)} collective-permute-done((bf16[288,128]{1,0:T(8,128)(2,1)S(1)}, bf16[288,128]{1,0:T(8,128)(2,1)S(1)}, u32[]{:S(2)}, u32[]{:S(2)}) %collective-permute-start.4) | collective-permute-done | bytes 73760 | tf_op jit(solution)/shard_map/ppermute | solution.py:349
  22.5 2.4 %collective-permute-start.5 = (bf16[288,128]{1,0:T(8,128)(2,1)S(1)}, bf16[288,128]{1,0:T(8,128)(2,1)S(1)}, u32[]{:S(2)}, u32[]{:S(2)}) collective-permute-start(bf16[288,128]{1,0:T(8,128)(2,1)S(1)} %add_convert_fusion.1), channel_id=1, source_target_pairs={{0,9},{1,2},{2,1},{3,10},{4,7},{5,12},{6,15},{7,4},{8,11},{9,0},{1... | collective-permute-start | bytes 221192 | tf_op jit(solution)/shard_map/ppermute | solution.py:349
  24.9 1.3 %shard_map.82 = bf16[64,16,384]{2,1,0:T(8,128)(2,1)} custom-call(bf16[8,64,384]{2,1,0:T(8,128)(2,1)S(1)} %shard_map.80.refs_0_, bf16[8,64,384]{2,1,0:T(8,128)(2,1)S(1)} %shard_map.81.refs_1_), custom_call_target="tpu_custom_call" | custom-call | tf_op jit(solution)/shard_map/pallas_call | solution.py:338
  26.2 0.7 %collective-permute-done.5 = bf16[288,128]{1,0:T(8,128)(2,1)S(1)} collective-permute-done((bf16[288,128]{1,0:T(8,128)(2,1)S(1)}, bf16[288,128]{1,0:T(8,128)(2,1)S(1)}, u32[]{:S(2)}, u32[]{:S(2)}) %collective-permute-start.5) | collective-permute-done | bytes 73760 | tf_op jit(solution)/shard_map/ppermute | solution.py:349
  27.0 2.3 %collective-permute-start.6 = (bf16[288,128]{1,0:T(8,128)(2,1)S(1)}, bf16[288,128]{1,0:T(8,128)(2,1)S(1)}, u32[]{:S(2)}, u32[]{:S(2)}) collective-permute-start(bf16[288,128]{1,0:T(8,128)(2,1)S(1)} %add_convert_fusion), channel_id=1, source_target_pairs={{0,17},{1,4},{2,7},{3,18},{4,1},{5,20},{6,23},{7,2},{8,13},{9,24},... | collective-permute-start | bytes 221192 | tf_op jit(solution)/shard_map/ppermute | solution.py:349
  29.3 2.0 %collective-permute-done.6 = bf16[288,128]{1,0:T(8,128)(2,1)S(1)} collective-permute-done((bf16[288,128]{1,0:T(8,128)(2,1)S(1)}, bf16[288,128]{1,0:T(8,128)(2,1)S(1)}, u32[]{:S(2)}, u32[]{:S(2)}) %collective-permute-start.6) | collective-permute-done | bytes 73760 | tf_op jit(solution)/shard_map/ppermute | solution.py:349
  31.4 0.3 collective-permute-start.7
  31.6 1.1 %collective-permute-done.7.theirs_ref = bf16[288,128]{1,0:T(8,128)(2,1)S(1)} collective-permute-done((bf16[288,128]{1,0:T(8,128)(2,1)S(1)}, bf16[288,128]{1,0:T(8,128)(2,1)S(1)}, u32[]{:S(2)}, u32[]{:S(2)}) %collective-permute-start.7) | collective-permute-done | bytes 73760 | tf_op jit(solution)/shard_map/ppermute | solution.py:349
  32.7 0.9 %shard_map.83 = (bf16[3,3,64,64]{3,2,1,0:T(8,128)(2,1)}, bf16[3,3,64,64]{3,2,1,0:T(8,128)(2,1)}) custom-call(bf16[288,128]{1,0:T(8,128)(2,1)S(1)} %multiply_convert_fusion.mine_ref, bf16[288,128]{1,0:T(8,128)(2,1)S(1)} %collective-permute-done.7.theirs_ref), custom_call_target="tpu_custom_call" | custom-call | tf_op jit(solution)/shard_map/pallas_call | solution.py:338
  (5 shorter events, 0.1 us)
Async XLA Ops:
  0.6 6.3 %copy-start = (bf16[3,3,64,64]{3,2,1,0:T(8,128)(2,1)S(1)}, bf16[3,3,64,64]{3,2,1,0:T(8,128)(2,1)}, u32[]{:S(2)}) copy-start(bf16[3,3,64,64]{3,2,1,0:T(8,128)(2,1)} %k1_ref.3) | copy-start | bytes 221188
  0.6 6.3 %copy-start.1 = (bf16[3,3,64,64]{3,2,1,0:T(8,128)(2,1)S(1)}, bf16[3,3,64,64]{3,2,1,0:T(8,128)(2,1)}, u32[]{:S(2)}) copy-start(bf16[3,3,64,64]{3,2,1,0:T(8,128)(2,1)} %k2_ref.1) | copy-start | bytes 221188
  2.4 9.2 %collective-permute-start = (bf16[2,2,64,384]{3,2,1,0:T(8,128)(2,1)S(1)}, bf16[2,2,64,384]{3,2,1,0:T(8,128)(2,1)S(1)}, u32[]{:S(2)}, u32[]{:S(2)}) collective-permute-start(bf16[2,2,64,384]{3,2,1,0:T(8,128)(2,1)S(1)} %get-tuple-element.46), channel_id=1, source_target_pairs={{0,7},{1,2},{2,1},{3,4},{4,3},{5,6},{6,5},{7,0},{8,15},{9,10},{10,... | collective-permute-start | bytes 589832 | tf_op jit(solution)/shard_map/ppermute | solution.py:349
  6.9 4.6 %collective-permute-start.1 = (bf16[2,2,64,384]{3,2,1,0:T(8,128)(2,1)S(1)}, bf16[2,2,64,384]{3,2,1,0:T(8,128)(2,1)S(1)}, u32[]{:S(2)}, u32[]{:S(2)}) collective-permute-start(bf16[2,2,64,384]{3,2,1,0:T(8,128)(2,1)S(1)} %get-tuple-element.47), channel_id=1, source_target_pairs={{0,1},{1,0},{2,3},{3,2},{4,5},{5,4},{6,7},{7,6},{8,9},{9,8},{10,11... | collective-permute-start | bytes 589832 | tf_op jit(solution)/shard_map/ppermute | solution.py:349
  12.5 1.3 %collective-permute-start.2 = (bf16[288,128]{1,0:T(8,128)(2,1)S(1)}, bf16[288,128]{1,0:T(8,128)(2,1)S(1)}, u32[]{:S(2)}, u32[]{:S(2)}) collective-permute-start(bf16[288,128]{1,0:T(8,128)(2,1)S(1)} %get-tuple-element.60), channel_id=1, source_target_pairs={{0,1},{1,0},{2,3},{3,2},{4,5},{5,4},{6,7},{7,6},{8,9},{9,8},{10,11... | collective-permute-start | bytes 221192 | tf_op jit(solution)/shard_map/ppermute | solution.py:349
  13.9 3.8 %collective-permute-start.3 = (bf16[288,128]{1,0:T(8,128)(2,1)S(1)}, bf16[288,128]{1,0:T(8,128)(2,1)S(1)}, u32[]{:S(2)}, u32[]{:S(2)}) collective-permute-start(bf16[288,128]{1,0:T(8,128)(2,1)S(1)} %add_convert_fusion.3), channel_id=1, source_target_pairs={{0,3},{1,8},{2,11},{3,0},{4,13},{5,6},{6,5},{7,14},{8,1},{9,10},{1... | collective-permute-start | bytes 221192 | tf_op jit(solution)/shard_map/ppermute | solution.py:349
  17.7 4.7 %collective-permute-start.4 = (bf16[288,128]{1,0:T(8,128)(2,1)S(1)}, bf16[288,128]{1,0:T(8,128)(2,1)S(1)}, u32[]{:S(2)}, u32[]{:S(2)}) collective-permute-start(bf16[288,128]{1,0:T(8,128)(2,1)S(1)} %add_convert_fusion.2), channel_id=1, source_target_pairs={{0,5},{1,16},{2,19},{3,6},{4,21},{5,0},{6,3},{7,22},{8,25},{9,12},... | collective-permute-start | bytes 221192 | tf_op jit(solution)/shard_map/ppermute | solution.py:349
  22.5 4.4 %collective-permute-start.5 = (bf16[288,128]{1,0:T(8,128)(2,1)S(1)}, bf16[288,128]{1,0:T(8,128)(2,1)S(1)}, u32[]{:S(2)}, u32[]{:S(2)}) collective-permute-start(bf16[288,128]{1,0:T(8,128)(2,1)S(1)} %add_convert_fusion.1), channel_id=1, source_target_pairs={{0,9},{1,2},{2,1},{3,10},{4,7},{5,12},{6,15},{7,4},{8,11},{9,0},{1... | collective-permute-start | bytes 221192 | tf_op jit(solution)/shard_map/ppermute | solution.py:349
  27.0 4.4 %collective-permute-start.6 = (bf16[288,128]{1,0:T(8,128)(2,1)S(1)}, bf16[288,128]{1,0:T(8,128)(2,1)S(1)}, u32[]{:S(2)}, u32[]{:S(2)}) collective-permute-start(bf16[288,128]{1,0:T(8,128)(2,1)S(1)} %add_convert_fusion), channel_id=1, source_target_pairs={{0,17},{1,4},{2,7},{3,18},{4,1},{5,20},{6,23},{7,2},{8,13},{9,24},... | collective-permute-start | bytes 221192 | tf_op jit(solution)/shard_map/ppermute | solution.py:349
  31.4 1.3 %collective-permute-start.7 = (bf16[288,128]{1,0:T(8,128)(2,1)S(1)}, bf16[288,128]{1,0:T(8,128)(2,1)S(1)}, u32[]{:S(2)}, u32[]{:S(2)}) collective-permute-start(bf16[288,128]{1,0:T(8,128)(2,1)S(1)} %multiply_convert_fusion.mine_ref), channel_id=1, source_target_pairs={{0,1},{1,0},{2,3},{3,2},{4,5},{5,4},{6,7},{7,6},{8,9},{9,8},{10,11... | collective-permute-start | bytes 221192 | tf_op jit(solution)/shard_map/ppermute | solution.py:349
